TPU v7x, 128 devices: a whole 4x4x4 slice. The times are simulated.
128 devices in a mesh: tm: 32 (over x, z, core), chan: 4 (over y).
Axes of the slice: x: 4, y: 4, z: 4, core: 2. Of those that a mesh axis runs over, the one named last changes fastest.
Arguments:
- raw: bfloat16 [12288, 16384], P(('tm', 'chan')), may hold values from -6 to 6
- taps: bfloat16 [127], replicated, may hold values from -0.5 to 0.5
- row_channel: int32 [12288], replicated, may hold values from 0 to 12287, each once
- ref_channel: int32 [256], replicated, may hold values from 0 to 12287, as said below
- owner_of_row: int32 [12288, 1], P(('tm', 'chan')), may hold values from 0 to 127; in each aligned block of 96 rows (0 to 95, 96 to 191, ...) at most 2 rows name the same one
Outputs:
- tiles: float32 [128, 256, 4096], P(('tm', 'chan'))
Inputs may be any that keep to these rules, and one draw needn't show every extreme that they name: `ref_channel`: distinct channel ids. `owner_of_row`: within each aligned block of 96 rows, at most 2 rows name the same setup.
All inputs are finite; a program needn't handle non-finite values.
Results may differ from a plain program's by a relative error of at most 0.013.
Values may be sent and summed in bfloat16 or wider, within the bound.
No kernel may reach another device: no remote copies, remote signals or barrier semaphores. Data moves between devices by JAX's collectives and lax.ppermute only.
A program may use at most 192 MiB of HBM per device.

v0:
```python
import math

import jax
import jax.numpy as jnp
from jax import lax
from jax.sharding import PartitionSpec as P

LAGS = 16
TAPS = 127
STRIDE = 8


def on_device(raw, taps, row_channel, ref_channel, owner_of_row):
    tm_count = lax.axis_size("tm")
    chan_count = lax.axis_size("chan")
    rows_dev = raw.shape[0]
    samples = raw.shape[1]
    total = samples // STRIDE
    count_q = (TAPS + STRIDE - 1) // STRIDE
    half = TAPS // 2
    padded = jnp.pad(raw, ((0, 0), (half, count_q * STRIDE - half)))
    pieces = padded.reshape(rows_dev, total + count_q, STRIDE)
    table = jnp.pad(taps, (0, count_q * STRIDE - TAPS)).reshape(count_q, STRIDE)
    accum = jnp.zeros((rows_dev, total), jnp.float32)
    for q in range(count_q):
        accum = accum + jnp.einsum(
            "rnm,m->rn", pieces[:, q : q + total], table[q], preferred_element_type=jnp.float32
        )
    decimated = accum.astype(jnp.bfloat16)
    own_block = lax.axis_index("tm") * chan_count + lax.axis_index("chan")
    local_ids = lax.dynamic_slice_in_dim(row_channel, own_block * rows_dev, rows_dev)
    select = (ref_channel[:, None] == local_ids[None, :]).astype(jnp.bfloat16)
    refs = lax.psum(
        jnp.dot(select, decimated, preferred_element_type=jnp.float32), ("tm", "chan")
    ).astype(jnp.bfloat16)
    extended = jnp.concatenate([decimated, jnp.zeros((rows_dev, LAGS), jnp.bfloat16)], axis=1)
    dslab = total // tm_count
    ref_slabs = refs.reshape(refs.shape[0], tm_count, dslab)
    terms = []
    for lag in range(1, LAGS + 1):
        shifted = lax.slice_in_dim(extended, lag, lag + total, axis=1).reshape(
            rows_dev, tm_count, dslab
        )
        part = jnp.einsum("rtn,jtn->trj", shifted, ref_slabs, preferred_element_type=jnp.float32)
        rounded = lax.optimization_barrier(part.astype(jnp.bfloat16))
        terms.append(jnp.sum(rounded.astype(jnp.float32), axis=0))
    summed = jnp.concatenate(terms, axis=1)
    tile_rows = summed * (1.0 / math.sqrt(total))
    width = tile_rows.shape[1]
    device_count = tm_count * chan_count
    capacity = max(2, 2 * rows_dev // device_count)
    owner = owner_of_row[:, 0]
    hits = (owner[:, None] == lax.broadcasted_iota(jnp.int32, (rows_dev, device_count), 1)).astype(
        jnp.int32
    )
    rank = jnp.sum(hits * (jnp.cumsum(hits, axis=0) - 1), axis=1)
    slot = owner * capacity + rank
    outgoing = jnp.zeros((device_count * capacity, width), jnp.float32).at[slot].set(tile_rows)
    arrived = lax.all_to_all(
        outgoing.reshape(device_count, capacity, width).astype(jnp.bfloat16),
        ("tm", "chan"),
        split_axis=0,
        concat_axis=0,
        tiled=True,
    ).astype(jnp.float32)
    return arrived.reshape(1, device_count * capacity, width)


def solution(mesh):
    in_specs = (P(("tm", "chan"), None), P(), P(), P(), P(("tm", "chan"), None))
    out_specs = P(("tm", "chan"), None, None)
    return jax.shard_map(
        on_device, mesh=mesh, in_specs=in_specs, out_specs=out_specs, check_vma=False
    )
```

profile of v0, /device:TPU:1, one launch (start us, length us, event | category | flops | bytes accessed | tf_op | source)
XLA Modules:
  0.0 250.2 jit_solution(2191485697765062156)
XLA Ops:
  0.0 1.3 slice_convert_fusion.13
  1.3 5.9 %copy.88 = bf16[96,16384]{0,1:T(8,128)(2,1)} copy(bf16[96,16384]{1,0:T(8,128)(2,1)} %param.5) | data formatting | bytes 6291456
  7.2 3.6 %pad_bitcast_fusion = bf16[96,2064,8]{0,2,1:T(8,128)(2,1)S(1)} fusion(bf16[96,16384]{0,1:T(8,128)(2,1)} %copy.88), kind=kLoop, calls=%fused_computation.17 | loop fusion | bytes 6316032 | tf_op jit(solution)/shard_map/reshape | solution.py:22
  10.8 32.1 %multiply_reduce_fusion.15 = (f32[96,2048]{0,1:T(8,128)S(1)}, f32[96,2048]{0,1:T(8,128)S(1)}, f32[96,2048]{0,1:T(8,128)}, f32[96,2048]{0,1:T(8,128)}, f32[96,204...) fusion(bf16[96,2064,8]{0,2,1:T(8,128)(2,1)S(1)} %pad_bitcast_fusion, f32[8]{0:T(128)S(1)} %get-tuple-element.50, ...), kind=kLoop, calls=%fused_computation.16 | loop fusion | flops 31653888 | bytes 27525344 | tf_op jit(solution)/shard_map/rnm,m->rn/dot_general | solution.py:26
  42.9 41.3 %multiply_reduce_fusion.14 = (f32[96,2048]{0,1:T(8,128)}, f32[96,2048]{0,1:T(8,128)}, f32[96,2048]{0,1:T(8,128)}, f32[96,2048]{0,1:T(8,128)}, f32[96,2048]{0,1:T...) fusion(bf16[96,2064,8]{0,2,1:T(8,128)(2,1)S(1)} %pad_bitcast_fusion, ...), kind=kLoop, calls=%fused_computation.15 | loop fusion | flops 40697856 | bytes 35389728 | tf_op jit(solution)/shard_map/rnm,m->rn/dot_general | solution.py:26
  84.2 6.0 %add_convert_fusion = bf16[96,2048]{0,1:T(8,128)(2,1)S(1)} fusion(f32[96,2048]{0,1:T(8,128)} %get-tuple-element.6, f32[96,2048]{0,1:T(8,128)} %get-tuple-element.7, f32[96,2048]{0,1:T(8,128)} %get-tuple-element.8, f32[96,2048]{0,1:T(8,128)} %get-tuple-element.9, f32[96,2048]{0,1:T(8,128)} %get-tuple-element.10, f32[96,2048]{0,1:T(8,128)} %get-tuple-element.11, ...), kind=kLoop, calls=%fused_computation.69 | loop fusion | flops 3145728 | bytes 12976128 | tf_op jit(solution)/shard_map/convert_element_type | solution.py:29
  90.2 2.5 pad_slice_fusion
  92.7 2.3 pad_slice_fusion.1
  95.0 0.8 dynamic_slice.3
  95.8 0.5 fusion.4
  96.2 78.6 %all-reduce.4 = bf16[256,2048]{1,0:T(8,128)(2,1)} all-reduce(f32[256,2048]{1,0:T(8,128)S(1)} %fusion.4), channel_id=1, replica_groups=mesh['tm'=32,'chan'=4] {'tm','chan'}, use_global_device_ids=true, to_apply=%region_2.3 | all-reduce | flops 524288 | bytes 3145728 | tf_op jit(solution)/shard_map/psum | solution.py:33
  174.8 1.5 copy.23
  176.3 1.7 convolution_convert_fusion.8
  178.0 0.2 convert_reduce_fusion.8
  178.3 0.6 convolution_convert_fusion.9
  178.9 0.2 convert_reduce_fusion.9
  179.1 0.6 convolution_convert_fusion.10
  179.8 0.2 convert_reduce_fusion.10
  180.0 0.6 convolution_convert_fusion.11
  180.6 0.2 convert_reduce_fusion.11
  180.9 0.6 convolution_convert_fusion.12
  181.5 0.9 convert_reduce_fusion.12
  182.4 0.6 convolution_convert_fusion.13
  183.0 0.0 copy-start.13
  183.0 0.9 convert_reduce_fusion.13
  183.9 0.6 convolution_convert_fusion.14
  184.5 0.8 convert_reduce_fusion.14
  185.3 0.0 copy-done.13
  185.3 0.6 convolution_convert_fusion.15
  186.0 0.0 copy-start.12
  186.0 0.2 convert_reduce_fusion.15
  186.2 0.6 constant_dynamic-update-slice_fusion.15
  186.8 0.0 copy-done
  186.9 0.6 convolution_convert_fusion.7
  187.5 0.8 convert_reduce_fusion.7
  188.3 0.6 convolution_convert_fusion.6
  189.0 0.9 convert_reduce_fusion.6
  189.8 0.6 convolution_convert_fusion.5
  190.5 0.0 copy-start.9
  190.5 0.9 convert_reduce_fusion.5
  191.3 0.0 copy-done.10
  191.3 0.6 convolution_convert_fusion.4
  192.0 0.8 convert_reduce_fusion.4
  192.8 0.6 convolution_convert_fusion.3
  193.4 0.9 convert_reduce_fusion.3
  194.3 0.6 convolution_convert_fusion.2
  194.9 0.9 convert_reduce_fusion.2
  195.8 0.6 convolution_convert_fusion.1
  196.4 0.0 copy-start.22
  196.4 0.0 copy-start.14
  196.4 0.9 convert_reduce_fusion.1
  197.3 0.9 convolution_convert_fusion
  198.2 0.2 convert_reduce_fusion
  198.5 0.1 fusion.8
  198.6 0.1 reduce_window_sum.11
  198.7 0.2 select_reduce_fusion
  198.9 0.9 constant_dynamic-update-slice_fusion.14
  199.8 0.9 constant_dynamic-update-slice_fusion.13
  200.7 0.9 constant_dynamic-update-slice_fusion.12
  201.9 3.8 %scatter_custom_fusion = f32[256,4096]{1,0:T(8,128)} fusion(s32[96]{0:T(128)S(1)} %fusion.9, f32[]{:T(128)} %constant.13.clone.1, f32[96,4096]{1,0:T(8,128)S(1)} %constant_dynamic-update-slice_fusion, f32[]{:T(128)} %constant.36.clone.1), kind=kCustom, calls=%fused_computation.50 | custom fusion | flops 393216 | bytes 5767176 | tf_op jit(solution)/shard_map/scatter | solution.py:58
  205.7 2.5 convert_element_type.152
  208.1 2.6 %convert_element_type.153 = bf16[128,2,4096]{2,1,0:T(2,128)(2,1)} reshape(bf16[256,4096]{1,0:T(8,128)(2,1)S(1)} %convert_element_type.152) | data formatting | bytes 4194304 | tf_op jit(solution)/shard_map/convert_element_type | solution.py:60
  210.8 36.8 %all_to_all.5 = bf16[128,2,4096]{2,1,0:T(2,128)(2,1)S(1)} all-to-all(bf16[128,2,4096]{2,1,0:T(2,128)(2,1)} %convert_element_type.153), channel_id=1, replica_groups=mesh['tm'=32,'chan'=4] {'tm','chan'}, dimensions={0} | all-to-all | bytes 4194304 | tf_op jit(solution)/shard_map/all_to_all | solution.py:59
  247.6 2.6 %reshape.119 = f32[1,256,4096]{2,1,0:T(8,128)} reshape(bf16[128,2,4096]{2,1,0:T(2,128)(2,1)S(1)} %all_to_all.5) | data formatting | bytes 6291456 | tf_op jit(solution)/shard_map/reshape | solution.py:66
  (53 shorter events, 0.2 us)
Async XLA Ops:
  92.7 3.1 %copy-start.23 = (s32[256]{0:T(256)S(1)}, s32[256]{0:T(256)}, u32[]{:S(2)}) copy-start(s32[256]{0:T(256)} %param.8) | copy-start | bytes 3076
  174.8 3.4 %copy-start.6 = (bf16[96,2048]{0,1:T(8,128)(2,1)S(1)}, bf16[96,2048]{0,1:T(8,128)(2,1)}, u32[]{:S(2)}) copy-start(bf16[96,2048]{0,1:T(8,128)(2,1)} %get-tuple-element.27) | copy-start | bytes 1179652
  178.0 1.1 copy-start.5
  178.9 1.1 copy-start.4
  179.8 1.1 copy-start.3
  180.6 1.7 copy-start.2
  181.5 2.4 copy-start.1
  183.0 2.4 copy-start.13
  184.5 2.4 copy-start
  186.0 2.4 copy-start.12
  187.5 2.4 copy-start.11
  189.0 2.4 copy-start.10
  190.5 2.3 copy-start.9
  191.9 2.4 copy-start.8
  193.4 2.4 copy-start.7
  196.4 2.0 copy-start.22
  196.4 2.5 copy-start.14
  198.2 3.5 %copy-start.15 = (f32[96,256]{1,0:T(8,128)S(1)}, f32[96,256]{1,0:T(8,128)}, u32[]{:S(2)}) copy-start(f32[96,256]{1,0:T(8,128)} %convert_reduce_fusion.7) | copy-start | bytes 294916
  198.2 3.5 %copy-start.16 = (f32[96,256]{1,0:T(8,128)S(1)}, f32[96,256]{1,0:T(8,128)}, u32[]{:S(2)}) copy-start(f32[96,256]{1,0:T(8,128)} %convert_reduce_fusion.6) | copy-start | bytes 294916
  198.2 3.5 %copy-start.17 = (f32[96,256]{1,0:T(8,128)S(1)}, f32[96,256]{1,0:T(8,128)}, u32[]{:S(2)}) copy-start(f32[96,256]{1,0:T(8,128)} %convert_reduce_fusion.5) | copy-start | bytes 294916
  198.2 3.6 %copy-start.18 = (f32[96,256]{1,0:T(8,128)S(1)}, f32[96,256]{1,0:T(8,128)}, u32[]{:S(2)}) copy-start(f32[96,256]{1,0:T(8,128)} %convert_reduce_fusion.4) | copy-start | bytes 294916
  198.2 3.6 %copy-start.19 = (f32[96,256]{1,0:T(8,128)S(1)}, f32[96,256]{1,0:T(8,128)}, u32[]{:S(2)}) copy-start(f32[96,256]{1,0:T(8,128)} %convert_reduce_fusion.3) | copy-start | bytes 294916
  198.2 3.6 %copy-start.20 = (f32[96,256]{1,0:T(8,128)S(1)}, f32[96,256]{1,0:T(8,128)}, u32[]{:S(2)}) copy-start(f32[96,256]{1,0:T(8,128)} %convert_reduce_fusion.2) | copy-start | bytes 294916
  198.2 3.6 %copy-start.21 = (f32[96,256]{1,0:T(8,128)S(1)}, f32[96,256]{1,0:T(8,128)}, u32[]{:S(2)}) copy-start(f32[96,256]{1,0:T(8,128)} %convert_reduce_fusion.1) | copy-start | bytes 294916
where the time goes:
time: 251 us; the launch traced here: 250 us
  blocking collectives  115 us (46%)
  other arithmetic  97.2 us (39%)
  local copies, waits for them, and re-layouts  25.4 us (10%)
  matrix products  11.7 us (5%)
    psum x1, blocking collectives, on_device(): lax.psum(jnp.dot(select, decimated, preferred_element_type=jnp.float32),...  78.6 us
    dot_general x2, other arithmetic, on_device(): jnp.einsum('rnm,m->rn', pieces[:, q:q + total], table[q], preferred_eleme...  73.4 us
    all_to_all x1, blocking collectives, on_device(): lax.all_to_all(outgoing.reshape(device_count, capacity, width).astype(jnp...  36.8 us
    dot_general x16, matrix products, on_device(): jnp.einsum('rtn,jtn->trj', shifted, ref_slabs, preferred_element_type=jnp...  11.2 us
    reduce_sum x16, other arithmetic, on_device(): terms.append(jnp.sum(rounded.astype(jnp.float32), axis=0))  9.85 us
    unnamed x64, local copies, waits for them, and re-layouts  9.43 us
    convert_element_type x1, other arithmetic, on_device(): decimated = accum.astype(jnp.bfloat16)  5.97 us

commit v1 on v0

v1 whole, which is shorter than its diff:
```python
import math

import jax
import jax.numpy as jnp
from jax import lax
from jax.experimental import pallas as pl
from jax.experimental.pallas import tpu as pltpu
from jax.sharding import PartitionSpec as P

LAGS = 16
TAPS = 127
STRIDE = 8
NREF = 256
LANES = 128
BLOCK = 128
HALO = 128
AXES = ("tm", "chan")
NT = (((1,), (1,)), ((), ()))


def dot_nt(a, b):
    return lax.dot_general(a, b, NT, preferred_element_type=jnp.float32)


def decimate_kernel(raw_ref, taps_ref, ids_ref, refch_ref, owner_ref, rows_ref, refs_ref, line, dect, stage):
    rows, samples = raw_ref.shape
    devices = rows_ref.shape[0] // 32
    window = BLOCK * STRIDE + 2 * HALO
    line[...] = jnp.zeros_like(line)
    line[0:1, 0:TAPS] = taps_ref[...].astype(jnp.float32)
    band = pltpu.roll(
        jnp.broadcast_to(line[0:1, :], (BLOCK, window)),
        HALO - TAPS // 2,
        1,
        stride=STRIDE,
        stride_axis=0,
    ).astype(jnp.bfloat16)
    blocks = samples // (BLOCK * STRIDE)
    for m in range(blocks):
        lo, hi = m * BLOCK * STRIDE - HALO, (m + 1) * BLOCK * STRIDE + HALO
        first, last = max(lo, 0), min(hi, samples)
        part = dot_nt(band[:, first - lo : last - lo], raw_ref[:, first:last])
        dect[m * BLOCK : (m + 1) * BLOCK, :rows] = part.astype(jnp.bfloat16).astype(jnp.float32)
    owner = owner_ref[...]
    hits = lax.broadcasted_iota(jnp.int32, (devices, rows), 0) == owner
    before = (
        lax.broadcasted_iota(jnp.int32, (rows, rows), 0)
        < lax.broadcasted_iota(jnp.int32, (rows, rows), 1)
    ).astype(jnp.bfloat16)
    rank = jnp.dot(hits.astype(jnp.bfloat16), before, preferred_element_type=jnp.float32)
    one = hits.astype(jnp.float32)
    first_row = jnp.where(rank < 0.5, one, 0.0)
    second_row = one - first_row
    refcol = jnp.transpose(jnp.broadcast_to(refch_ref[...], (LANES, NREF)))[:, :rows]
    ref_rows = (refcol == ids_ref[...]).astype(jnp.float32)
    select = jnp.concatenate([first_row, second_row, ref_rows], axis=0).astype(jnp.bfloat16)
    for b in range(0, LAGS, 2):
        planes = jnp.concatenate(
            [dect[pl.ds(b + h, LANES, stride=LAGS), :][:, :rows] for h in range(2)], axis=0
        ).astype(jnp.bfloat16)
        picked = dot_nt(select, planes)
        for s in range(4):
            for h in range(2):
                stage[s // 2, pl.ds((s % 2) * LAGS + b + h, devices, stride=2 * LAGS), :] = picked[
                    s * devices : (s + 1) * devices, h * LANES : (h + 1) * LANES
                ]
    rows_ref[...] = stage[0].astype(jnp.bfloat16)
    refs_ref[...] = stage[1].astype(jnp.bfloat16)


def spread_kernel(got_ref, out_ref):
    size, width = got_ref.shape
    block = 2 * LAGS
    total = jnp.sum(got_ref[...].astype(jnp.float32).reshape(size // block, block, width), axis=0)
    out_ref[...] = (
        jnp.broadcast_to(total[None], (size // block, block, width))
        .reshape(size, width)
        .astype(jnp.bfloat16)
    )


def correlate_kernel(rows_ref, refs_ref, out_ref, wide, ext, ref_planes):
    step = pl.program_id(0)
    devices = rows_ref.shape[0] // 32
    total = LAGS * LANES

    @pl.when(step == 0)
    def _():
        wide[...] = refs_ref[...].astype(jnp.float32)
        for s in range(2):
            for b in range(LAGS):
                ref_planes[s * devices : (s + 1) * devices, b * LANES : (b + 1) * LANES] = wide[
                    pl.ds(s * LAGS + b, devices, stride=2 * LAGS), :
                ].astype(jnp.bfloat16)
        wide[...] = rows_ref[...].astype(jnp.float32)
        last_lane = lax.broadcasted_iota(jnp.int32, (2 * devices, LANES), 1) == LANES - 1
        for b in range(LAGS):
            plane = wide[pl.ds(b, 2 * devices, stride=LAGS), :]
            ext[:, b * LANES : (b + 1) * LANES] = plane.astype(jnp.bfloat16)
            moved = jnp.where(last_lane, 0.0, pltpu.roll(plane, LANES - 1, 1))
            ext[:, total + b * LANES : total + (b + 1) * LANES] = moved.astype(jnp.bfloat16)

    start = pl.multiple_of((step + 1) * LANES, LANES)
    out_ref[0] = dot_nt(ext[:, pl.ds(start, total)], ref_planes[...]) * (1.0 / math.sqrt(total))


def on_device(raw, taps, row_channel, ref_channel, owner_of_row):
    devices = lax.axis_size("tm") * lax.axis_size("chan")
    rows_dev, samples = raw.shape
    total = samples // STRIDE
    own = lax.axis_index("tm") * lax.axis_size("chan") + lax.axis_index("chan")
    ids = lax.dynamic_slice_in_dim(row_channel, own * rows_dev, rows_dev).reshape(1, rows_dev)
    packet = jax.ShapeDtypeStruct((devices * 32, LANES), jnp.bfloat16)
    vmem = pl.BlockSpec(memory_space=pltpu.VMEM)
    rows_out, refs_out = pl.pallas_call(
        decimate_kernel,
        out_shape=(packet, packet),
        in_specs=[vmem] * 5,
        out_specs=(vmem, vmem),
        scratch_shapes=[
            pltpu.VMEM((8, BLOCK * STRIDE + 2 * HALO), jnp.float32),
            pltpu.VMEM((total, LANES), jnp.float32),
            pltpu.VMEM((2, devices * 32, LANES), jnp.float32),
        ],
        compiler_params=pltpu.CompilerParams(vmem_limit_bytes=40 << 20),
        name="decimate",
    )(raw, taps.reshape(1, TAPS), ids, ref_channel.reshape(1, NREF), owner_of_row.reshape(1, rows_dev))
    refs_in = lax.all_to_all(refs_out, AXES, 0, 0, tiled=True)
    rows_in = lax.all_to_all(rows_out, AXES, 0, 0, tiled=True)
    refs_mine = pl.pallas_call(
        spread_kernel,
        out_shape=packet,
        in_specs=[vmem],
        out_specs=vmem,
        compiler_params=pltpu.CompilerParams(vmem_limit_bytes=32 << 20),
        name="spread",
    )(refs_in)
    refs_all = lax.all_to_all(refs_mine, AXES, 0, 0, tiled=True)
    return pl.pallas_call(
        correlate_kernel,
        grid=(LAGS,),
        out_shape=jax.ShapeDtypeStruct((1, 2 * devices, LAGS * NREF), jnp.float32),
        in_specs=[vmem, vmem],
        out_specs=pl.BlockSpec((1, 2 * devices, NREF), lambda i: (0, 0, i)),
        scratch_shapes=[
            pltpu.VMEM((devices * 32, LANES), jnp.float32),
            pltpu.VMEM((2 * devices, 2 * total), jnp.bfloat16),
            pltpu.VMEM((NREF, total), jnp.bfloat16),
        ],
        compiler_params=pltpu.CompilerParams(vmem_limit_bytes=40 << 20),
        name="correlate",
    )(rows_in, refs_all)


def solution(mesh):
    in_specs = (P(AXES, None), P(), P(), P(), P(AXES, None))
    out_specs = P(AXES, None, None)
    return jax.shard_map(
        on_device, mesh=mesh, in_specs=in_specs, out_specs=out_specs, check_vma=False
    )
```

time: 251 us -> 100 us (0.40)
  other arithmetic: 97.2 us -> 0 us
  blocking collectives: 115 us -> 54 us
  local copies, waits for them, and re-layouts: 25.4 us -> 4.75 us
  waiting for transfers between devices: 0 us -> 19.7 us
  Pallas kernels: 0 us -> 17.9 us
  matrix products: 11.7 us -> 0 us
  starting transfers between devices: 0 us -> 3.66 us
    psum x1 -> x0, blocking collectives: 78.6 us -> none  [on_device(): lax.psum(jnp.dot(select, decimated, preferred_element_type=jnp.float32),...]
    dot_general x2 -> x0, other arithmetic: 73.4 us -> none  [on_device(): jnp.einsum('rnm,m->rn', pieces[:, q:q + total], table[q], preferred_eleme...]
    all_to_all x0 -> x1, waiting for transfers between devices: none -> 19.7 us  [on_device(): rows_in = lax.all_to_all(rows_out, AXES, 0, 0, tiled=True)]
    pallas_call x0 -> x3, Pallas kernels: none -> 17.9 us  [the longest x1 12.4 us: on_device(): pl.pallas_call(correlate_kernel, grid=(LAGS,), out_shape=jax.ShapeDtypeSt...]
    all_to_all x1 -> x2, blocking collectives: 36.8 us -> 54 us  [the longest x1 31.1 us: on_device(): refs_in = lax.all_to_all(refs_out, AXES, 0, 0, tiled=True)]
    dot_general x17 -> x0, matrix products: 11.7 us -> none  [the longest x16 11.2 us: on_device(): jnp.einsum('rtn,jtn->trj', shifted, ref_slabs, preferred_element_type=jnp...]
    reduce_sum x17 -> x0, other arithmetic: 10 us -> none  [the longest x16 9.85 us: on_device(): terms.append(jnp.sum(rounded.astype(jnp.float32), axis=0))]
    convert_element_type x3 -> x0, other arithmetic: 8.51 us -> none  [the longest x1 5.97 us: on_device(): decimated = accum.astype(jnp.bfloat16)]
  transfers between devices with their start and end apart: 0 -> 1, of which waited for: 0 -> 1; matrix products, arithmetic and copies ran while one was open for 0% -> 0% of each run, Pallas kernels for 0% -> 0%
where the time goes in v1:
time: 100 us
  blocking collectives  54 us (54%)
  waiting for transfers between devices  19.7 us (20%)
  Pallas kernels  17.9 us (18%)
  local copies, waits for them, and re-layouts  4.75 us (5%)
  starting transfers between devices  3.66 us (4%)
    all_to_all x1, blocking collectives, on_device(): refs_in = lax.all_to_all(refs_out, AXES, 0, 0, tiled=True)  31.1 us
    all_to_all x1, blocking collectives, on_device(): refs_all = lax.all_to_all(refs_mine, AXES, 0, 0, tiled=True)  23 us
    all_to_all x1, waiting for transfers between devices, on_device(): rows_in = lax.all_to_all(rows_out, AXES, 0, 0, tiled=True)  19.7 us
    pallas_call x1, Pallas kernels, on_device(): pl.pallas_call(correlate_kernel, grid=(LAGS,), out_shape=jax.ShapeDtypeSt...  12.4 us
    pallas_call x1, Pallas kernels, on_device(): pl.pallas_call(decimate_kernel, out_shape=(packet, packet), in_specs=[vme...  5.28 us
    unnamed x10, local copies, waits for them, and re-layouts  4.68 us
    all_to_all x1, starting transfers between devices, on_device(): rows_in = lax.all_to_all(rows_out, AXES, 0, 0, tiled=True)  3.66 us
  transfers between devices with their start and end apart: 1, of which 1 were waited for; matrix products, arithmetic and copies ran while one was open for 0% of the time, Pallas kernels for 0%

profile of v1, /device:TPU:1, one launch (start us, length us, event | category | flops | bytes accessed | tf_op | source)
XLA Modules:
  0.0 100.0 jit_solution(12910063137148528048)
XLA Ops:
  0.0 0.0 copy-start
  0.0 0.8 copy-done
  0.8 0.1 dynamic-slice_bitcast_fusion.ids_ref
  0.9 0.0 copy-start.1
  0.9 1.9 %copy-done.1 = bf16[96,16384]{1,0:T(8,128)(2,1)S(1)} copy-done((bf16[96,16384]{1,0:T(8,128)(2,1)S(1)}, bf16[96,16384]{1,0:T(8,128)(2,1)}, u32[]{:S(2)}) %copy-start.1) | copy-done | bytes 3145752
  2.8 0.0 copy-start.2
  2.8 0.7 copy-done.2
  3.4 0.0 copy-start.3
  3.4 0.7 copy-done.3
  4.1 0.0 copy-start.4
  4.1 0.7 copy-done.4
  4.8 5.3 %decimate.1 = (bf16[4096,128]{1,0:T(8,128)(2,1)}, bf16[4096,128]{1,0:T(8,128)(2,1)S(1)}) custom-call(bf16[96,16384]{1,0:T(8,128)(2,1)S(1)} %copy-done.1, bf16[1,127]{1,0:T(2,128)(2,1)S(1)} %bitcast.17, s32[1,96]{1,0:T(1,128)S(1)} %dynamic-slice_bitcast_fusion.ids_ref, s32[1,256]{1,0:T(1,128)S(1)} %bitcast.16, s32[1,96]{1,0:T(1,128)S(1)} %bitcast.18), custom_call_target="tpu_custom_call" | custom-call | tf_op jit(solution)/shard_map/decimate/pallas_call | solution.py:115
  10.0 31.1 %all_to_all.33 = bf16[128,32,128]{2,1,0:T(8,128)(2,1)S(1)} all-to-all(bf16[128,32,128]{2,1,0:T(8,128)(2,1)S(1)} %bitcast.15), channel_id=1, replica_groups=mesh['tm'=32,'chan'=4] {'tm','chan'}, dimensions={0} | all-to-all | bytes 2097152 | tf_op jit(solution)/shard_map/all_to_all | solution.py:128
  41.1 3.7 %all-to-all-start = ((bf16[128,32,128]{2,1,0:T(8,128)(2,1)}), bf16[128,32,128]{2,1,0:T(8,128)(2,1)S(1)}, u32[]{:S(2)}, u32[]{:S(2)}) async-start(bf16[128,32,128]{2,1,0:T(8,128)(2,1)} %bitcast.4), calls=%async_computation | async-start | bytes 2097152 | tf_op jit(solution)/shard_map/all_to_all | solution.py:129
  44.8 0.2 spread.1
  45.0 19.7 %all-to-all-done = bf16[128,32,128]{2,1,0:T(8,128)(2,1)S(1)} async-done(((bf16[128,32,128]{2,1,0:T(8,128)(2,1)}), bf16[128,32,128]{2,1,0:T(8,128)(2,1)S(1)}, u32[]{:S(2)}, u32[]{:S(2)}) %all-to-all-start) | async-done | bytes 1048608 | tf_op jit(solution)/shard_map/all_to_all | solution.py:129
  64.7 23.0 %all_to_all.34 = bf16[128,32,128]{2,1,0:T(8,128)(2,1)S(1)} all-to-all(bf16[128,32,128]{2,1,0:T(8,128)(2,1)S(1)} %bitcast.12), channel_id=1, replica_groups=mesh['tm'=32,'chan'=4] {'tm','chan'}, dimensions={0} | all-to-all | bytes 2097152 | tf_op jit(solution)/shard_map/all_to_all | solution.py:138
  87.6 12.4 %correlate.1 = f32[1,256,4096]{2,1,0:T(8,128)} custom-call(bf16[4096,128]{1,0:T(8,128)(2,1)S(1)} %bitcast.13, bf16[4096,128]{1,0:T(8,128)(2,1)S(1)} %bitcast.14), custom_call_target="tpu_custom_call" | custom-call | tf_op jit(solution)/shard_map/correlate/pallas_call | solution.py:139
Async XLA Ops:
  0.0 0.8 copy-start
  0.9 1.9 %copy-start.1 = (bf16[96,16384]{1,0:T(8,128)(2,1)S(1)}, bf16[96,16384]{1,0:T(8,128)(2,1)}, u32[]{:S(2)}) copy-start(bf16[96,16384]{1,0:T(8,128)(2,1)} %raw_ref.1) | copy-start | bytes 9437188
  2.8 0.7 copy-start.2
  3.4 0.7 copy-start.3
  4.1 0.7 copy-start.4
  41.1 23.6 %all-to-all-start = ((bf16[128,32,128]{2,1,0:T(8,128)(2,1)}), bf16[128,32,128]{2,1,0:T(8,128)(2,1)S(1)}, u32[]{:S(2)}, u32[]{:S(2)}) async-start(bf16[128,32,128]{2,1,0:T(8,128)(2,1)} %bitcast.4), calls=%async_computation | async-start | bytes 2097152 | tf_op jit(solution)/shard_map/all_to_all | solution.py:129

commit v2 on v0

v2 whole, which is shorter than its diff:
```python
import math

import jax
import jax.numpy as jnp
from jax import lax
from jax.experimental import pallas as pl
from jax.experimental.pallas import tpu as pltpu
from jax.sharding import Mesh
from jax.sharding import PartitionSpec as P

LAGS = 16
TAPS = 127
STRIDE = 8
NREF = 256
LANES = 128
BLOCK = 128
HALO = 128
CHIPS = 64
AXES = ("x", "z", "core", "chan")
SAME = ("x", "z", "chan")
NT = (((1,), (1,)), ((), ()))
VMEM = pl.BlockSpec(memory_space=pltpu.VMEM)
HBM = pl.BlockSpec(memory_space=pltpu.HBM)
F32, BF16 = jnp.float32, jnp.bfloat16


def dot_nt(a, b):
    return lax.dot_general(a, b, NT, preferred_element_type=F32)


def params(mib=48):
    return pltpu.CompilerParams(vmem_limit_bytes=mib << 20)


def iota(shape, dim):
    return lax.broadcasted_iota(jnp.int32, shape, dim)


def decimate_kernel(raw_hbm, taps_hbm, ids_hbm, refch_hbm, planes_ref, keep_ref, give_ref,
                    raw, taps, ids, refch, line, dect, stage, raw_sem, small_sem):
    rows, samples = raw.shape
    blocks = samples // (BLOCK * STRIDE)
    chunk = BLOCK * STRIDE
    loads = [
        pltpu.make_async_copy(
            raw_hbm.at[:, pl.ds(m * chunk, chunk)], raw.at[:, pl.ds(m * chunk, chunk)], raw_sem.at[m]
        )
        for m in range(blocks)
    ]
    small = [
        pltpu.make_async_copy(taps_hbm, taps, small_sem.at[0]),
        pltpu.make_async_copy(ids_hbm, ids, small_sem.at[1]),
        pltpu.make_async_copy(refch_hbm, refch, small_sem.at[2]),
    ]
    for copy in small + loads:
        copy.start()
    core = lax.axis_index("core")
    own = lax.axis_index(AXES)
    window = chunk + 2 * HALO
    small[0].wait()
    line[...] = jnp.zeros_like(line)
    line[0:1, 0:TAPS] = taps[...].astype(F32)
    band = pltpu.roll(
        jnp.broadcast_to(line[0:1, :], (BLOCK, window)), HALO - TAPS // 2, 1, stride=STRIDE, stride_axis=0
    ).astype(BF16)
    small[1].wait()
    small[2].wait()
    at = own * rows
    line0 = at // LANES
    line1 = jnp.minimum(line0 + 1, ids.shape[0] - 1)
    shift = at - line0 * LANES
    turn = LANES - shift
    pair = [
        pltpu.roll(jnp.broadcast_to(ids[pl.ds(i, 1), :], (8, LANES)), turn, 1) for i in (line0, line1)
    ]
    mine = jnp.where(iota((8, LANES), 1) < turn, pair[0], pair[1])[0:1, :rows]
    refcol = jnp.transpose(jnp.broadcast_to(refch[...], (LANES, NREF)))[:, :rows]
    select = jnp.where(refcol == mine, 1.0, 0.0).astype(BF16)
    for m in range(blocks):
        lo, hi = m * chunk - HALO, (m + 1) * chunk + HALO
        first, last = max(lo, 0), min(hi, samples)
        if m == 0:
            loads[0].wait()
        if m + 1 < blocks:
            loads[m + 1].wait()
        part = dot_nt(band[:, first - lo : last - lo], raw[:, first:last])
        dect[m * BLOCK : (m + 1) * BLOCK, :rows] = part.astype(BF16).astype(F32)
    for b in range(0, LAGS, 2):
        planes = jnp.concatenate(
            [dect[pl.ds(b + h, LANES, stride=LAGS), :] for h in range(2)], axis=0
        ).astype(BF16)
        planes_ref[b * LANES : (b + 2) * LANES, :] = planes
        picked = dot_nt(select, planes[:, :rows])
        for g in range(4):
            for h in range(2):
                stage[g // 2, pl.ds((g % 2) * LAGS + b + h, CHIPS, stride=2 * LAGS), :] = picked[
                    g * CHIPS : (g + 1) * CHIPS, h * LANES : (h + 1) * LANES
                ]
    shape = (CHIPS, 2 * LAGS, LANES)
    keep_ref[...] = stage[core].astype(BF16).reshape(shape)
    give_ref[...] = stage[1 - core].astype(BF16).reshape(shape)


def route_kernel(planes_ref, owner_ref, keep_ref, got_ref, packet_ref, stage):
    rows = owner_ref.shape[1]
    owner = owner_ref[...]
    chip = iota((CHIPS, rows), 0)
    before = (iota((rows, rows), 0) < iota((rows, rows), 1)).astype(BF16)
    parts = []
    for core in range(2):
        device = (chip // 4) * 8 + core * 4 + chip % 4
        one = jnp.where(device == owner, 1.0, 0.0)
        rank = jnp.dot(one.astype(BF16), before, preferred_element_type=F32)
        first = jnp.where(rank < 0.5, one, 0.0)
        parts += [first, one - first]
    select = jnp.concatenate(parts, axis=0).astype(BF16)
    for b in range(0, LAGS, 2):
        picked = dot_nt(select, planes_ref[b * LANES : (b + 2) * LANES, :][:, :rows])
        for g in range(4):
            for h in range(2):
                stage[pl.ds(g * LAGS + b + h, CHIPS, stride=4 * LAGS), :] = picked[
                    g * CHIPS : (g + 1) * CHIPS, h * LANES : (h + 1) * LANES
                ]
    packet_ref[:, : 4 * LAGS, :] = stage[...].astype(BF16).reshape(CHIPS, 4 * LAGS, LANES)
    packet_ref[:, 4 * LAGS :, :] = (keep_ref[...].astype(F32) + got_ref[...].astype(F32)).astype(BF16)


def spread_kernel(arrived_ref, spread_ref, give_ref):
    core = lax.axis_index("core")
    total = jnp.sum(arrived_ref[:, 4 * LAGS :, :].astype(F32), axis=0, keepdims=True)
    spread_ref[...] = jnp.broadcast_to(total, spread_ref.shape).astype(BF16)
    other = pl.multiple_of((1 - core) * 2 * LAGS, 2 * LAGS)
    give_ref[...] = arrived_ref[:, pl.ds(other, 2 * LAGS), :]


def widen_kernel(arrived_ref, got_ref, ext_ref, wide):
    core = lax.axis_index("core")
    size = CHIPS * 2 * LAGS
    mine = pl.multiple_of(core * 2 * LAGS, 2 * LAGS)
    wide[core] = arrived_ref[:, pl.ds(mine, 2 * LAGS), :].astype(F32).reshape(size, LANES)
    wide[1 - core] = got_ref[...].astype(F32).reshape(size, LANES)
    total = LAGS * LANES
    last_lane = iota((4 * CHIPS, LANES), 1) == LANES - 1
    for b in range(LAGS):
        halves = [wide[c, pl.ds(b, 2 * CHIPS, stride=LAGS), :].reshape(CHIPS // 4, 1, 8, LANES) for c in range(2)]
        plane = jnp.concatenate(halves, axis=1).reshape(4 * CHIPS, LANES)
        ext_ref[:, b * LANES : (b + 1) * LANES] = plane.astype(BF16)
        moved = jnp.where(last_lane, 0.0, pltpu.roll(plane, LANES - 1, 1))
        ext_ref[:, total + b * LANES : total + (b + 1) * LANES] = moved.astype(BF16)


def correlate_kernel(per, ext_ref, own_ref, other_ref, out_ref, wide, ref_planes):
    step = pl.program_id(0)
    total = LAGS * LANES
    size = CHIPS * 2 * LAGS

    @pl.when(step == 0)
    def _():
        core = lax.axis_index("core")
        wide[core] = own_ref[...].astype(F32).reshape(size, LANES)
        wide[1 - core] = other_ref[...].astype(F32).reshape(size, LANES)
        for g in range(4):
            for b in range(LAGS):
                ref_planes[g * CHIPS : (g + 1) * CHIPS, b * LANES : (b + 1) * LANES] = wide[
                    g // 2, pl.ds((g % 2) * LAGS + b, CHIPS, stride=2 * LAGS), :
                ].astype(BF16)

    start = pl.multiple_of((step * per + 1) * LANES, LANES)
    lagged = jnp.concatenate([ext_ref[:, pl.ds(start + i * LANES, total)] for i in range(per)], axis=0)
    sums = dot_nt(lagged, ref_planes[...]) * (1.0 / math.sqrt(total))
    for i in range(per):
        out_ref[0, :, i * NREF : (i + 1) * NREF] = sums[i * 4 * CHIPS : (i + 1) * 4 * CHIPS]


def swap_cores(x):
    return lax.ppermute(x, "core", [(0, 1), (1, 0)])


def on_device(raw, taps, row_channel, ref_channel, owner_of_row):
    rows_dev, samples = raw.shape
    total = samples // STRIDE
    window = BLOCK * STRIDE + 2 * HALO
    half = jax.ShapeDtypeStruct((CHIPS, 2 * LAGS, LANES), BF16)
    ids = row_channel.reshape(-1, LANES)
    planes, keep, give = pl.pallas_call(
        decimate_kernel,
        out_shape=(jax.ShapeDtypeStruct((total, LANES), BF16), half, half),
        in_specs=[HBM] * 4,
        out_specs=(VMEM, VMEM, VMEM),
        scratch_shapes=[
            pltpu.VMEM((rows_dev, samples), BF16),
            pltpu.VMEM((1, TAPS), BF16),
            pltpu.VMEM(ids.shape, jnp.int32),
            pltpu.VMEM((1, NREF), jnp.int32),
            pltpu.VMEM((8, window), F32),
            pltpu.VMEM((total, LANES), F32),
            pltpu.VMEM((2, CHIPS * 2 * LAGS, LANES), F32),
            pltpu.SemaphoreType.DMA((samples // (BLOCK * STRIDE),)),
            pltpu.SemaphoreType.DMA((3,)),
        ],
        compiler_params=params(60),
        name="decimate",
    )(raw, taps.reshape(1, TAPS), ids, ref_channel.reshape(1, NREF))
    got = swap_cores(give)
    packet = pl.pallas_call(
        route_kernel,
        out_shape=jax.ShapeDtypeStruct((CHIPS, 6 * LAGS, LANES), BF16),
        in_specs=[VMEM] * 4,
        out_specs=VMEM,
        scratch_shapes=[pltpu.VMEM((CHIPS * 4 * LAGS, LANES), F32)],
        compiler_params=params(),
        name="route",
    )(planes, owner_of_row.reshape(1, rows_dev), keep, got)
    arrived = lax.all_to_all(packet, SAME, 0, 0, tiled=True)
    spread, rows_give = pl.pallas_call(
        spread_kernel,
        out_shape=(half, half),
        in_specs=[VMEM],
        out_specs=(VMEM, VMEM),
        compiler_params=params(),
        name="spread",
    )(arrived)
    refs_own = lax.all_to_all(spread, SAME, 0, 0, tiled=True)
    rows_got = swap_cores(rows_give)
    ext = pl.pallas_call(
        widen_kernel,
        out_shape=jax.ShapeDtypeStruct((4 * CHIPS, 2 * total), BF16),
        in_specs=[VMEM, VMEM],
        out_specs=VMEM,
        scratch_shapes=[pltpu.VMEM((2, CHIPS * 2 * LAGS, LANES), F32)],
        compiler_params=params(),
        name="widen",
    )(arrived, rows_got)
    refs_other = swap_cores(refs_own)
    per = 4
    return pl.pallas_call(
        lambda *refs: correlate_kernel(per, *refs),
        grid=(LAGS // per,),
        out_shape=jax.ShapeDtypeStruct((1, 4 * CHIPS, LAGS * NREF), F32),
        in_specs=[VMEM, VMEM, VMEM],
        out_specs=pl.BlockSpec((1, 4 * CHIPS, per * NREF), lambda i: (0, 0, i)),
        scratch_shapes=[
            pltpu.VMEM((2, CHIPS * 2 * LAGS, LANES), F32),
            pltpu.VMEM((NREF, total), BF16),
        ],
        compiler_params=params(),
        name="correlate",
    )(ext, refs_own, refs_other)


def solution(mesh):
    parts = Mesh(mesh.devices.reshape(4, 4, 2, 4), AXES)
    return jax.shard_map(
        on_device,
        mesh=parts,
        in_specs=(P(AXES, None), P(), P(), P(), P(AXES, None)),
        out_specs=P(AXES, None, None),
        check_vma=False,
    )
```

time: 251 us -> 80.4 us (0.32)
  other arithmetic: 97.2 us -> 0 us
  blocking collectives: 115 us -> 33.4 us
  local copies, waits for them, and re-layouts: 25.4 us -> 2.09 us
  Pallas kernels: 0 us -> 21.1 us
  starting transfers between devices: 0 us -> 12.3 us
  matrix products: 11.7 us -> 0 us
  waiting for transfers between devices: 0 us -> 11.1 us
    psum x1 -> x0, blocking collectives: 78.6 us -> none  [on_device(): lax.psum(jnp.dot(select, decimated, preferred_element_type=jnp.float32),...]
    dot_general x2 -> x0, other arithmetic: 73.4 us -> none  [on_device(): jnp.einsum('rnm,m->rn', pieces[:, q:q + total], table[q], preferred_eleme...]
    pallas_call x0 -> x5, Pallas kernels: none -> 21.1 us  [the longest x1 9.45 us: on_device(): pl.pallas_call(decimate_kernel, out_shape=(jax.ShapeDtypeStruct((total, L...]
    dot_general x17 -> x0, matrix products: 11.7 us -> none  [the longest x16 11.2 us: on_device(): jnp.einsum('rtn,jtn->trj', shifted, ref_slabs, preferred_element_type=jnp...]
    reduce_sum x17 -> x0, other arithmetic: 10 us -> none  [the longest x16 9.85 us: on_device(): terms.append(jnp.sum(rounded.astype(jnp.float32), axis=0))]
    all_to_all x0 -> x1, waiting for transfers between devices: none -> 9.09 us  [on_device(): refs_own = lax.all_to_all(spread, SAME, 0, 0, tiled=True)]
    convert_element_type x3 -> x0, other arithmetic: 8.51 us -> none  [the longest x1 5.97 us: on_device(): decimated = accum.astype(jnp.bfloat16)]
    unnamed x64 -> x6, local copies, waits for them, and re-layouts: 9.43 us -> 2.09 us
  transfers between devices with their start and end apart: 0 -> 4, of which waited for: 0 -> 3; matrix products, arithmetic and copies ran while one was open for 0% -> 0% of each run, Pallas kernels for 0% -> 2%
where the time goes in v2:
time: 80.4 us; the launch traced here: 80 us
  blocking collectives  33.4 us (42%)
  Pallas kernels  21.1 us (26%)
  starting transfers between devices  12.3 us (15%)
  waiting for transfers between devices  11.1 us (14%)
  local copies, waits for them, and re-layouts  2.09 us (3%)
    all_to_all x1, blocking collectives, on_device(): arrived = lax.all_to_all(packet, SAME, 0, 0, tiled=True)  33.4 us
    pallas_call x1, Pallas kernels, on_device(): pl.pallas_call(decimate_kernel, out_shape=(jax.ShapeDtypeStruct((total, L...  9.45 us
    all_to_all x1, waiting for transfers between devices, on_device(): refs_own = lax.all_to_all(spread, SAME, 0, 0, tiled=True)  9.09 us
    pallas_call x1, Pallas kernels, on_device(): pl.pallas_call(lambda *refs: correlate_kernel(per, *refs), grid=(LAGS //...  7.61 us
    ppermute x3, starting transfers between devices, swap_cores(): return lax.ppermute(x, 'core', [(0, 1), (1, 0)])  6.47 us
    all_to_all x1, starting transfers between devices, on_device(): refs_own = lax.all_to_all(spread, SAME, 0, 0, tiled=True)  5.82 us
    unnamed x6, local copies, waits for them, and re-layouts  2.09 us
    ppermute x3, waiting for transfers between devices, swap_cores(): return lax.ppermute(x, 'core', [(0, 1), (1, 0)])  2.02 us
  transfers between devices with their start and end apart: 4, of which 3 were waited for; matrix products, arithmetic and copies ran while one was open for 0% of the time, Pallas kernels for 2%

profile of v2, /device:TPU:1, one launch (start us, length us, event | category | flops | bytes accessed | tf_op | source)
XLA Modules:
  0.0 80.0 jit_solution(11481704530005175622)
XLA Ops:
  0.0 0.0 copy-start.2
  0.0 9.4 %decimate.1 = (bf16[2048,128]{1,0:T(8,128)(2,1)}, bf16[64,32,128]{2,1,0:T(8,128)(2,1)}, bf16[64,32,128]{2,1,0:T(8,128)(2,1)}) custom-call(bf16[96,16384]{1,0:T(8,128)(2,1)} %raw_hbm.1, bf16[1,127]{1,0:T(2,128)(2,1)} %bitcast.7, s32[96,128]{1,0:T(8,128)} %bitcast.5, s32[1,256]{1,0:T(1,128)} %bitcast.6), custom_call_target="tpu_custom_call" | custom-call | tf_op jit(solution)/shard_map/decimate/pallas_call | solution.py:185
  9.5 1.5 %collective-permute-start = (bf16[64,32,128]{2,1,0:T(8,128)(2,1)}, bf16[64,32,128]{2,1,0:T(8,128)(2,1)S(1)}, u32[]{:S(2)}, u32[]{:S(2)}) collective-permute-start(bf16[64,32,128]{2,1,0:T(8,128)(2,1)} %get-tuple-element.12), channel_id=1, source_target_pairs={{0,4},{4,0},{1,5},{5,1},{2,6},{6,2},{3,7},{7,3},{8,12},{12,8},{9,1... | collective-permute-start | bytes 1572872 | tf_op jit(solution)/shard_map/ppermute | solution.py:176
  11.0 1.7 %collective-permute-done.got_ref = bf16[64,32,128]{2,1,0:T(8,128)(2,1)S(1)} collective-permute-done((bf16[64,32,128]{2,1,0:T(8,128)(2,1)}, bf16[64,32,128]{2,1,0:T(8,128)(2,1)S(1)}, u32[]{:S(2)}, u32[]{:S(2)}) %collective-permute-start) | collective-permute-done | bytes 524320 | tf_op jit(solution)/shard_map/ppermute | solution.py:176
  12.7 0.0 copy-done.2
  12.7 0.0 copy-start
  12.7 1.0 %copy-done = bf16[2048,128]{1,0:T(8,128)(2,1)S(1)} copy-done((bf16[2048,128]{1,0:T(8,128)(2,1)S(1)}, bf16[2048,128]{1,0:T(8,128)(2,1)}, u32[]{:S(2)}) %copy-start) | copy-done | bytes 524312
  13.8 0.0 copy-start.1
  13.8 1.0 %copy-done.1 = bf16[64,32,128]{2,1,0:T(8,128)(2,1)S(1)} copy-done((bf16[64,32,128]{2,1,0:T(8,128)(2,1)S(1)}, bf16[64,32,128]{2,1,0:T(8,128)(2,1)}, u32[]{:S(2)}) %copy-start.1) | copy-done | bytes 524312
  14.8 1.9 %route.1 = bf16[64,96,128]{2,1,0:T(8,128)(2,1)S(1)} custom-call(bf16[2048,128]{1,0:T(8,128)(2,1)S(1)} %copy-done, s32[1,96]{1,0:T(1,128)S(1)} %bitcast.4, bf16[64,32,128]{2,1,0:T(8,128)(2,1)S(1)} %copy-done.1, bf16[64,32,128]{2,1,0:T(8,128)(2,1)S(1)} %collective-permute-done.got_ref), custom_call_target="tpu_custom_call" | custom-call | tf_op jit(solution)/shard_map/route/pallas_call | solution.py:205
  16.7 33.4 %all_to_all.10.arrived_ref = bf16[64,96,128]{2,1,0:T(8,128)(2,1)S(1)} all-to-all(bf16[64,96,128]{2,1,0:T(8,128)(2,1)S(1)} %route.1), channel_id=1, replica_groups=mesh['x'=4,'z'=4,'core'=2,'chan'=4] {'x','z','chan'}, dimensions={0} | all-to-all | bytes 3145728 | tf_op jit(solution)/shard_map/all_to_all | solution.py:214
  50.1 0.9 %spread.1 = (bf16[64,32,128]{2,1,0:T(8,128)(2,1)}, bf16[64,32,128]{2,1,0:T(8,128)(2,1)S(1)}) custom-call(bf16[64,96,128]{2,1,0:T(8,128)(2,1)S(1)} %all_to_all.10.arrived_ref), custom_call_target="tpu_custom_call" | custom-call | tf_op jit(solution)/shard_map/spread/pallas_call | solution.py:215
  51.0 5.8 %all-to-all-start.1 = ((bf16[64,32,128]{2,1,0:T(8,128)(2,1)}), bf16[64,32,128]{2,1,0:T(8,128)(2,1)S(1)}, u32[]{:S(2)}, u32[]{:S(2)}) async-start(bf16[64,32,128]{2,1,0:T(8,128)(2,1)} %get-tuple-element.14), calls=%async_computation.1 | async-start | bytes 1048576 | tf_op jit(solution)/shard_map/all_to_all | solution.py:223
  56.8 1.8 %collective-permute-start.1 = (bf16[64,32,128]{2,1,0:T(8,128)(2,1)S(1)}, bf16[64,32,128]{2,1,0:T(8,128)(2,1)S(1)}, u32[]{:S(2)}, u32[]{:S(2)}) collective-permute-start(bf16[64,32,128]{2,1,0:T(8,128)(2,1)S(1)} %get-tuple-element.13), channel_id=1, source_target_pairs={{0,4},{4,0},{1,5},{5,1},{2,6},{6,2},{3,7},{7,3},{8,12},{12,8},{9,1... | collective-permute-start | bytes 1572872 | tf_op jit(solution)/shard_map/ppermute | solution.py:176
  58.6 9.1 %all-to-all-done.1.refs_1_ = bf16[64,32,128]{2,1,0:T(8,128)(2,1)S(1)} async-done(((bf16[64,32,128]{2,1,0:T(8,128)(2,1)}), bf16[64,32,128]{2,1,0:T(8,128)(2,1)S(1)}, u32[]{:S(2)}, u32[]{:S(2)}) %all-to-all-start.1) | async-done | bytes 524320 | tf_op jit(solution)/shard_map/all_to_all | solution.py:223
  67.7 3.2 %collective-permute-start.2 = (bf16[64,32,128]{2,1,0:T(8,128)(2,1)S(1)}, bf16[64,32,128]{2,1,0:T(8,128)(2,1)S(1)}, u32[]{:S(2)}, u32[]{:S(2)}) collective-permute-start(bf16[64,32,128]{2,1,0:T(8,128)(2,1)S(1)} %all-to-all-done.1.refs_1_), channel_id=1, source_target_pairs={{0,4},{4,0},{1,5},{5,1},{2,6},{6,2},{3,7},{7,3},{8,12},{12,8},{9,1... | collective-permute-start | bytes 1572872 | tf_op jit(solution)/shard_map/ppermute | solution.py:176
  70.9 0.0 collective-permute-done.1.got_ref
  70.9 1.3 %widen.1.refs_0_ = bf16[256,4096]{1,0:T(8,128)(2,1)S(1)} custom-call(bf16[64,96,128]{2,1,0:T(8,128)(2,1)S(1)} %all_to_all.10.arrived_ref, bf16[64,32,128]{2,1,0:T(8,128)(2,1)S(1)} %collective-permute-done.1.got_ref), custom_call_target="tpu_custom_call" | custom-call | tf_op jit(solution)/shard_map/widen/pallas_call | solution.py:225
  72.2 0.3 collective-permute-done.2.refs_2_
  72.4 7.6 %correlate.1 = f32[1,256,4096]{2,1,0:T(8,128)} custom-call(bf16[256,4096]{1,0:T(8,128)(2,1)S(1)} %widen.1.refs_0_, bf16[64,32,128]{2,1,0:T(8,128)(2,1)S(1)} %all-to-all-done.1.refs_1_, bf16[64,32,128]{2,1,0:T(8,128)(2,1)S(1)} %collective-permute-done.2.refs_2_), custom_call_target="tpu_custom_call" | custom-call | tf_op jit(solution)/shard_map/correlate/pallas_call | solution.py:236
Async XLA Ops:
  0.0 12.7 %copy-start.2 = (s32[96,1]{0,1:T(1,128)S(1)}, s32[96,1]{0,1:T(1,128)}, u32[]{:S(2)}) copy-start(s32[96,1]{0,1:T(1,128)} %param.9) | copy-start | bytes 1156
  9.5 3.3 %collective-permute-start = (bf16[64,32,128]{2,1,0:T(8,128)(2,1)}, bf16[64,32,128]{2,1,0:T(8,128)(2,1)S(1)}, u32[]{:S(2)}, u32[]{:S(2)}) collective-permute-start(bf16[64,32,128]{2,1,0:T(8,128)(2,1)} %get-tuple-element.12), channel_id=1, source_target_pairs={{0,4},{4,0},{1,5},{5,1},{2,6},{6,2},{3,7},{7,3},{8,12},{12,8},{9,1... | collective-permute-start | bytes 1572872 | tf_op jit(solution)/shard_map/ppermute | solution.py:176
  12.7 1.0 %copy-start = (bf16[2048,128]{1,0:T(8,128)(2,1)S(1)}, bf16[2048,128]{1,0:T(8,128)(2,1)}, u32[]{:S(2)}) copy-start(bf16[2048,128]{1,0:T(8,128)(2,1)} %get-tuple-element.10.planes_ref) | copy-start | bytes 1572868
  13.8 1.0 %copy-start.1 = (bf16[64,32,128]{2,1,0:T(8,128)(2,1)S(1)}, bf16[64,32,128]{2,1,0:T(8,128)(2,1)}, u32[]{:S(2)}) copy-start(bf16[64,32,128]{2,1,0:T(8,128)(2,1)} %get-tuple-element.11.keep_ref) | copy-start | bytes 1572868
  51.0 16.7 %all-to-all-start.1 = ((bf16[64,32,128]{2,1,0:T(8,128)(2,1)}), bf16[64,32,128]{2,1,0:T(8,128)(2,1)S(1)}, u32[]{:S(2)}, u32[]{:S(2)}) async-start(bf16[64,32,128]{2,1,0:T(8,128)(2,1)} %get-tuple-element.14), calls=%async_computation.1 | async-start | bytes 1048576 | tf_op jit(solution)/shard_map/all_to_all | solution.py:223
  56.8 14.1 %collective-permute-start.1 = (bf16[64,32,128]{2,1,0:T(8,128)(2,1)S(1)}, bf16[64,32,128]{2,1,0:T(8,128)(2,1)S(1)}, u32[]{:S(2)}, u32[]{:S(2)}) collective-permute-start(bf16[64,32,128]{2,1,0:T(8,128)(2,1)S(1)} %get-tuple-element.13), channel_id=1, source_target_pairs={{0,4},{4,0},{1,5},{5,1},{2,6},{6,2},{3,7},{7,3},{8,12},{12,8},{9,1... | collective-permute-start | bytes 1572872 | tf_op jit(solution)/shard_map/ppermute | solution.py:176
  67.7 4.7 %collective-permute-start.2 = (bf16[64,32,128]{2,1,0:T(8,128)(2,1)S(1)}, bf16[64,32,128]{2,1,0:T(8,128)(2,1)S(1)}, u32[]{:S(2)}, u32[]{:S(2)}) collective-permute-start(bf16[64,32,128]{2,1,0:T(8,128)(2,1)S(1)} %all-to-all-done.1.refs_1_), channel_id=1, source_target_pairs={{0,4},{4,0},{1,5},{5,1},{2,6},{6,2},{3,7},{7,3},{8,12},{12,8},{9,1... | collective-permute-start | bytes 1572872 | tf_op jit(solution)/shard_map/ppermute | solution.py:176

commit v3 on v2

--- a/solution.py
+++ b/solution.py
@@ -36,16 +36,18 @@
     return lax.broadcasted_iota(jnp.int32, shape, dim)
 
 
-def decimate_kernel(raw_hbm, taps_hbm, ids_hbm, refch_hbm, planes_ref, keep_ref, give_ref,
-                    raw, taps, ids, refch, line, dect, stage, raw_sem, small_sem):
-    rows, samples = raw.shape
-    blocks = samples // (BLOCK * STRIDE)
+def decimate_kernel(raw_hbm, taps_hbm, ids_hbm, refch_hbm, dec_ref, keep_ref, give_ref,
+                    raw, taps, ids, refch, line, dec, stage, raw_sem, small_sem):
+    rows = dec_ref.shape[0]
+    groups = raw_sem.shape[0]
     chunk = BLOCK * STRIDE
+    window = chunk + 2 * HALO
+    span = raw_hbm.shape[1] // groups
     loads = [
         pltpu.make_async_copy(
-            raw_hbm.at[:, pl.ds(m * chunk, chunk)], raw.at[:, pl.ds(m * chunk, chunk)], raw_sem.at[m]
+            raw_hbm.at[:, pl.ds(m * span, span)], raw.at[:, pl.ds(HALO + m * span, span)], raw_sem.at[m]
         )
-        for m in range(blocks)
+        for m in range(groups)
     ]
     small = [
         pltpu.make_async_copy(taps_hbm, taps, small_sem.at[0]),
@@ -56,41 +58,51 @@
         copy.start()
     core = lax.axis_index("core")
     own = lax.axis_index(AXES)
-    window = chunk + 2 * HALO
+    raw[:, :HALO] = jnp.zeros((rows, HALO), BF16)
+    raw[:, raw.shape[1] - HALO :] = jnp.zeros((rows, HALO), BF16)
+    line[...] = jnp.zeros_like(line)
     small[0].wait()
-    line[...] = jnp.zeros_like(line)
     line[0:1, 0:TAPS] = taps[...].astype(F32)
     band = pltpu.roll(
         jnp.broadcast_to(line[0:1, :], (BLOCK, window)), HALO - TAPS // 2, 1, stride=STRIDE, stride_axis=0
-    ).astype(BF16)
+    )
+    band = jnp.transpose(band).astype(BF16)
     small[1].wait()
     small[2].wait()
     at = own * rows
     line0 = at // LANES
     line1 = jnp.minimum(line0 + 1, ids.shape[0] - 1)
-    shift = at - line0 * LANES
-    turn = LANES - shift
+    turn = LANES - (at - line0 * LANES)
     pair = [
         pltpu.roll(jnp.broadcast_to(ids[pl.ds(i, 1), :], (8, LANES)), turn, 1) for i in (line0, line1)
     ]
     mine = jnp.where(iota((8, LANES), 1) < turn, pair[0], pair[1])[0:1, :rows]
     refcol = jnp.transpose(jnp.broadcast_to(refch[...], (LANES, NREF)))[:, :rows]
     select = jnp.where(refcol == mine, 1.0, 0.0).astype(BF16)
-    for m in range(blocks):
-        lo, hi = m * chunk - HALO, (m + 1) * chunk + HALO
-        first, last = max(lo, 0), min(hi, samples)
-        if m == 0:
-            loads[0].wait()
-        if m + 1 < blocks:
+    per = span // chunk
+    loads[0].wait()
+    for m in range(groups):
+        if m + 1 < groups:
             loads[m + 1].wait()
-        part = dot_nt(band[:, first - lo : last - lo], raw[:, first:last])
-        dect[m * BLOCK : (m + 1) * BLOCK, :rows] = part.astype(BF16).astype(F32)
+        windows = [raw[:, pl.ds((m * per + i) * chunk, window)] for i in range(per)]
+        part = jnp.dot(jnp.concatenate(windows, axis=0), band, preferred_element_type=F32).astype(BF16)
+        for i in range(per):
+            at = (m * per + i) * LANES
+            dec[:, at : at + LANES] = part[i * rows : (i + 1) * rows].astype(F32)
+    lane = iota((16, LANES), 1)
+    for r in range(0, rows, 16):
+        pieces = [dec[r : r + 16, m * LANES : (m + 1) * LANES] for m in range(LAGS)]
+        for k in (1, 2, 4, 8):
+            low = (lane & k) == 0
+            for t in range(LAGS):
+                if not t & k:
+                    x, y = pieces[t], pieces[t | k]
+                    pieces[t] = jnp.where(low, x, pltpu.roll(y, k, 1))
+                    pieces[t | k] = jnp.where(low, pltpu.roll(x, LANES - k, 1), y)
+        for b in range(LAGS):
+            dec_ref[r : r + 16, b * LANES : (b + 1) * LANES] = pieces[b].astype(BF16)
     for b in range(0, LAGS, 2):
-        planes = jnp.concatenate(
-            [dect[pl.ds(b + h, LANES, stride=LAGS), :] for h in range(2)], axis=0
-        ).astype(BF16)
-        planes_ref[b * LANES : (b + 2) * LANES, :] = planes
-        picked = dot_nt(select, planes[:, :rows])
+        picked = jnp.dot(select, dec_ref[:, b * LANES : (b + 2) * LANES], preferred_element_type=F32)
         for g in range(4):
             for h in range(2):
                 stage[g // 2, pl.ds((g % 2) * LAGS + b + h, CHIPS, stride=2 * LAGS), :] = picked[
@@ -101,7 +113,7 @@
     give_ref[...] = stage[1 - core].astype(BF16).reshape(shape)
 
 
-def route_kernel(planes_ref, owner_ref, keep_ref, got_ref, packet_ref, stage):
+def route_kernel(dec_ref, owner_ref, packet_ref, stage):
     rows = owner_ref.shape[1]
     owner = owner_ref[...]
     chip = iota((CHIPS, rows), 0)
@@ -115,13 +127,17 @@
         parts += [first, one - first]
     select = jnp.concatenate(parts, axis=0).astype(BF16)
     for b in range(0, LAGS, 2):
-        picked = dot_nt(select, planes_ref[b * LANES : (b + 2) * LANES, :][:, :rows])
+        picked = jnp.dot(select, dec_ref[:, b * LANES : (b + 2) * LANES], preferred_element_type=F32)
         for g in range(4):
             for h in range(2):
                 stage[pl.ds(g * LAGS + b + h, CHIPS, stride=4 * LAGS), :] = picked[
                     g * CHIPS : (g + 1) * CHIPS, h * LANES : (h + 1) * LANES
                 ]
     packet_ref[:, : 4 * LAGS, :] = stage[...].astype(BF16).reshape(CHIPS, 4 * LAGS, LANES)
+
+
+def add_refs_kernel(packet_in, keep_ref, got_ref, packet_ref):
+    del packet_in
     packet_ref[:, 4 * LAGS :, :] = (keep_ref[...].astype(F32) + got_ref[...].astype(F32)).astype(BF16)
 
 
@@ -140,12 +156,15 @@
     wide[core] = arrived_ref[:, pl.ds(mine, 2 * LAGS), :].astype(F32).reshape(size, LANES)
     wide[1 - core] = got_ref[...].astype(F32).reshape(size, LANES)
     total = LAGS * LANES
-    last_lane = iota((4 * CHIPS, LANES), 1) == LANES - 1
+    lane = iota((4 * CHIPS, LANES), 1)
     for b in range(LAGS):
         halves = [wide[c, pl.ds(b, 2 * CHIPS, stride=LAGS), :].reshape(CHIPS // 4, 1, 8, LANES) for c in range(2)]
         plane = jnp.concatenate(halves, axis=1).reshape(4 * CHIPS, LANES)
         ext_ref[:, b * LANES : (b + 1) * LANES] = plane.astype(BF16)
-        moved = jnp.where(last_lane, 0.0, pltpu.roll(plane, LANES - 1, 1))
+        moved = jnp.where(
+            lane < LANES - LAGS, pltpu.roll(plane, LANES - LAGS, 1), pltpu.roll(plane, LANES - LAGS - 1, 1)
+        )
+        moved = jnp.where(lane == LANES - 1, 0.0, moved)
         ext_ref[:, total + b * LANES : total + (b + 1) * LANES] = moved.astype(BF16)
 
 
@@ -182,35 +201,46 @@
     window = BLOCK * STRIDE + 2 * HALO
     half = jax.ShapeDtypeStruct((CHIPS, 2 * LAGS, LANES), BF16)
     ids = row_channel.reshape(-1, LANES)
-    planes, keep, give = pl.pallas_call(
+    dec, keep, give = pl.pallas_call(
         decimate_kernel,
-        out_shape=(jax.ShapeDtypeStruct((total, LANES), BF16), half, half),
+        out_shape=(jax.ShapeDtypeStruct((rows_dev, total), BF16), half, half),
         in_specs=[HBM] * 4,
         out_specs=(VMEM, VMEM, VMEM),
         scratch_shapes=[
-            pltpu.VMEM((rows_dev, samples), BF16),
+            pltpu.VMEM((rows_dev, samples + 2 * HALO), BF16),
             pltpu.VMEM((1, TAPS), BF16),
             pltpu.VMEM(ids.shape, jnp.int32),
             pltpu.VMEM((1, NREF), jnp.int32),
             pltpu.VMEM((8, window), F32),
-            pltpu.VMEM((total, LANES), F32),
+            pltpu.VMEM((rows_dev, total), F32),
             pltpu.VMEM((2, CHIPS * 2 * LAGS, LANES), F32),
-            pltpu.SemaphoreType.DMA((samples // (BLOCK * STRIDE),)),
+            pltpu.SemaphoreType.DMA((4,)),
             pltpu.SemaphoreType.DMA((3,)),
         ],
-        compiler_params=params(60),
+        compiler_params=params(54),
         name="decimate",
     )(raw, taps.reshape(1, TAPS), ids, ref_channel.reshape(1, NREF))
     got = swap_cores(give)
+    packet_shape = jax.ShapeDtypeStruct((CHIPS, 6 * LAGS, LANES), BF16)
     packet = pl.pallas_call(
         route_kernel,
-        out_shape=jax.ShapeDtypeStruct((CHIPS, 6 * LAGS, LANES), BF16),
-        in_specs=[VMEM] * 4,
+        out_shape=packet_shape,
+        in_specs=[VMEM, VMEM],
         out_specs=VMEM,
         scratch_shapes=[pltpu.VMEM((CHIPS * 4 * LAGS, LANES), F32)],
         compiler_params=params(),
+        cost_estimate=pl.CostEstimate(flops=100_000_000, bytes_accessed=4_000_000, transcendentals=0),
         name="route",
-    )(planes, owner_of_row.reshape(1, rows_dev), keep, got)
+    )(dec, owner_of_row.reshape(1, rows_dev))
+    packet = pl.pallas_call(
+        add_refs_kernel,
+        out_shape=packet_shape,
+        in_specs=[VMEM] * 3,
+        out_specs=VMEM,
+        input_output_aliases={0: 0},
+        compiler_params=params(),
+        name="add_refs",
+    )(packet, keep, got)
     arrived = lax.all_to_all(packet, SAME, 0, 0, tiled=True)
     spread, rows_give = pl.pallas_call(
         spread_kernel,

time: 80.4 us -> 75.1 us (0.934)
  Pallas kernels: 21.1 us -> 18.8 us
  waiting for transfers between devices: 11.1 us -> 9.24 us
  local copies, waits for them, and re-layouts: 2.09 us -> 1.01 us
    pallas_call x2 -> x3, Pallas kernels: 11.3 us -> 8.69 us  [the longest x1 6.96 us: on_device(): pl.pallas_call(decimate_kernel, out_shape=(jax.ShapeDtypeStruct((rows_dev...]
    ppermute x3, waiting for transfers between devices: 2.02 us -> 0.01 us  [swap_cores(): return lax.ppermute(x, 'core', [(0, 1), (1, 0)])]
    unnamed x6, local copies, waits for them, and re-layouts: 2.09 us -> 1.01 us
  transfers between devices with their start and end apart: 4 -> 4, of which waited for: 3 -> 1; matrix products, arithmetic and copies ran while one was open for 0% -> 0% of each run, Pallas kernels for 2% -> 4%
where the time goes in v3:
time: 75.1 us; the launch traced here: 74.9 us
  blocking collectives  33.4 us (44%)
  Pallas kernels  18.8 us (25%)
  starting transfers between devices  12.3 us (16%)
  waiting for transfers between devices  9.24 us (12%)
  local copies, waits for them, and re-layouts  1.01 us (1%)
    all_to_all x1, blocking collectives, on_device(): arrived = lax.all_to_all(packet, SAME, 0, 0, tiled=True)  33.4 us
    all_to_all x1, waiting for transfers between devices, on_device(): refs_own = lax.all_to_all(spread, SAME, 0, 0, tiled=True)  9.23 us
    pallas_call x1, Pallas kernels, on_device(): pl.pallas_call(lambda *refs: correlate_kernel(per, *refs), grid=(LAGS //...  7.63 us
    pallas_call x1, Pallas kernels, on_device(): pl.pallas_call(decimate_kernel, out_shape=(jax.ShapeDtypeStruct((rows_dev...  6.96 us
    ppermute x3, starting transfers between devices, swap_cores(): return lax.ppermute(x, 'core', [(0, 1), (1, 0)])  6.33 us
    all_to_all x1, starting transfers between devices, on_device(): refs_own = lax.all_to_all(spread, SAME, 0, 0, tiled=True)  6.02 us
    pallas_call x1, Pallas kernels, on_device(): pl.pallas_call(route_kernel, out_shape=packet_shape, in_specs=[VMEM, VMEM...  1.6 us
    pallas_call x1, Pallas kernels, on_device(): pl.pallas_call(widen_kernel, out_shape=jax.ShapeDtypeStruct((4 * CHIPS, 2...  1.55 us
  transfers between devices with their start and end apart: 4, of which 1 were waited for; matrix products, arithmetic and copies ran while one was open for 0% of the time, Pallas kernels for 4%

profile of v3, /device:TPU:1, one launch (start us, length us, event | category | flops | bytes accessed | tf_op | source)
XLA Modules:
  0.0 74.9 jit_solution(8336187091818937632)
XLA Ops:
  0.0 0.0 copy-start.2
  0.0 7.0 %decimate.1 = (bf16[96,2048]{1,0:T(8,128)(2,1)}, bf16[64,32,128]{2,1,0:T(8,128)(2,1)}, bf16[64,32,128]{2,1,0:T(8,128)(2,1)}) custom-call(bf16[96,16384]{1,0:T(8,128)(2,1)} %raw_hbm.1, bf16[1,127]{1,0:T(2,128)(2,1)} %bitcast.7, s32[96,128]{1,0:T(8,128)} %bitcast.5, s32[1,256]{1,0:T(1,128)} %bitcast.6), custom_call_target="tpu_custom_call" | custom-call | tf_op jit(solution)/shard_map/decimate/pallas_call | solution.py:204
  7.0 0.0 copy-start
  7.0 1.5 %collective-permute-start = (bf16[64,32,128]{2,1,0:T(8,128)(2,1)}, bf16[64,32,128]{2,1,0:T(8,128)(2,1)S(1)}, u32[]{:S(2)}, u32[]{:S(2)}) collective-permute-start(bf16[64,32,128]{2,1,0:T(8,128)(2,1)} %get-tuple-element.12), channel_id=1, source_target_pairs={{0,4},{4,0},{1,5},{5,1},{2,6},{6,2},{3,7},{7,3},{8,12},{12,8},{9,1... | collective-permute-start | bytes 1572872 | tf_op jit(solution)/shard_map/ppermute | solution.py:195
  8.5 0.0 copy-done.2
  8.5 0.0 copy-start.1
  8.5 1.0 %copy-done.1 = bf16[96,2048]{1,0:T(8,128)(2,1)S(1)} copy-done((bf16[96,2048]{1,0:T(8,128)(2,1)S(1)}, bf16[96,2048]{1,0:T(8,128)(2,1)}, u32[]{:S(2)}) %copy-start.1) | copy-done | bytes 393240
  9.5 1.6 %route.1.packet_in = bf16[64,96,128]{2,1,0:T(8,128)(2,1)S(1)} custom-call(bf16[96,2048]{1,0:T(8,128)(2,1)S(1)} %copy-done.1, s32[1,96]{1,0:T(1,128)S(1)} %bitcast.4), custom_call_target="tpu_custom_call" | custom-call | flops 100000000 | bytes 4000000 | tf_op jit(solution)/shard_map/route/pallas_call | solution.py:225
  11.1 0.0 collective-permute-done.got_ref
  11.1 0.0 copy-done
  11.1 0.1 add_refs.1
  11.3 33.4 %all_to_all.10.arrived_ref = bf16[64,96,128]{2,1,0:T(8,128)(2,1)S(1)} all-to-all(bf16[64,96,128]{2,1,0:T(8,128)(2,1)S(1)} %add_refs.1), channel_id=1, replica_groups=mesh['x'=4,'z'=4,'core'=2,'chan'=4] {'x','z','chan'}, dimensions={0} | all-to-all | bytes 3145728 | tf_op jit(solution)/shard_map/all_to_all | solution.py:244
  44.7 0.9 %spread.1 = (bf16[64,32,128]{2,1,0:T(8,128)(2,1)}, bf16[64,32,128]{2,1,0:T(8,128)(2,1)S(1)}) custom-call(bf16[64,96,128]{2,1,0:T(8,128)(2,1)S(1)} %all_to_all.10.arrived_ref), custom_call_target="tpu_custom_call" | custom-call | tf_op jit(solution)/shard_map/spread/pallas_call | solution.py:245
  45.6 6.0 %all-to-all-start.1 = ((bf16[64,32,128]{2,1,0:T(8,128)(2,1)}), bf16[64,32,128]{2,1,0:T(8,128)(2,1)S(1)}, u32[]{:S(2)}, u32[]{:S(2)}) async-start(bf16[64,32,128]{2,1,0:T(8,128)(2,1)} %get-tuple-element.14), calls=%async_computation.1 | async-start | bytes 1048576 | tf_op jit(solution)/shard_map/all_to_all | solution.py:253
  51.6 1.7 %collective-permute-start.1 = (bf16[64,32,128]{2,1,0:T(8,128)(2,1)S(1)}, bf16[64,32,128]{2,1,0:T(8,128)(2,1)S(1)}, u32[]{:S(2)}, u32[]{:S(2)}) collective-permute-start(bf16[64,32,128]{2,1,0:T(8,128)(2,1)S(1)} %get-tuple-element.13), channel_id=1, source_target_pairs={{0,4},{4,0},{1,5},{5,1},{2,6},{6,2},{3,7},{7,3},{8,12},{12,8},{9,1... | collective-permute-start | bytes 1572872 | tf_op jit(solution)/shard_map/ppermute | solution.py:195
  53.3 9.2 %all-to-all-done.1.refs_1_ = bf16[64,32,128]{2,1,0:T(8,128)(2,1)S(1)} async-done(((bf16[64,32,128]{2,1,0:T(8,128)(2,1)}), bf16[64,32,128]{2,1,0:T(8,128)(2,1)S(1)}, u32[]{:S(2)}, u32[]{:S(2)}) %all-to-all-start.1) | async-done | bytes 524320 | tf_op jit(solution)/shard_map/all_to_all | solution.py:253
  62.5 3.1 %collective-permute-start.2 = (bf16[64,32,128]{2,1,0:T(8,128)(2,1)S(1)}, bf16[64,32,128]{2,1,0:T(8,128)(2,1)S(1)}, u32[]{:S(2)}, u32[]{:S(2)}) collective-permute-start(bf16[64,32,128]{2,1,0:T(8,128)(2,1)S(1)} %all-to-all-done.1.refs_1_), channel_id=1, source_target_pairs={{0,4},{4,0},{1,5},{5,1},{2,6},{6,2},{3,7},{7,3},{8,12},{12,8},{9,1... | collective-permute-start | bytes 1572872 | tf_op jit(solution)/shard_map/ppermute | solution.py:195
  65.7 0.0 collective-permute-done.1.got_ref
  65.7 1.5 %widen.1.refs_0_ = bf16[256,4096]{1,0:T(8,128)(2,1)S(1)} custom-call(bf16[64,96,128]{2,1,0:T(8,128)(2,1)S(1)} %all_to_all.10.arrived_ref, bf16[64,32,128]{2,1,0:T(8,128)(2,1)S(1)} %collective-permute-done.1.got_ref), custom_call_target="tpu_custom_call" | custom-call | tf_op jit(solution)/shard_map/widen/pallas_call | solution.py:255
  67.2 0.0 collective-permute-done.2.refs_2_
  67.2 7.6 %correlate.1 = f32[1,256,4096]{2,1,0:T(8,128)} custom-call(bf16[256,4096]{1,0:T(8,128)(2,1)S(1)} %widen.1.refs_0_, bf16[64,32,128]{2,1,0:T(8,128)(2,1)S(1)} %all-to-all-done.1.refs_1_, bf16[64,32,128]{2,1,0:T(8,128)(2,1)S(1)} %collective-permute-done.2.refs_2_), custom_call_target="tpu_custom_call" | custom-call | tf_op jit(solution)/shard_map/correlate/pallas_call | solution.py:266
Async XLA Ops:
  0.0 8.5 %copy-start.2 = (s32[96,1]{0,1:T(1,128)S(1)}, s32[96,1]{0,1:T(1,128)}, u32[]{:S(2)}) copy-start(s32[96,1]{0,1:T(1,128)} %param.9) | copy-start | bytes 1156
  7.0 4.1 %copy-start = (bf16[64,32,128]{2,1,0:T(8,128)(2,1)S(1)}, bf16[64,32,128]{2,1,0:T(8,128)(2,1)}, u32[]{:S(2)}) copy-start(bf16[64,32,128]{2,1,0:T(8,128)(2,1)} %get-tuple-element.11.keep_ref) | copy-start | bytes 1572868
  7.0 4.1 %collective-permute-start = (bf16[64,32,128]{2,1,0:T(8,128)(2,1)}, bf16[64,32,128]{2,1,0:T(8,128)(2,1)S(1)}, u32[]{:S(2)}, u32[]{:S(2)}) collective-permute-start(bf16[64,32,128]{2,1,0:T(8,128)(2,1)} %get-tuple-element.12), channel_id=1, source_target_pairs={{0,4},{4,0},{1,5},{5,1},{2,6},{6,2},{3,7},{7,3},{8,12},{12,8},{9,1... | collective-permute-start | bytes 1572872 | tf_op jit(solution)/shard_map/ppermute | solution.py:195
  8.5 1.0 %copy-start.1 = (bf16[96,2048]{1,0:T(8,128)(2,1)S(1)}, bf16[96,2048]{1,0:T(8,128)(2,1)}, u32[]{:S(2)}) copy-start(bf16[96,2048]{1,0:T(8,128)(2,1)} %get-tuple-element.10.dec_ref) | copy-start | bytes 1179652
  45.6 17.0 %all-to-all-start.1 = ((bf16[64,32,128]{2,1,0:T(8,128)(2,1)}), bf16[64,32,128]{2,1,0:T(8,128)(2,1)S(1)}, u32[]{:S(2)}, u32[]{:S(2)}) async-start(bf16[64,32,128]{2,1,0:T(8,128)(2,1)} %get-tuple-element.14), calls=%async_computation.1 | async-start | bytes 1048576 | tf_op jit(solution)/shard_map/all_to_all | solution.py:253
  51.6 14.1 %collective-permute-start.1 = (bf16[64,32,128]{2,1,0:T(8,128)(2,1)S(1)}, bf16[64,32,128]{2,1,0:T(8,128)(2,1)S(1)}, u32[]{:S(2)}, u32[]{:S(2)}) collective-permute-start(bf16[64,32,128]{2,1,0:T(8,128)(2,1)S(1)} %get-tuple-element.13), channel_id=1, source_target_pairs={{0,4},{4,0},{1,5},{5,1},{2,6},{6,2},{3,7},{7,3},{8,12},{12,8},{9,1... | collective-permute-start | bytes 1572872 | tf_op jit(solution)/shard_map/ppermute | solution.py:195
  62.5 4.7 %collective-permute-start.2 = (bf16[64,32,128]{2,1,0:T(8,128)(2,1)S(1)}, bf16[64,32,128]{2,1,0:T(8,128)(2,1)S(1)}, u32[]{:S(2)}, u32[]{:S(2)}) collective-permute-start(bf16[64,32,128]{2,1,0:T(8,128)(2,1)S(1)} %all-to-all-done.1.refs_1_), channel_id=1, source_target_pairs={{0,4},{4,0},{1,5},{5,1},{2,6},{6,2},{3,7},{7,3},{8,12},{12,8},{9,1... | collective-permute-start | bytes 1572872 | tf_op jit(solution)/shard_map/ppermute | solution.py:195

commit v4 on v3

--- a/solution.py
+++ b/solution.py
@@ -36,9 +36,9 @@
     return lax.broadcasted_iota(jnp.int32, shape, dim)
 
 
-def decimate_kernel(raw_hbm, taps_hbm, ids_hbm, refch_hbm, dec_ref, keep_ref, give_ref,
-                    raw, taps, ids, refch, line, dec, stage, raw_sem, small_sem):
-    rows = dec_ref.shape[0]
+def decimate_kernel(raw_hbm, taps_hbm, ids_hbm, refch_hbm, dec_hbm, keep_hbm, give_hbm,
+                    raw, taps, ids, refch, line, dec, planes, stage, keep, give, raw_sem, small_sem, out_sem):
+    rows = planes.shape[0]
     groups = raw_sem.shape[0]
     chunk = BLOCK * STRIDE
     window = chunk + 2 * HALO
@@ -100,20 +100,32 @@
                     pieces[t] = jnp.where(low, x, pltpu.roll(y, k, 1))
                     pieces[t | k] = jnp.where(low, pltpu.roll(x, LANES - k, 1), y)
         for b in range(LAGS):
-            dec_ref[r : r + 16, b * LANES : (b + 1) * LANES] = pieces[b].astype(BF16)
+            planes[r : r + 16, b * LANES : (b + 1) * LANES] = pieces[b].astype(BF16)
+    stores = [
+        pltpu.make_async_copy(planes, dec_hbm, out_sem.at[0]),
+        pltpu.make_async_copy(give, give_hbm, out_sem.at[1]),
+        pltpu.make_async_copy(keep, keep_hbm, out_sem.at[2]),
+    ]
+    stores[0].start()
     for b in range(0, LAGS, 2):
-        picked = jnp.dot(select, dec_ref[:, b * LANES : (b + 2) * LANES], preferred_element_type=F32)
+        picked = jnp.dot(select, planes[:, b * LANES : (b + 2) * LANES], preferred_element_type=F32)
         for g in range(4):
             for h in range(2):
                 stage[g // 2, pl.ds((g % 2) * LAGS + b + h, CHIPS, stride=2 * LAGS), :] = picked[
                     g * CHIPS : (g + 1) * CHIPS, h * LANES : (h + 1) * LANES
                 ]
     shape = (CHIPS, 2 * LAGS, LANES)
-    keep_ref[...] = stage[core].astype(BF16).reshape(shape)
-    give_ref[...] = stage[1 - core].astype(BF16).reshape(shape)
-
-
-def route_kernel(dec_ref, owner_ref, packet_ref, stage):
+    give[...] = stage[1 - core].astype(BF16).reshape(shape)
+    stores[1].start()
+    keep[...] = stage[core].astype(BF16).reshape(shape)
+    stores[2].start()
+    for store in stores:
+        store.wait()
+
+
+def route_kernel(dec_hbm, owner_ref, packet_ref, planes, stage, sem):
+    load = pltpu.make_async_copy(dec_hbm, planes, sem)
+    load.start()
     rows = owner_ref.shape[1]
     owner = owner_ref[...]
     chip = iota((CHIPS, rows), 0)
@@ -126,8 +138,9 @@
         first = jnp.where(rank < 0.5, one, 0.0)
         parts += [first, one - first]
     select = jnp.concatenate(parts, axis=0).astype(BF16)
+    load.wait()
     for b in range(0, LAGS, 2):
-        picked = jnp.dot(select, dec_ref[:, b * LANES : (b + 2) * LANES], preferred_element_type=F32)
+        picked = jnp.dot(select, planes[:, b * LANES : (b + 2) * LANES], preferred_element_type=F32)
         for g in range(4):
             for h in range(2):
                 stage[pl.ds(g * LAGS + b + h, CHIPS, stride=4 * LAGS), :] = picked[
@@ -141,11 +154,13 @@
     packet_ref[:, 4 * LAGS :, :] = (keep_ref[...].astype(F32) + got_ref[...].astype(F32)).astype(BF16)
 
 
-def spread_kernel(arrived_ref, spread_ref, give_ref):
-    core = lax.axis_index("core")
+def spread_kernel(arrived_ref, spread_ref):
     total = jnp.sum(arrived_ref[:, 4 * LAGS :, :].astype(F32), axis=0, keepdims=True)
     spread_ref[...] = jnp.broadcast_to(total, spread_ref.shape).astype(BF16)
-    other = pl.multiple_of((1 - core) * 2 * LAGS, 2 * LAGS)
+
+
+def give_kernel(arrived_ref, give_ref):
+    other = pl.multiple_of((1 - lax.axis_index("core")) * 2 * LAGS, 2 * LAGS)
     give_ref[...] = arrived_ref[:, pl.ds(other, 2 * LAGS), :]
 
 
@@ -168,27 +183,60 @@
         ext_ref[:, total + b * LANES : total + (b + 1) * LANES] = moved.astype(BF16)
 
 
-def correlate_kernel(per, ext_ref, own_ref, other_ref, out_ref, wide, ref_planes):
-    step = pl.program_id(0)
+def correlate_kernel(own, ext_ref, ref_ref, *rest):
+    out_hbm, wide, refs, sums, sem = rest[-5:]
+    core = lax.axis_index("core")
+    side = core if own else 1 - core
     total = LAGS * LANES
-    size = CHIPS * 2 * LAGS
-
-    @pl.when(step == 0)
-    def _():
-        core = lax.axis_index("core")
-        wide[core] = own_ref[...].astype(F32).reshape(size, LANES)
-        wide[1 - core] = other_ref[...].astype(F32).reshape(size, LANES)
-        for g in range(4):
-            for b in range(LAGS):
-                ref_planes[g * CHIPS : (g + 1) * CHIPS, b * LANES : (b + 1) * LANES] = wide[
-                    g // 2, pl.ds((g % 2) * LAGS + b, CHIPS, stride=2 * LAGS), :
-                ].astype(BF16)
-
-    start = pl.multiple_of((step * per + 1) * LANES, LANES)
-    lagged = jnp.concatenate([ext_ref[:, pl.ds(start + i * LANES, total)] for i in range(per)], axis=0)
-    sums = dot_nt(lagged, ref_planes[...]) * (1.0 / math.sqrt(total))
-    for i in range(per):
-        out_ref[0, :, i * NREF : (i + 1) * NREF] = sums[i * 4 * CHIPS : (i + 1) * 4 * CHIPS]
+    count = 2 * CHIPS
+    wide[...] = ref_ref[...].astype(F32).reshape(wide.shape)
+    refs[:count, total:] = jnp.zeros((count, LANES), BF16)
+    refs[count:, :LANES] = jnp.zeros((count, LANES), BF16)
+    for s in range(2):
+        for b in range(LAGS):
+            plane = wide[pl.ds(s * LAGS + b, CHIPS, stride=2 * LAGS), :].astype(BF16)
+            for h in range(2):
+                at = h * count + s * CHIPS
+                refs[at : at + CHIPS, (b + h) * LANES : (b + h + 1) * LANES] = plane
+    rows = ext_ref.shape[0]
+    copies = []
+    lag = 1
+    for pairs in (4, 2, 1, 1):
+        windows = [ext_ref[:, pl.ds((lag + 2 * i) * LANES, total + LANES)] for i in range(pairs)]
+        part = dot_nt(jnp.concatenate(windows, axis=0), refs[...]) * (1.0 / math.sqrt(total))
+        for i in range(pairs):
+            for h in range(2):
+                at = lag - 1 + 2 * i + h
+                sums[:, at * count : (at + 1) * count] = part[i * rows : (i + 1) * rows, h * count : (h + 1) * count]
+                column = pl.multiple_of(at * 2 * count + side * count, count)
+                copy = pltpu.make_async_copy(
+                    sums.at[:, pl.ds(at * count, count)], out_hbm.at[0, :, pl.ds(column, count)], sem.at[at]
+                )
+                copy.start()
+                copies.append(copy)
+        lag += 2 * pairs
+    for copy in copies:
+        copy.wait()
+
+
+def correlate(own, ext, refs, *out):
+    total = LAGS * LANES
+    return pl.pallas_call(
+        lambda *args: correlate_kernel(own, *args),
+        out_shape=jax.ShapeDtypeStruct((1, 4 * CHIPS, LAGS * NREF), F32),
+        in_specs=[VMEM, VMEM] + [HBM] * len(out),
+        out_specs=HBM,
+        scratch_shapes=[
+            pltpu.VMEM((CHIPS * 2 * LAGS, LANES), F32),
+            pltpu.VMEM((NREF, total + LANES), BF16),
+            pltpu.VMEM((4 * CHIPS, total), F32),
+            pltpu.SemaphoreType.DMA((LAGS,)),
+        ],
+        input_output_aliases={2: 0} if out else {},
+        compiler_params=params(24),
+        cost_estimate=pl.CostEstimate(flops=2_400_000_000, bytes_accessed=4_000_000, transcendentals=0),
+        name="correlate_own" if own else "correlate_other",
+    )(ext, refs, *out)
 
 
 def swap_cores(x):
@@ -205,7 +253,7 @@
         decimate_kernel,
         out_shape=(jax.ShapeDtypeStruct((rows_dev, total), BF16), half, half),
         in_specs=[HBM] * 4,
-        out_specs=(VMEM, VMEM, VMEM),
+        out_specs=(HBM, HBM, HBM),
         scratch_shapes=[
             pltpu.VMEM((rows_dev, samples + 2 * HALO), BF16),
             pltpu.VMEM((1, TAPS), BF16),
@@ -213,8 +261,12 @@
             pltpu.VMEM((1, NREF), jnp.int32),
             pltpu.VMEM((8, window), F32),
             pltpu.VMEM((rows_dev, total), F32),
+            pltpu.VMEM((rows_dev, total), BF16),
             pltpu.VMEM((2, CHIPS * 2 * LAGS, LANES), F32),
+            pltpu.VMEM(half.shape, BF16),
+            pltpu.VMEM(half.shape, BF16),
             pltpu.SemaphoreType.DMA((4,)),
+            pltpu.SemaphoreType.DMA((3,)),
             pltpu.SemaphoreType.DMA((3,)),
         ],
         compiler_params=params(54),
@@ -225,9 +277,13 @@
     packet = pl.pallas_call(
         route_kernel,
         out_shape=packet_shape,
-        in_specs=[VMEM, VMEM],
-        out_specs=VMEM,
-        scratch_shapes=[pltpu.VMEM((CHIPS * 4 * LAGS, LANES), F32)],
+        in_specs=[HBM, VMEM],
+        out_specs=VMEM,
+        scratch_shapes=[
+            pltpu.VMEM((rows_dev, total), BF16),
+            pltpu.VMEM((CHIPS * 4 * LAGS, LANES), F32),
+            pltpu.SemaphoreType.DMA,
+        ],
         compiler_params=params(),
         cost_estimate=pl.CostEstimate(flops=100_000_000, bytes_accessed=4_000_000, transcendentals=0),
         name="route",
@@ -242,13 +298,21 @@
         name="add_refs",
     )(packet, keep, got)
     arrived = lax.all_to_all(packet, SAME, 0, 0, tiled=True)
-    spread, rows_give = pl.pallas_call(
+    spread = pl.pallas_call(
         spread_kernel,
-        out_shape=(half, half),
+        out_shape=half,
         in_specs=[VMEM],
-        out_specs=(VMEM, VMEM),
+        out_specs=VMEM,
         compiler_params=params(),
         name="spread",
+    )(arrived)
+    rows_give = pl.pallas_call(
+        give_kernel,
+        out_shape=half,
+        in_specs=[VMEM],
+        out_specs=VMEM,
+        compiler_params=params(),
+        name="give",
     )(arrived)
     refs_own = lax.all_to_all(spread, SAME, 0, 0, tiled=True)
     rows_got = swap_cores(rows_give)
@@ -262,20 +326,8 @@
         name="widen",
     )(arrived, rows_got)
     refs_other = swap_cores(refs_own)
-    per = 4
-    return pl.pallas_call(
-        lambda *refs: correlate_kernel(per, *refs),
-        grid=(LAGS // per,),
-        out_shape=jax.ShapeDtypeStruct((1, 4 * CHIPS, LAGS * NREF), F32),
-        in_specs=[VMEM, VMEM, VMEM],
-        out_specs=pl.BlockSpec((1, 4 * CHIPS, per * NREF), lambda i: (0, 0, i)),
-        scratch_shapes=[
-            pltpu.VMEM((2, CHIPS * 2 * LAGS, LANES), F32),
-            pltpu.VMEM((NREF, total), BF16),
-        ],
-        compiler_params=params(),
-        name="correlate",
-    )(ext, refs_own, refs_other)
+    out = correlate(True, ext, refs_own)
+    return correlate(False, ext, refs_other, out)
 
 
 def solution(mesh):

time: 75.1 us -> 76.2 us (1.015)
  Pallas kernels: 18.8 us -> 19.8 us
    pallas_call x3 -> x5, Pallas kernels: 10.1 us -> 11.1 us  [the longest x2 8.28 us: correlate(): pl.pallas_call(lambda *args: correlate_kernel(own, *args), out_shape=jax....]
  transfers between devices with their start and end apart: 4 -> 4, of which waited for: 1 -> 1; matrix products, arithmetic and copies ran while one was open for 0% -> 0% of each run, Pallas kernels for 4% -> 10%
where the time goes in v4:
time: 76.2 us; the launch traced here: 76 us
  blocking collectives  33.4 us (44%)
  Pallas kernels  19.8 us (26%)
  starting transfers between devices  12.3 us (16%)
  waiting for transfers between devices  9.22 us (12%)
  local copies, waits for them, and re-layouts  1.01 us (1%)
    all_to_all x1, blocking collectives, on_device(): arrived = lax.all_to_all(packet, SAME, 0, 0, tiled=True)  33.4 us
    all_to_all x1, waiting for transfers between devices, on_device(): refs_own = lax.all_to_all(spread, SAME, 0, 0, tiled=True)  9.21 us
    pallas_call x2, Pallas kernels, correlate(): pl.pallas_call(lambda *args: correlate_kernel(own, *args), out_shape=jax....  8.28 us
    pallas_call x1, Pallas kernels, on_device(): pl.pallas_call(decimate_kernel, out_shape=(jax.ShapeDtypeStruct((rows_dev...  6.98 us
    ppermute x3, starting transfers between devices, swap_cores(): return lax.ppermute(x, 'core', [(0, 1), (1, 0)])  6.29 us
    all_to_all x1, starting transfers between devices, on_device(): refs_own = lax.all_to_all(spread, SAME, 0, 0, tiled=True)  6.02 us
    pallas_call x1, Pallas kernels, on_device(): pl.pallas_call(route_kernel, out_shape=packet_shape, in_specs=[HBM, VMEM]...  1.89 us
    pallas_call x1, Pallas kernels, on_device(): pl.pallas_call(widen_kernel, out_shape=jax.ShapeDtypeStruct((4 * CHIPS, 2...  1.55 us
  transfers between devices with their start and end apart: 4, of which 1 were waited for; matrix products, arithmetic and copies ran while one was open for 0% of the time, Pallas kernels for 10%

profile of v4, /device:TPU:1, one launch (start us, length us, event | category | flops | bytes accessed | tf_op | source)
XLA Modules:
  0.0 76.0 jit_solution(12910196443813068686)
XLA Ops:
  0.0 0.0 copy-start.2
  0.0 7.0 %decimate.1 = (bf16[96,2048]{1,0:T(8,128)(2,1)}, bf16[64,32,128]{2,1,0:T(8,128)(2,1)}, bf16[64,32,128]{2,1,0:T(8,128)(2,1)}) custom-call(bf16[96,16384]{1,0:T(8,128)(2,1)} %raw_hbm.1, bf16[1,127]{1,0:T(2,128)(2,1)} %bitcast.7, s32[96,128]{1,0:T(8,128)} %bitcast.5, s32[1,256]{1,0:T(1,128)} %bitcast.6), custom_call_target="tpu_custom_call" | custom-call | tf_op jit(solution)/shard_map/decimate/pallas_call | solution.py:252
  7.0 0.0 copy-start
  7.0 1.5 %collective-permute-start = (bf16[64,32,128]{2,1,0:T(8,128)(2,1)}, bf16[64,32,128]{2,1,0:T(8,128)(2,1)S(1)}, u32[]{:S(2)}, u32[]{:S(2)}) collective-permute-start(bf16[64,32,128]{2,1,0:T(8,128)(2,1)} %get-tuple-element.10), channel_id=1, source_target_pairs={{0,4},{4,0},{1,5},{5,1},{2,6},{6,2},{3,7},{7,3},{8,12},{12,8},{9,1... | collective-permute-start | bytes 1572872 | tf_op jit(solution)/shard_map/ppermute | solution.py:243
  8.5 0.0 copy-done.2
  8.5 0.0 copy-start.1
  8.5 1.0 %copy-done.1 = bf16[96,2048]{1,0:T(8,128)(2,1)S(1)} copy-done((bf16[96,2048]{1,0:T(8,128)(2,1)S(1)}, bf16[96,2048]{1,0:T(8,128)(2,1)}, u32[]{:S(2)}) %copy-start.1) | copy-done | bytes 393240
  9.5 1.9 %route.1.packet_in = bf16[64,96,128]{2,1,0:T(8,128)(2,1)S(1)} custom-call(bf16[96,2048]{1,0:T(8,128)(2,1)S(1)} %copy-done.1, s32[1,96]{1,0:T(1,128)S(1)} %bitcast.4), custom_call_target="tpu_custom_call" | custom-call | flops 100000000 | bytes 4000000 | tf_op jit(solution)/shard_map/route/pallas_call | solution.py:277
  11.4 0.0 collective-permute-done.got_ref
  11.4 0.0 copy-done
  11.4 0.1 add_refs.1
  11.5 33.4 %all_to_all.10.arrived_ref = bf16[64,96,128]{2,1,0:T(8,128)(2,1)S(1)} all-to-all(bf16[64,96,128]{2,1,0:T(8,128)(2,1)S(1)} %add_refs.1), channel_id=1, replica_groups=mesh['x'=4,'z'=4,'core'=2,'chan'=4] {'x','z','chan'}, dimensions={0} | all-to-all | bytes 3145728 | tf_op jit(solution)/shard_map/all_to_all | solution.py:300
  45.0 0.9 %spread.1 = bf16[64,32,128]{2,1,0:T(8,128)(2,1)} custom-call(bf16[64,96,128]{2,1,0:T(8,128)(2,1)S(1)} %all_to_all.10.arrived_ref), custom_call_target="tpu_custom_call" | custom-call | tf_op jit(solution)/shard_map/spread/pallas_call | solution.py:301
  45.9 6.0 %all-to-all-start.1 = ((bf16[64,32,128]{2,1,0:T(8,128)(2,1)}), bf16[64,32,128]{2,1,0:T(8,128)(2,1)S(1)}, u32[]{:S(2)}, u32[]{:S(2)}) async-start(bf16[64,32,128]{2,1,0:T(8,128)(2,1)} %spread.1), calls=%async_computation.1 | async-start | bytes 1048576 | tf_op jit(solution)/shard_map/all_to_all | solution.py:317
  52.0 1.7 %collective-permute-start.1 = (bf16[64,32,128]{2,1,0:T(8,128)(2,1)S(1)}, bf16[64,32,128]{2,1,0:T(8,128)(2,1)S(1)}, u32[]{:S(2)}, u32[]{:S(2)}) collective-permute-start(bf16[64,32,128]{2,1,0:T(8,128)(2,1)S(1)} %give.1), channel_id=1, source_target_pairs={{0,4},{4,0},{1,5},{5,1},{2,6},{6,2},{3,7},{7,3},{8,12},{12,8},{9,1... | collective-permute-start | bytes 1572872 | tf_op jit(solution)/shard_map/ppermute | solution.py:243
  53.7 9.2 %all-to-all-done.1.args_1_ = bf16[64,32,128]{2,1,0:T(8,128)(2,1)S(1)} async-done(((bf16[64,32,128]{2,1,0:T(8,128)(2,1)}), bf16[64,32,128]{2,1,0:T(8,128)(2,1)S(1)}, u32[]{:S(2)}, u32[]{:S(2)}) %all-to-all-start.1) | async-done | bytes 524320 | tf_op jit(solution)/shard_map/all_to_all | solution.py:317
  62.9 3.1 %collective-permute-start.2 = (bf16[64,32,128]{2,1,0:T(8,128)(2,1)S(1)}, bf16[64,32,128]{2,1,0:T(8,128)(2,1)S(1)}, u32[]{:S(2)}, u32[]{:S(2)}) collective-permute-start(bf16[64,32,128]{2,1,0:T(8,128)(2,1)S(1)} %all-to-all-done.1.args_1_), channel_id=1, source_target_pairs={{0,4},{4,0},{1,5},{5,1},{2,6},{6,2},{3,7},{7,3},{8,12},{12,8},{9,1... | collective-permute-start | bytes 1572872 | tf_op jit(solution)/shard_map/ppermute | solution.py:243
  66.0 0.0 collective-permute-done.1.got_ref
  66.0 1.5 %widen.1.args_0_ = bf16[256,4096]{1,0:T(8,128)(2,1)S(1)} custom-call(bf16[64,96,128]{2,1,0:T(8,128)(2,1)S(1)} %all_to_all.10.arrived_ref, bf16[64,32,128]{2,1,0:T(8,128)(2,1)S(1)} %collective-permute-done.1.got_ref), custom_call_target="tpu_custom_call" | custom-call | tf_op jit(solution)/shard_map/widen/pallas_call | solution.py:319
  67.5 4.1 %correlate_own.1.args_2_ = f32[1,256,4096]{2,1,0:T(8,128)} custom-call(bf16[256,4096]{1,0:T(8,128)(2,1)S(1)} %widen.1.args_0_, bf16[64,32,128]{2,1,0:T(8,128)(2,1)S(1)} %all-to-all-done.1.args_1_), custom_call_target="tpu_custom_call" | custom-call | flops 2400000000 | bytes 4000000 | tf_op jit(solution)/shard_map/correlate_own/pallas_call | solution.py:224
  71.7 0.0 collective-permute-done.2.args_1_
  71.7 4.1 %correlate_other.1 = f32[1,256,4096]{2,1,0:T(8,128)} custom-call(bf16[256,4096]{1,0:T(8,128)(2,1)S(1)} %widen.1.args_0_, bf16[64,32,128]{2,1,0:T(8,128)(2,1)S(1)} %collective-permute-done.2.args_1_, f32[1,256,4096]{2,1,0:T(8,128)} %correlate_own.1.args_2_), custom_call_target="tpu_custom_call", output_to_operand_aliasing={{}: (2, {})} | custom-call | flops 2400000000 | bytes 4000000 | tf_op jit(solution)/shard_map/correlate_other/pallas_call | solution.py:224
  (1 shorter events, 0.0 us)
Async XLA Ops:
  0.0 8.5 %copy-start.2 = (s32[96,1]{0,1:T(1,128)S(1)}, s32[96,1]{0,1:T(1,128)}, u32[]{:S(2)}) copy-start(s32[96,1]{0,1:T(1,128)} %param.9) | copy-start | bytes 1156
  7.0 4.4 %copy-start = (bf16[64,32,128]{2,1,0:T(8,128)(2,1)S(1)}, bf16[64,32,128]{2,1,0:T(8,128)(2,1)}, u32[]{:S(2)}) copy-start(bf16[64,32,128]{2,1,0:T(8,128)(2,1)} %get-tuple-element.9.keep_ref) | copy-start | bytes 1572868
  7.0 4.4 %collective-permute-start = (bf16[64,32,128]{2,1,0:T(8,128)(2,1)}, bf16[64,32,128]{2,1,0:T(8,128)(2,1)S(1)}, u32[]{:S(2)}, u32[]{:S(2)}) collective-permute-start(bf16[64,32,128]{2,1,0:T(8,128)(2,1)} %get-tuple-element.10), channel_id=1, source_target_pairs={{0,4},{4,0},{1,5},{5,1},{2,6},{6,2},{3,7},{7,3},{8,12},{12,8},{9,1... | collective-permute-start | bytes 1572872 | tf_op jit(solution)/shard_map/ppermute | solution.py:243
  8.5 1.0 %copy-start.1 = (bf16[96,2048]{1,0:T(8,128)(2,1)S(1)}, bf16[96,2048]{1,0:T(8,128)(2,1)}, u32[]{:S(2)}) copy-start(bf16[96,2048]{1,0:T(8,128)(2,1)} %get-tuple-element.8.dec_hbm) | copy-start | bytes 1179652
  45.9 17.0 %all-to-all-start.1 = ((bf16[64,32,128]{2,1,0:T(8,128)(2,1)}), bf16[64,32,128]{2,1,0:T(8,128)(2,1)S(1)}, u32[]{:S(2)}, u32[]{:S(2)}) async-start(bf16[64,32,128]{2,1,0:T(8,128)(2,1)} %spread.1), calls=%async_computation.1 | async-start | bytes 1048576 | tf_op jit(solution)/shard_map/all_to_all | solution.py:317
  52.0 14.0 %collective-permute-start.1 = (bf16[64,32,128]{2,1,0:T(8,128)(2,1)S(1)}, bf16[64,32,128]{2,1,0:T(8,128)(2,1)S(1)}, u32[]{:S(2)}, u32[]{:S(2)}) collective-permute-start(bf16[64,32,128]{2,1,0:T(8,128)(2,1)S(1)} %give.1), channel_id=1, source_target_pairs={{0,4},{4,0},{1,5},{5,1},{2,6},{6,2},{3,7},{7,3},{8,12},{12,8},{9,1... | collective-permute-start | bytes 1572872 | tf_op jit(solution)/shard_map/ppermute | solution.py:243
  62.9 8.8 %collective-permute-start.2 = (bf16[64,32,128]{2,1,0:T(8,128)(2,1)S(1)}, bf16[64,32,128]{2,1,0:T(8,128)(2,1)S(1)}, u32[]{:S(2)}, u32[]{:S(2)}) collective-permute-start(bf16[64,32,128]{2,1,0:T(8,128)(2,1)S(1)} %all-to-all-done.1.args_1_), channel_id=1, source_target_pairs={{0,4},{4,0},{1,5},{5,1},{2,6},{6,2},{3,7},{7,3},{8,12},{12,8},{9,1... | collective-permute-start | bytes 1572872 | tf_op jit(solution)/shard_map/ppermute | solution.py:243

commit v5 on v3

--- a/solution.py
+++ b/solution.py
@@ -16,6 +16,7 @@
 BLOCK = 128
 HALO = 128
 CHIPS = 64
+LAG_STEPS = (3, 5, 4, 2, 2)
 AXES = ("x", "z", "core", "chan")
 SAME = ("x", "z", "chan")
 NT = (((1,), (1,)), ((), ()))
@@ -168,27 +169,31 @@
         ext_ref[:, total + b * LANES : total + (b + 1) * LANES] = moved.astype(BF16)
 
 
-def correlate_kernel(per, ext_ref, own_ref, other_ref, out_ref, wide, ref_planes):
-    step = pl.program_id(0)
+def correlate_kernel(ext_ref, own_ref, other_ref, out_hbm, wide, refs, sums, sem):
     total = LAGS * LANES
     size = CHIPS * 2 * LAGS
-
-    @pl.when(step == 0)
-    def _():
-        core = lax.axis_index("core")
-        wide[core] = own_ref[...].astype(F32).reshape(size, LANES)
-        wide[1 - core] = other_ref[...].astype(F32).reshape(size, LANES)
-        for g in range(4):
-            for b in range(LAGS):
-                ref_planes[g * CHIPS : (g + 1) * CHIPS, b * LANES : (b + 1) * LANES] = wide[
-                    g // 2, pl.ds((g % 2) * LAGS + b, CHIPS, stride=2 * LAGS), :
-                ].astype(BF16)
-
-    start = pl.multiple_of((step * per + 1) * LANES, LANES)
-    lagged = jnp.concatenate([ext_ref[:, pl.ds(start + i * LANES, total)] for i in range(per)], axis=0)
-    sums = dot_nt(lagged, ref_planes[...]) * (1.0 / math.sqrt(total))
-    for i in range(per):
-        out_ref[0, :, i * NREF : (i + 1) * NREF] = sums[i * 4 * CHIPS : (i + 1) * 4 * CHIPS]
+    core = lax.axis_index("core")
+    wide[core] = own_ref[...].astype(F32).reshape(size, LANES)
+    wide[1 - core] = other_ref[...].astype(F32).reshape(size, LANES)
+    for g in range(4):
+        for b in range(LAGS):
+            refs[g * CHIPS : (g + 1) * CHIPS, b * LANES : (b + 1) * LANES] = wide[
+                g // 2, pl.ds((g % 2) * LAGS + b, CHIPS, stride=2 * LAGS), :
+            ].astype(BF16)
+    rows = ext_ref.shape[0]
+    copies = []
+    lag = 1
+    for step, per in enumerate(LAG_STEPS):
+        windows = [ext_ref[:, pl.ds((lag + i) * LANES, total)] for i in range(per)]
+        part = dot_nt(jnp.concatenate(windows, axis=0), refs[...]) * (1.0 / math.sqrt(total))
+        for i in range(per):
+            sums[:, (lag - 1 + i) * NREF : (lag + i) * NREF] = part[i * rows : (i + 1) * rows]
+        span = pl.ds((lag - 1) * NREF, per * NREF)
+        copies.append(pltpu.make_async_copy(sums.at[:, span], out_hbm.at[0, :, span], sem.at[step]))
+        copies[-1].start()
+        lag += per
+    for copy in copies:
+        copy.wait()
 
 
 def swap_cores(x):
@@ -262,18 +267,18 @@
         name="widen",
     )(arrived, rows_got)
     refs_other = swap_cores(refs_own)
-    per = 4
     return pl.pallas_call(
-        lambda *refs: correlate_kernel(per, *refs),
-        grid=(LAGS // per,),
+        correlate_kernel,
         out_shape=jax.ShapeDtypeStruct((1, 4 * CHIPS, LAGS * NREF), F32),
         in_specs=[VMEM, VMEM, VMEM],
-        out_specs=pl.BlockSpec((1, 4 * CHIPS, per * NREF), lambda i: (0, 0, i)),
+        out_specs=HBM,
         scratch_shapes=[
             pltpu.VMEM((2, CHIPS * 2 * LAGS, LANES), F32),
             pltpu.VMEM((NREF, total), BF16),
+            pltpu.VMEM((4 * CHIPS, LAGS * NREF), F32),
+            pltpu.SemaphoreType.DMA((len(LAG_STEPS),)),
         ],
-        compiler_params=params(),
+        compiler_params=params(24),
         name="correlate",
     )(ext, refs_own, refs_other)
 

time: 75.1 us -> 74 us (0.985)
  Pallas kernels: 18.8 us -> 17.4 us
    pallas_call x1, Pallas kernels: 7.63 us -> 6.31 us  [on_device(): pl.pallas_call(correlate_kernel, out_shape=jax.ShapeDtypeStruct((1, 4 * C...]
where the time goes in v5:
time: 74 us; the launch traced here: 73.7 us
  blocking collectives  33.4 us (45%)
  Pallas kernels  17.4 us (24%)
  starting transfers between devices  12.3 us (17%)
  waiting for transfers between devices  9.24 us (12%)
  local copies, waits for them, and re-layouts  1.01 us (1%)
    all_to_all x1, blocking collectives, on_device(): arrived = lax.all_to_all(packet, SAME, 0, 0, tiled=True)  33.4 us
    all_to_all x1, waiting for transfers between devices, on_device(): refs_own = lax.all_to_all(spread, SAME, 0, 0, tiled=True)  9.23 us
    pallas_call x1, Pallas kernels, on_device(): pl.pallas_call(decimate_kernel, out_shape=(jax.ShapeDtypeStruct((rows_dev...  6.96 us
    ppermute x3, starting transfers between devices, swap_cores(): return lax.ppermute(x, 'core', [(0, 1), (1, 0)])  6.32 us
    pallas_call x1, Pallas kernels, on_device(): pl.pallas_call(correlate_kernel, out_shape=jax.ShapeDtypeStruct((1, 4 * C...  6.31 us
    all_to_all x1, starting transfers between devices, on_device(): refs_own = lax.all_to_all(spread, SAME, 0, 0, tiled=True)  6.02 us
    pallas_call x1, Pallas kernels, on_device(): pl.pallas_call(route_kernel, out_shape=packet_shape, in_specs=[VMEM, VMEM...  1.6 us
    pallas_call x1, Pallas kernels, on_device(): pl.pallas_call(widen_kernel, out_shape=jax.ShapeDtypeStruct((4 * CHIPS, 2...  1.55 us
  transfers between devices with their start and end apart: 4, of which 1 were waited for; matrix products, arithmetic and copies ran while one was open for 0% of the time, Pallas kernels for 4%

profile of v5, /device:TPU:1, one launch (start us, length us, event | category | flops | bytes accessed | tf_op | source)
XLA Modules:
  0.0 73.7 jit_solution(11157776728149175669)
XLA Ops:
  0.0 0.0 copy-start.2
  0.0 7.0 %decimate.1 = (bf16[96,2048]{1,0:T(8,128)(2,1)}, bf16[64,32,128]{2,1,0:T(8,128)(2,1)}, bf16[64,32,128]{2,1,0:T(8,128)(2,1)}) custom-call(bf16[96,16384]{1,0:T(8,128)(2,1)} %raw_hbm.1, bf16[1,127]{1,0:T(2,128)(2,1)} %bitcast.7, s32[96,128]{1,0:T(8,128)} %bitcast.5, s32[1,256]{1,0:T(1,128)} %bitcast.6), custom_call_target="tpu_custom_call" | custom-call | tf_op jit(solution)/shard_map/decimate/pallas_call | solution.py:209
  7.0 0.0 copy-start
  7.0 1.5 %collective-permute-start = (bf16[64,32,128]{2,1,0:T(8,128)(2,1)}, bf16[64,32,128]{2,1,0:T(8,128)(2,1)S(1)}, u32[]{:S(2)}, u32[]{:S(2)}) collective-permute-start(bf16[64,32,128]{2,1,0:T(8,128)(2,1)} %get-tuple-element.12), channel_id=1, source_target_pairs={{0,4},{4,0},{1,5},{5,1},{2,6},{6,2},{3,7},{7,3},{8,12},{12,8},{9,1... | collective-permute-start | bytes 1572872 | tf_op jit(solution)/shard_map/ppermute | solution.py:200
  8.5 0.0 copy-done.2
  8.5 0.0 copy-start.1
  8.5 1.0 %copy-done.1 = bf16[96,2048]{1,0:T(8,128)(2,1)S(1)} copy-done((bf16[96,2048]{1,0:T(8,128)(2,1)S(1)}, bf16[96,2048]{1,0:T(8,128)(2,1)}, u32[]{:S(2)}) %copy-start.1) | copy-done | bytes 393240
  9.5 1.6 %route.1.packet_in = bf16[64,96,128]{2,1,0:T(8,128)(2,1)S(1)} custom-call(bf16[96,2048]{1,0:T(8,128)(2,1)S(1)} %copy-done.1, s32[1,96]{1,0:T(1,128)S(1)} %bitcast.4), custom_call_target="tpu_custom_call" | custom-call | flops 100000000 | bytes 4000000 | tf_op jit(solution)/shard_map/route/pallas_call | solution.py:230
  11.1 0.0 collective-permute-done.got_ref
  11.1 0.0 copy-done
  11.1 0.1 add_refs.1
  11.2 33.4 %all_to_all.10.arrived_ref = bf16[64,96,128]{2,1,0:T(8,128)(2,1)S(1)} all-to-all(bf16[64,96,128]{2,1,0:T(8,128)(2,1)S(1)} %add_refs.1), channel_id=1, replica_groups=mesh['x'=4,'z'=4,'core'=2,'chan'=4] {'x','z','chan'}, dimensions={0} | all-to-all | bytes 3145728 | tf_op jit(solution)/shard_map/all_to_all | solution.py:249
  44.7 0.9 %spread.1 = (bf16[64,32,128]{2,1,0:T(8,128)(2,1)}, bf16[64,32,128]{2,1,0:T(8,128)(2,1)S(1)}) custom-call(bf16[64,96,128]{2,1,0:T(8,128)(2,1)S(1)} %all_to_all.10.arrived_ref), custom_call_target="tpu_custom_call" | custom-call | tf_op jit(solution)/shard_map/spread/pallas_call | solution.py:250
  45.6 6.0 %all-to-all-start.1 = ((bf16[64,32,128]{2,1,0:T(8,128)(2,1)}), bf16[64,32,128]{2,1,0:T(8,128)(2,1)S(1)}, u32[]{:S(2)}, u32[]{:S(2)}) async-start(bf16[64,32,128]{2,1,0:T(8,128)(2,1)} %get-tuple-element.14), calls=%async_computation.1 | async-start | bytes 1048576 | tf_op jit(solution)/shard_map/all_to_all | solution.py:258
  51.6 1.7 %collective-permute-start.1 = (bf16[64,32,128]{2,1,0:T(8,128)(2,1)S(1)}, bf16[64,32,128]{2,1,0:T(8,128)(2,1)S(1)}, u32[]{:S(2)}, u32[]{:S(2)}) collective-permute-start(bf16[64,32,128]{2,1,0:T(8,128)(2,1)S(1)} %get-tuple-element.13), channel_id=1, source_target_pairs={{0,4},{4,0},{1,5},{5,1},{2,6},{6,2},{3,7},{7,3},{8,12},{12,8},{9,1... | collective-permute-start | bytes 1572872 | tf_op jit(solution)/shard_map/ppermute | solution.py:200
  53.3 9.2 %all-to-all-done.1.own_ref = bf16[64,32,128]{2,1,0:T(8,128)(2,1)S(1)} async-done(((bf16[64,32,128]{2,1,0:T(8,128)(2,1)}), bf16[64,32,128]{2,1,0:T(8,128)(2,1)S(1)}, u32[]{:S(2)}, u32[]{:S(2)}) %all-to-all-start.1) | async-done | bytes 524320 | tf_op jit(solution)/shard_map/all_to_all | solution.py:258
  62.5 3.1 %collective-permute-start.2 = (bf16[64,32,128]{2,1,0:T(8,128)(2,1)S(1)}, bf16[64,32,128]{2,1,0:T(8,128)(2,1)S(1)}, u32[]{:S(2)}, u32[]{:S(2)}) collective-permute-start(bf16[64,32,128]{2,1,0:T(8,128)(2,1)S(1)} %all-to-all-done.1.own_ref), channel_id=1, source_target_pairs={{0,4},{4,0},{1,5},{5,1},{2,6},{6,2},{3,7},{7,3},{8,12},{12,8},{9,1... | collective-permute-start | bytes 1572872 | tf_op jit(solution)/shard_map/ppermute | solution.py:200
  65.7 0.0 collective-permute-done.1.got_ref
  65.7 1.5 %widen.1.ext_ref = bf16[256,4096]{1,0:T(8,128)(2,1)S(1)} custom-call(bf16[64,96,128]{2,1,0:T(8,128)(2,1)S(1)} %all_to_all.10.arrived_ref, bf16[64,32,128]{2,1,0:T(8,128)(2,1)S(1)} %collective-permute-done.1.got_ref), custom_call_target="tpu_custom_call" | custom-call | tf_op jit(solution)/shard_map/widen/pallas_call | solution.py:260
  67.2 0.0 collective-permute-done.2.other_ref
  67.2 6.3 %correlate.1 = f32[1,256,4096]{2,1,0:T(8,128)} custom-call(bf16[256,4096]{1,0:T(8,128)(2,1)S(1)} %widen.1.ext_ref, bf16[64,32,128]{2,1,0:T(8,128)(2,1)S(1)} %all-to-all-done.1.own_ref, bf16[64,32,128]{2,1,0:T(8,128)(2,1)S(1)} %collective-permute-done.2.other_ref), custom_call_target="tpu_custom_call" | custom-call | tf_op jit(solution)/shard_map/correlate/pallas_call | solution.py:270
Async XLA Ops:
  0.0 8.5 %copy-start.2 = (s32[96,1]{0,1:T(1,128)S(1)}, s32[96,1]{0,1:T(1,128)}, u32[]{:S(2)}) copy-start(s32[96,1]{0,1:T(1,128)} %param.9) | copy-start | bytes 1156
  7.0 4.1 %copy-start = (bf16[64,32,128]{2,1,0:T(8,128)(2,1)S(1)}, bf16[64,32,128]{2,1,0:T(8,128)(2,1)}, u32[]{:S(2)}) copy-start(bf16[64,32,128]{2,1,0:T(8,128)(2,1)} %get-tuple-element.11.keep_ref) | copy-start | bytes 1572868
  7.0 4.1 %collective-permute-start = (bf16[64,32,128]{2,1,0:T(8,128)(2,1)}, bf16[64,32,128]{2,1,0:T(8,128)(2,1)S(1)}, u32[]{:S(2)}, u32[]{:S(2)}) collective-permute-start(bf16[64,32,128]{2,1,0:T(8,128)(2,1)} %get-tuple-element.12), channel_id=1, source_target_pairs={{0,4},{4,0},{1,5},{5,1},{2,6},{6,2},{3,7},{7,3},{8,12},{12,8},{9,1... | collective-permute-start | bytes 1572872 | tf_op jit(solution)/shard_map/ppermute | solution.py:200
  8.5 1.0 %copy-start.1 = (bf16[96,2048]{1,0:T(8,128)(2,1)S(1)}, bf16[96,2048]{1,0:T(8,128)(2,1)}, u32[]{:S(2)}) copy-start(bf16[96,2048]{1,0:T(8,128)(2,1)} %get-tuple-element.10.dec_ref) | copy-start | bytes 1179652
  45.6 17.0 %all-to-all-start.1 = ((bf16[64,32,128]{2,1,0:T(8,128)(2,1)}), bf16[64,32,128]{2,1,0:T(8,128)(2,1)S(1)}, u32[]{:S(2)}, u32[]{:S(2)}) async-start(bf16[64,32,128]{2,1,0:T(8,128)(2,1)} %get-tuple-element.14), calls=%async_computation.1 | async-start | bytes 1048576 | tf_op jit(solution)/shard_map/all_to_all | solution.py:258
  51.6 14.1 %collective-permute-start.1 = (bf16[64,32,128]{2,1,0:T(8,128)(2,1)S(1)}, bf16[64,32,128]{2,1,0:T(8,128)(2,1)S(1)}, u32[]{:S(2)}, u32[]{:S(2)}) collective-permute-start(bf16[64,32,128]{2,1,0:T(8,128)(2,1)S(1)} %get-tuple-element.13), channel_id=1, source_target_pairs={{0,4},{4,0},{1,5},{5,1},{2,6},{6,2},{3,7},{7,3},{8,12},{12,8},{9,1... | collective-permute-start | bytes 1572872 | tf_op jit(solution)/shard_map/ppermute | solution.py:200
  62.5 4.7 %collective-permute-start.2 = (bf16[64,32,128]{2,1,0:T(8,128)(2,1)S(1)}, bf16[64,32,128]{2,1,0:T(8,128)(2,1)S(1)}, u32[]{:S(2)}, u32[]{:S(2)}) collective-permute-start(bf16[64,32,128]{2,1,0:T(8,128)(2,1)S(1)} %all-to-all-done.1.own_ref), channel_id=1, source_target_pairs={{0,4},{4,0},{1,5},{5,1},{2,6},{6,2},{3,7},{7,3},{8,12},{12,8},{9,1... | collective-permute-start | bytes 1572872 | tf_op jit(solution)/shard_map/ppermute | solution.py:200

commit v6 on v5

--- a/solution.py
+++ b/solution.py
@@ -38,36 +38,32 @@
 
 
 def decimate_kernel(raw_hbm, taps_hbm, ids_hbm, refch_hbm, dec_ref, keep_ref, give_ref,
-                    raw, taps, ids, refch, line, dec, stage, raw_sem, small_sem):
+                    raw, taps, ids, refch, line, band, dec, stage, raw_sem, small_sem):
     rows = dec_ref.shape[0]
-    groups = raw_sem.shape[0]
     chunk = BLOCK * STRIDE
     window = chunk + 2 * HALO
-    span = raw_hbm.shape[1] // groups
-    loads = [
-        pltpu.make_async_copy(
-            raw_hbm.at[:, pl.ds(m * span, span)], raw.at[:, pl.ds(HALO + m * span, span)], raw_sem.at[m]
-        )
-        for m in range(groups)
-    ]
+    load = pltpu.make_async_copy(raw_hbm, raw.at[:, pl.ds(HALO, raw_hbm.shape[1])], raw_sem)
     small = [
         pltpu.make_async_copy(taps_hbm, taps, small_sem.at[0]),
         pltpu.make_async_copy(ids_hbm, ids, small_sem.at[1]),
         pltpu.make_async_copy(refch_hbm, refch, small_sem.at[2]),
     ]
-    for copy in small + loads:
+    for copy in small + [load]:
         copy.start()
     core = lax.axis_index("core")
     own = lax.axis_index(AXES)
     raw[:, :HALO] = jnp.zeros((rows, HALO), BF16)
     raw[:, raw.shape[1] - HALO :] = jnp.zeros((rows, HALO), BF16)
     line[...] = jnp.zeros_like(line)
+    band[...] = jnp.zeros_like(band)
     small[0].wait()
     line[0:1, 0:TAPS] = taps[...].astype(F32)
-    band = pltpu.roll(
-        jnp.broadcast_to(line[0:1, :], (BLOCK, window)), HALO - TAPS // 2, 1, stride=STRIDE, stride_axis=0
-    )
-    band = jnp.transpose(band).astype(BF16)
+    width = line.shape[1]
+    first = pltpu.roll(
+        jnp.broadcast_to(line[0:1, :], (16, width)), HALO - TAPS // 2, 1, stride=STRIDE, stride_axis=0
+    ).astype(BF16)
+    for i in range(BLOCK // 16):
+        band[16 * i : 16 * (i + 1), LANES * i : LANES * i + width] = first
     small[1].wait()
     small[2].wait()
     at = own * rows
@@ -80,16 +76,12 @@
     mine = jnp.where(iota((8, LANES), 1) < turn, pair[0], pair[1])[0:1, :rows]
     refcol = jnp.transpose(jnp.broadcast_to(refch[...], (LANES, NREF)))[:, :rows]
     select = jnp.where(refcol == mine, 1.0, 0.0).astype(BF16)
-    per = span // chunk
-    loads[0].wait()
-    for m in range(groups):
-        if m + 1 < groups:
-            loads[m + 1].wait()
-        windows = [raw[:, pl.ds((m * per + i) * chunk, window)] for i in range(per)]
-        part = jnp.dot(jnp.concatenate(windows, axis=0), band, preferred_element_type=F32).astype(BF16)
-        for i in range(per):
-            at = (m * per + i) * LANES
-            dec[:, at : at + LANES] = part[i * rows : (i + 1) * rows].astype(F32)
+    load.wait()
+    for at in range(0, LAGS, 2):
+        windows = [raw[:, pl.ds((at + i) * chunk, window)] for i in range(2)]
+        part = dot_nt(jnp.concatenate(windows, axis=0), band[...])
+        for i in range(2):
+            dec[:, (at + i) * LANES : (at + i + 1) * LANES] = part[i * rows : (i + 1) * rows].astype(BF16)
     lane = iota((16, LANES), 1)
     for r in range(0, rows, 16):
         pieces = [dec[r : r + 16, m * LANES : (m + 1) * LANES] for m in range(LAGS)]
@@ -101,7 +93,7 @@
                     pieces[t] = jnp.where(low, x, pltpu.roll(y, k, 1))
                     pieces[t | k] = jnp.where(low, pltpu.roll(x, LANES - k, 1), y)
         for b in range(LAGS):
-            dec_ref[r : r + 16, b * LANES : (b + 1) * LANES] = pieces[b].astype(BF16)
+            dec_ref[r : r + 16, b * LANES : (b + 1) * LANES] = pieces[b]
     for b in range(0, LAGS, 2):
         picked = jnp.dot(select, dec_ref[:, b * LANES : (b + 2) * LANES], preferred_element_type=F32)
         for g in range(4):
@@ -216,10 +208,11 @@
             pltpu.VMEM((1, TAPS), BF16),
             pltpu.VMEM(ids.shape, jnp.int32),
             pltpu.VMEM((1, NREF), jnp.int32),
-            pltpu.VMEM((8, window), F32),
-            pltpu.VMEM((rows_dev, total), F32),
+            pltpu.VMEM((8, 3 * LANES), F32),
+            pltpu.VMEM((BLOCK, window), BF16),
+            pltpu.VMEM((rows_dev, total), BF16),
             pltpu.VMEM((2, CHIPS * 2 * LAGS, LANES), F32),
-            pltpu.SemaphoreType.DMA((4,)),
+            pltpu.SemaphoreType.DMA,
             pltpu.SemaphoreType.DMA((3,)),
         ],
         compiler_params=params(54),

time: 74 us -> 73.2 us (0.989)
    pallas_call x1, Pallas kernels: 6.96 us -> 6.21 us  [on_device(): pl.pallas_call(decimate_kernel, out_shape=(jax.ShapeDtypeStruct((rows_dev...]
where the time goes in v6:
time: 73.2 us; the launch traced here: 73 us
  blocking collectives  33.4 us (46%)
  Pallas kernels  16.7 us (23%)
  starting transfers between devices  12.3 us (17%)
  waiting for transfers between devices  9.24 us (13%)
  local copies, waits for them, and re-layouts  1.01 us (1%)
    all_to_all x1, blocking collectives, on_device(): arrived = lax.all_to_all(packet, SAME, 0, 0, tiled=True)  33.4 us
    all_to_all x1, waiting for transfers between devices, on_device(): refs_own = lax.all_to_all(spread, SAME, 0, 0, tiled=True)  9.23 us
    ppermute x3, starting transfers between devices, swap_cores(): return lax.ppermute(x, 'core', [(0, 1), (1, 0)])  6.32 us
    pallas_call x1, Pallas kernels, on_device(): pl.pallas_call(correlate_kernel, out_shape=jax.ShapeDtypeStruct((1, 4 * C...  6.3 us
    pallas_call x1, Pallas kernels, on_device(): pl.pallas_call(decimate_kernel, out_shape=(jax.ShapeDtypeStruct((rows_dev...  6.21 us
    all_to_all x1, starting transfers between devices, on_device(): refs_own = lax.all_to_all(spread, SAME, 0, 0, tiled=True)  6.02 us
    pallas_call x1, Pallas kernels, on_device(): pl.pallas_call(route_kernel, out_shape=packet_shape, in_specs=[VMEM, VMEM...  1.6 us
    pallas_call x1, Pallas kernels, on_device(): pl.pallas_call(widen_kernel, out_shape=jax.ShapeDtypeStruct((4 * CHIPS, 2...  1.55 us
  transfers between devices with their start and end apart: 4, of which 1 were waited for; matrix products, arithmetic and copies ran while one was open for 0% of the time, Pallas kernels for 4%

profile of v6, /device:TPU:1, one launch (start us, length us, event | category | flops | bytes accessed | tf_op | source)
XLA Modules:
  0.0 73.0 jit_solution(5976601044625797607)
XLA Ops:
  0.0 0.0 copy-start.2
  0.0 6.2 %decimate.1 = (bf16[96,2048]{1,0:T(8,128)(2,1)}, bf16[64,32,128]{2,1,0:T(8,128)(2,1)}, bf16[64,32,128]{2,1,0:T(8,128)(2,1)}) custom-call(bf16[96,16384]{1,0:T(8,128)(2,1)} %raw_hbm.1, bf16[1,127]{1,0:T(2,128)(2,1)} %bitcast.7, s32[96,128]{1,0:T(8,128)} %bitcast.5, s32[1,256]{1,0:T(1,128)} %bitcast.6), custom_call_target="tpu_custom_call" | custom-call | tf_op jit(solution)/shard_map/decimate/pallas_call | solution.py:201
  6.2 0.0 copy-start
  6.2 1.5 %collective-permute-start = (bf16[64,32,128]{2,1,0:T(8,128)(2,1)}, bf16[64,32,128]{2,1,0:T(8,128)(2,1)S(1)}, u32[]{:S(2)}, u32[]{:S(2)}) collective-permute-start(bf16[64,32,128]{2,1,0:T(8,128)(2,1)} %get-tuple-element.12), channel_id=1, source_target_pairs={{0,4},{4,0},{1,5},{5,1},{2,6},{6,2},{3,7},{7,3},{8,12},{12,8},{9,1... | collective-permute-start | bytes 1572872 | tf_op jit(solution)/shard_map/ppermute | solution.py:192
  7.7 0.0 copy-done.2
  7.7 0.0 copy-start.1
  7.7 1.0 %copy-done.1 = bf16[96,2048]{1,0:T(8,128)(2,1)S(1)} copy-done((bf16[96,2048]{1,0:T(8,128)(2,1)S(1)}, bf16[96,2048]{1,0:T(8,128)(2,1)}, u32[]{:S(2)}) %copy-start.1) | copy-done | bytes 393240
  8.7 1.6 %route.1.packet_in = bf16[64,96,128]{2,1,0:T(8,128)(2,1)S(1)} custom-call(bf16[96,2048]{1,0:T(8,128)(2,1)S(1)} %copy-done.1, s32[1,96]{1,0:T(1,128)S(1)} %bitcast.4), custom_call_target="tpu_custom_call" | custom-call | flops 100000000 | bytes 4000000 | tf_op jit(solution)/shard_map/route/pallas_call | solution.py:223
  10.3 0.0 collective-permute-done.got_ref
  10.4 0.0 copy-done
  10.4 0.1 add_refs.1
  10.5 33.4 %all_to_all.10.arrived_ref = bf16[64,96,128]{2,1,0:T(8,128)(2,1)S(1)} all-to-all(bf16[64,96,128]{2,1,0:T(8,128)(2,1)S(1)} %add_refs.1), channel_id=1, replica_groups=mesh['x'=4,'z'=4,'core'=2,'chan'=4] {'x','z','chan'}, dimensions={0} | all-to-all | bytes 3145728 | tf_op jit(solution)/shard_map/all_to_all | solution.py:242
  43.9 0.9 %spread.1 = (bf16[64,32,128]{2,1,0:T(8,128)(2,1)}, bf16[64,32,128]{2,1,0:T(8,128)(2,1)S(1)}) custom-call(bf16[64,96,128]{2,1,0:T(8,128)(2,1)S(1)} %all_to_all.10.arrived_ref), custom_call_target="tpu_custom_call" | custom-call | tf_op jit(solution)/shard_map/spread/pallas_call | solution.py:243
  44.8 6.0 %all-to-all-start.1 = ((bf16[64,32,128]{2,1,0:T(8,128)(2,1)}), bf16[64,32,128]{2,1,0:T(8,128)(2,1)S(1)}, u32[]{:S(2)}, u32[]{:S(2)}) async-start(bf16[64,32,128]{2,1,0:T(8,128)(2,1)} %get-tuple-element.14), calls=%async_computation.1 | async-start | bytes 1048576 | tf_op jit(solution)/shard_map/all_to_all | solution.py:251
  50.9 1.7 %collective-permute-start.1 = (bf16[64,32,128]{2,1,0:T(8,128)(2,1)S(1)}, bf16[64,32,128]{2,1,0:T(8,128)(2,1)S(1)}, u32[]{:S(2)}, u32[]{:S(2)}) collective-permute-start(bf16[64,32,128]{2,1,0:T(8,128)(2,1)S(1)} %get-tuple-element.13), channel_id=1, source_target_pairs={{0,4},{4,0},{1,5},{5,1},{2,6},{6,2},{3,7},{7,3},{8,12},{12,8},{9,1... | collective-permute-start | bytes 1572872 | tf_op jit(solution)/shard_map/ppermute | solution.py:192
  52.6 9.2 %all-to-all-done.1.own_ref = bf16[64,32,128]{2,1,0:T(8,128)(2,1)S(1)} async-done(((bf16[64,32,128]{2,1,0:T(8,128)(2,1)}), bf16[64,32,128]{2,1,0:T(8,128)(2,1)S(1)}, u32[]{:S(2)}, u32[]{:S(2)}) %all-to-all-start.1) | async-done | bytes 524320 | tf_op jit(solution)/shard_map/all_to_all | solution.py:251
  61.8 3.1 %collective-permute-start.2 = (bf16[64,32,128]{2,1,0:T(8,128)(2,1)S(1)}, bf16[64,32,128]{2,1,0:T(8,128)(2,1)S(1)}, u32[]{:S(2)}, u32[]{:S(2)}) collective-permute-start(bf16[64,32,128]{2,1,0:T(8,128)(2,1)S(1)} %all-to-all-done.1.own_ref), channel_id=1, source_target_pairs={{0,4},{4,0},{1,5},{5,1},{2,6},{6,2},{3,7},{7,3},{8,12},{12,8},{9,1... | collective-permute-start | bytes 1572872 | tf_op jit(solution)/shard_map/ppermute | solution.py:192
  64.9 0.0 collective-permute-done.1.got_ref
  64.9 1.5 %widen.1.ext_ref = bf16[256,4096]{1,0:T(8,128)(2,1)S(1)} custom-call(bf16[64,96,128]{2,1,0:T(8,128)(2,1)S(1)} %all_to_all.10.arrived_ref, bf16[64,32,128]{2,1,0:T(8,128)(2,1)S(1)} %collective-permute-done.1.got_ref), custom_call_target="tpu_custom_call" | custom-call | tf_op jit(solution)/shard_map/widen/pallas_call | solution.py:253
  66.5 0.0 collective-permute-done.2.other_ref
  66.5 6.3 %correlate.1 = f32[1,256,4096]{2,1,0:T(8,128)} custom-call(bf16[256,4096]{1,0:T(8,128)(2,1)S(1)} %widen.1.ext_ref, bf16[64,32,128]{2,1,0:T(8,128)(2,1)S(1)} %all-to-all-done.1.own_ref, bf16[64,32,128]{2,1,0:T(8,128)(2,1)S(1)} %collective-permute-done.2.other_ref), custom_call_target="tpu_custom_call" | custom-call | tf_op jit(solution)/shard_map/correlate/pallas_call | solution.py:263
Async XLA Ops:
  0.0 7.7 %copy-start.2 = (s32[96,1]{0,1:T(1,128)S(1)}, s32[96,1]{0,1:T(1,128)}, u32[]{:S(2)}) copy-start(s32[96,1]{0,1:T(1,128)} %param.9) | copy-start | bytes 1156
  6.2 4.1 %copy-start = (bf16[64,32,128]{2,1,0:T(8,128)(2,1)S(1)}, bf16[64,32,128]{2,1,0:T(8,128)(2,1)}, u32[]{:S(2)}) copy-start(bf16[64,32,128]{2,1,0:T(8,128)(2,1)} %get-tuple-element.11.keep_ref) | copy-start | bytes 1572868
  6.2 4.1 %collective-permute-start = (bf16[64,32,128]{2,1,0:T(8,128)(2,1)}, bf16[64,32,128]{2,1,0:T(8,128)(2,1)S(1)}, u32[]{:S(2)}, u32[]{:S(2)}) collective-permute-start(bf16[64,32,128]{2,1,0:T(8,128)(2,1)} %get-tuple-element.12), channel_id=1, source_target_pairs={{0,4},{4,0},{1,5},{5,1},{2,6},{6,2},{3,7},{7,3},{8,12},{12,8},{9,1... | collective-permute-start | bytes 1572872 | tf_op jit(solution)/shard_map/ppermute | solution.py:192
  7.7 1.0 %copy-start.1 = (bf16[96,2048]{1,0:T(8,128)(2,1)S(1)}, bf16[96,2048]{1,0:T(8,128)(2,1)}, u32[]{:S(2)}) copy-start(bf16[96,2048]{1,0:T(8,128)(2,1)} %get-tuple-element.10.dec_ref) | copy-start | bytes 1179652
  44.8 17.0 %all-to-all-start.1 = ((bf16[64,32,128]{2,1,0:T(8,128)(2,1)}), bf16[64,32,128]{2,1,0:T(8,128)(2,1)S(1)}, u32[]{:S(2)}, u32[]{:S(2)}) async-start(bf16[64,32,128]{2,1,0:T(8,128)(2,1)} %get-tuple-element.14), calls=%async_computation.1 | async-start | bytes 1048576 | tf_op jit(solution)/shard_map/all_to_all | solution.py:251
  50.9 14.1 %collective-permute-start.1 = (bf16[64,32,128]{2,1,0:T(8,128)(2,1)S(1)}, bf16[64,32,128]{2,1,0:T(8,128)(2,1)S(1)}, u32[]{:S(2)}, u32[]{:S(2)}) collective-permute-start(bf16[64,32,128]{2,1,0:T(8,128)(2,1)S(1)} %get-tuple-element.13), channel_id=1, source_target_pairs={{0,4},{4,0},{1,5},{5,1},{2,6},{6,2},{3,7},{7,3},{8,12},{12,8},{9,1... | collective-permute-start | bytes 1572872 | tf_op jit(solution)/shard_map/ppermute | solution.py:192
  61.8 4.7 %collective-permute-start.2 = (bf16[64,32,128]{2,1,0:T(8,128)(2,1)S(1)}, bf16[64,32,128]{2,1,0:T(8,128)(2,1)S(1)}, u32[]{:S(2)}, u32[]{:S(2)}) collective-permute-start(bf16[64,32,128]{2,1,0:T(8,128)(2,1)S(1)} %all-to-all-done.1.own_ref), channel_id=1, source_target_pairs={{0,4},{4,0},{1,5},{5,1},{2,6},{6,2},{3,7},{7,3},{8,12},{12,8},{9,1... | collective-permute-start | bytes 1572872 | tf_op jit(solution)/shard_map/ppermute | solution.py:192

commit v7 on v6

--- a/solution.py
+++ b/solution.py
@@ -37,26 +37,16 @@
     return lax.broadcasted_iota(jnp.int32, shape, dim)
 
 
-def decimate_kernel(raw_hbm, taps_hbm, ids_hbm, refch_hbm, dec_ref, keep_ref, give_ref,
-                    raw, taps, ids, refch, line, band, dec, stage, raw_sem, small_sem):
+def decimate_kernel(raw_hbm, taps, dec_ref, raw, line, band, dec, sem):
     rows = dec_ref.shape[0]
     chunk = BLOCK * STRIDE
     window = chunk + 2 * HALO
-    load = pltpu.make_async_copy(raw_hbm, raw.at[:, pl.ds(HALO, raw_hbm.shape[1])], raw_sem)
-    small = [
-        pltpu.make_async_copy(taps_hbm, taps, small_sem.at[0]),
-        pltpu.make_async_copy(ids_hbm, ids, small_sem.at[1]),
-        pltpu.make_async_copy(refch_hbm, refch, small_sem.at[2]),
-    ]
-    for copy in small + [load]:
-        copy.start()
-    core = lax.axis_index("core")
-    own = lax.axis_index(AXES)
+    load = pltpu.make_async_copy(raw_hbm, raw.at[:, pl.ds(HALO, raw_hbm.shape[1])], sem)
+    load.start()
     raw[:, :HALO] = jnp.zeros((rows, HALO), BF16)
     raw[:, raw.shape[1] - HALO :] = jnp.zeros((rows, HALO), BF16)
     line[...] = jnp.zeros_like(line)
     band[...] = jnp.zeros_like(band)
-    small[0].wait()
     line[0:1, 0:TAPS] = taps[...].astype(F32)
     width = line.shape[1]
     first = pltpu.roll(
@@ -64,18 +54,6 @@
     ).astype(BF16)
     for i in range(BLOCK // 16):
         band[16 * i : 16 * (i + 1), LANES * i : LANES * i + width] = first
-    small[1].wait()
-    small[2].wait()
-    at = own * rows
-    line0 = at // LANES
-    line1 = jnp.minimum(line0 + 1, ids.shape[0] - 1)
-    turn = LANES - (at - line0 * LANES)
-    pair = [
-        pltpu.roll(jnp.broadcast_to(ids[pl.ds(i, 1), :], (8, LANES)), turn, 1) for i in (line0, line1)
-    ]
-    mine = jnp.where(iota((8, LANES), 1) < turn, pair[0], pair[1])[0:1, :rows]
-    refcol = jnp.transpose(jnp.broadcast_to(refch[...], (LANES, NREF)))[:, :rows]
-    select = jnp.where(refcol == mine, 1.0, 0.0).astype(BF16)
     load.wait()
     for at in range(0, LAGS, 2):
         windows = [raw[:, pl.ds((at + i) * chunk, window)] for i in range(2)]
@@ -94,6 +72,22 @@
                     pieces[t | k] = jnp.where(low, pltpu.roll(x, LANES - k, 1), y)
         for b in range(LAGS):
             dec_ref[r : r + 16, b * LANES : (b + 1) * LANES] = pieces[b]
+
+
+def pick_kernel(dec_ref, ids, refch, keep_ref, give_ref, stage):
+    rows = dec_ref.shape[0]
+    core = lax.axis_index("core")
+    own = lax.axis_index(AXES)
+    at = own * rows
+    line0 = at // LANES
+    line1 = jnp.minimum(line0 + 1, ids.shape[0] - 1)
+    turn = LANES - (at - line0 * LANES)
+    pair = [
+        pltpu.roll(jnp.broadcast_to(ids[pl.ds(i, 1), :], (8, LANES)), turn, 1) for i in (line0, line1)
+    ]
+    mine = jnp.where(iota((8, LANES), 1) < turn, pair[0], pair[1])[0:1, :rows]
+    refcol = jnp.transpose(jnp.broadcast_to(refch[...], (LANES, NREF)))[:, :rows]
+    select = jnp.where(refcol == mine, 1.0, 0.0).astype(BF16)
     for b in range(0, LAGS, 2):
         picked = jnp.dot(select, dec_ref[:, b * LANES : (b + 2) * LANES], preferred_element_type=F32)
         for g in range(4):
@@ -198,26 +192,30 @@
     window = BLOCK * STRIDE + 2 * HALO
     half = jax.ShapeDtypeStruct((CHIPS, 2 * LAGS, LANES), BF16)
     ids = row_channel.reshape(-1, LANES)
-    dec, keep, give = pl.pallas_call(
+    dec = pl.pallas_call(
         decimate_kernel,
-        out_shape=(jax.ShapeDtypeStruct((rows_dev, total), BF16), half, half),
-        in_specs=[HBM] * 4,
-        out_specs=(VMEM, VMEM, VMEM),
+        out_shape=jax.ShapeDtypeStruct((rows_dev, total), BF16),
+        in_specs=[HBM, VMEM],
+        out_specs=VMEM,
         scratch_shapes=[
             pltpu.VMEM((rows_dev, samples + 2 * HALO), BF16),
-            pltpu.VMEM((1, TAPS), BF16),
-            pltpu.VMEM(ids.shape, jnp.int32),
-            pltpu.VMEM((1, NREF), jnp.int32),
             pltpu.VMEM((8, 3 * LANES), F32),
             pltpu.VMEM((BLOCK, window), BF16),
             pltpu.VMEM((rows_dev, total), BF16),
-            pltpu.VMEM((2, CHIPS * 2 * LAGS, LANES), F32),
             pltpu.SemaphoreType.DMA,
-            pltpu.SemaphoreType.DMA((3,)),
         ],
-        compiler_params=params(54),
+        compiler_params=params(52),
         name="decimate",
-    )(raw, taps.reshape(1, TAPS), ids, ref_channel.reshape(1, NREF))
+    )(raw, taps.reshape(1, TAPS))
+    keep, give = pl.pallas_call(
+        pick_kernel,
+        out_shape=(half, half),
+        in_specs=[VMEM] * 3,
+        out_specs=(VMEM, VMEM),
+        scratch_shapes=[pltpu.VMEM((2, CHIPS * 2 * LAGS, LANES), F32)],
+        compiler_params=params(),
+        name="pick",
+    )(dec, ids, ref_channel.reshape(1, NREF))
     got = swap_cores(give)
     packet_shape = jax.ShapeDtypeStruct((CHIPS, 6 * LAGS, LANES), BF16)
     packet = pl.pallas_call(

time: 73.2 us -> 71.7 us (0.980)
  Pallas kernels: 16.7 us -> 15.6 us
    pallas_call x1 -> x2, Pallas kernels: 6.21 us -> 5.12 us  [the longest x1 3.48 us: on_device(): pl.pallas_call(decimate_kernel, out_shape=jax.ShapeDtypeStruct((rows_dev,...]
where the time goes in v7:
time: 71.7 us; the launch traced here: 71.4 us
  blocking collectives  33.6 us (47%)
  Pallas kernels  15.6 us (22%)
  starting transfers between devices  12.1 us (17%)
  waiting for transfers between devices  9.23 us (13%)
    all_to_all x1, blocking collectives, on_device(): arrived = lax.all_to_all(packet, SAME, 0, 0, tiled=True)  33.6 us
    all_to_all x1, waiting for transfers between devices, on_device(): refs_own = lax.all_to_all(spread, SAME, 0, 0, tiled=True)  9.22 us
    ppermute x3, starting transfers between devices, swap_cores(): return lax.ppermute(x, 'core', [(0, 1), (1, 0)])  6.33 us
    pallas_call x1, Pallas kernels, on_device(): pl.pallas_call(correlate_kernel, out_shape=jax.ShapeDtypeStruct((1, 4 * C...  6.31 us
    all_to_all x1, starting transfers between devices, on_device(): refs_own = lax.all_to_all(spread, SAME, 0, 0, tiled=True)  5.73 us
    pallas_call x1, Pallas kernels, on_device(): pl.pallas_call(decimate_kernel, out_shape=jax.ShapeDtypeStruct((rows_dev,...  3.48 us
    pallas_call x1, Pallas kernels, on_device(): pl.pallas_call(pick_kernel, out_shape=(half, half), in_specs=[VMEM] * 3,...  1.64 us
    pallas_call x1, Pallas kernels, on_device(): pl.pallas_call(route_kernel, out_shape=packet_shape, in_specs=[VMEM, VMEM...  1.6 us
  transfers between devices with their start and end apart: 4, of which 1 were waited for; matrix products, arithmetic and copies ran while one was open for 0% of the time, Pallas kernels for 4%

profile of v7, /device:TPU:1, one launch (start us, length us, event | category | flops | bytes accessed | tf_op | source)
XLA Modules:
  0.0 71.4 jit_solution(4721773154963878923)
XLA Ops:
  0.0 0.0 copy-start.1
  0.0 0.0 copy-start
  0.0 0.0 copy-start.2
  0.0 0.0 copy-start.3
  0.0 0.7 copy-done.3
  0.7 3.5 %decimate.1.dec_ref = bf16[96,2048]{1,0:T(8,128)(2,1)S(1)} custom-call(bf16[96,16384]{1,0:T(8,128)(2,1)} %raw_hbm.1, bf16[1,127]{1,0:T(2,128)(2,1)S(1)} %bitcast.7), custom_call_target="tpu_custom_call" | custom-call | tf_op jit(solution)/shard_map/decimate/pallas_call | solution.py:195
  4.2 0.0 copy-done.1
  4.2 0.0 copy-done
  4.2 1.6 %pick.1 = (bf16[64,32,128]{2,1,0:T(8,128)(2,1)S(1)}, bf16[64,32,128]{2,1,0:T(8,128)(2,1)S(1)}) custom-call(bf16[96,2048]{1,0:T(8,128)(2,1)S(1)} %decimate.1.dec_ref, s32[96,128]{1,0:T(8,128)S(1)} %bitcast.4, s32[1,256]{1,0:T(1,128)S(1)} %bitcast.5), custom_call_target="tpu_custom_call" | custom-call | tf_op jit(solution)/shard_map/pick/pallas_call | solution.py:210
  5.8 1.5 %collective-permute-start = (bf16[64,32,128]{2,1,0:T(8,128)(2,1)S(1)}, bf16[64,32,128]{2,1,0:T(8,128)(2,1)S(1)}, u32[]{:S(2)}, u32[]{:S(2)}) collective-permute-start(bf16[64,32,128]{2,1,0:T(8,128)(2,1)S(1)} %get-tuple-element.10), channel_id=1, source_target_pairs={{0,4},{4,0},{1,5},{5,1},{2,6},{6,2},{3,7},{7,3},{8,12},{12,8},{9,1... | collective-permute-start | bytes 1572872 | tf_op jit(solution)/shard_map/ppermute | solution.py:186
  7.3 0.0 copy-done.2
  7.3 1.6 %route.1.packet_in = bf16[64,96,128]{2,1,0:T(8,128)(2,1)S(1)} custom-call(bf16[96,2048]{1,0:T(8,128)(2,1)S(1)} %decimate.1.dec_ref, s32[1,96]{1,0:T(1,128)S(1)} %bitcast.6), custom_call_target="tpu_custom_call" | custom-call | flops 100000000 | bytes 4000000 | tf_op jit(solution)/shard_map/route/pallas_call | solution.py:221
  9.0 0.0 collective-permute-done.got_ref
  9.0 0.1 add_refs.1
  9.1 33.6 %all_to_all.10.arrived_ref = bf16[64,96,128]{2,1,0:T(8,128)(2,1)S(1)} all-to-all(bf16[64,96,128]{2,1,0:T(8,128)(2,1)S(1)} %add_refs.1), channel_id=1, replica_groups=mesh['x'=4,'z'=4,'core'=2,'chan'=4] {'x','z','chan'}, dimensions={0} | all-to-all | bytes 3145728 | tf_op jit(solution)/shard_map/all_to_all | solution.py:240
  42.7 0.9 %spread.1 = (bf16[64,32,128]{2,1,0:T(8,128)(2,1)}, bf16[64,32,128]{2,1,0:T(8,128)(2,1)S(1)}) custom-call(bf16[64,96,128]{2,1,0:T(8,128)(2,1)S(1)} %all_to_all.10.arrived_ref), custom_call_target="tpu_custom_call" | custom-call | tf_op jit(solution)/shard_map/spread/pallas_call | solution.py:241
  43.6 5.7 %all-to-all-start.1 = ((bf16[64,32,128]{2,1,0:T(8,128)(2,1)}), bf16[64,32,128]{2,1,0:T(8,128)(2,1)S(1)}, u32[]{:S(2)}, u32[]{:S(2)}) async-start(bf16[64,32,128]{2,1,0:T(8,128)(2,1)} %get-tuple-element.12), calls=%async_computation.1 | async-start | bytes 1048576 | tf_op jit(solution)/shard_map/all_to_all | solution.py:249
  49.3 1.7 %collective-permute-start.1 = (bf16[64,32,128]{2,1,0:T(8,128)(2,1)S(1)}, bf16[64,32,128]{2,1,0:T(8,128)(2,1)S(1)}, u32[]{:S(2)}, u32[]{:S(2)}) collective-permute-start(bf16[64,32,128]{2,1,0:T(8,128)(2,1)S(1)} %get-tuple-element.11), channel_id=1, source_target_pairs={{0,4},{4,0},{1,5},{5,1},{2,6},{6,2},{3,7},{7,3},{8,12},{12,8},{9,1... | collective-permute-start | bytes 1572872 | tf_op jit(solution)/shard_map/ppermute | solution.py:186
  51.0 9.2 %all-to-all-done.1.own_ref = bf16[64,32,128]{2,1,0:T(8,128)(2,1)S(1)} async-done(((bf16[64,32,128]{2,1,0:T(8,128)(2,1)}), bf16[64,32,128]{2,1,0:T(8,128)(2,1)S(1)}, u32[]{:S(2)}, u32[]{:S(2)}) %all-to-all-start.1) | async-done | bytes 524320 | tf_op jit(solution)/shard_map/all_to_all | solution.py:249
  60.2 3.1 %collective-permute-start.2 = (bf16[64,32,128]{2,1,0:T(8,128)(2,1)S(1)}, bf16[64,32,128]{2,1,0:T(8,128)(2,1)S(1)}, u32[]{:S(2)}, u32[]{:S(2)}) collective-permute-start(bf16[64,32,128]{2,1,0:T(8,128)(2,1)S(1)} %all-to-all-done.1.own_ref), channel_id=1, source_target_pairs={{0,4},{4,0},{1,5},{5,1},{2,6},{6,2},{3,7},{7,3},{8,12},{12,8},{9,1... | collective-permute-start | bytes 1572872 | tf_op jit(solution)/shard_map/ppermute | solution.py:186
  63.4 0.0 collective-permute-done.1.got_ref
  63.4 1.5 %widen.1.ext_ref = bf16[256,4096]{1,0:T(8,128)(2,1)S(1)} custom-call(bf16[64,96,128]{2,1,0:T(8,128)(2,1)S(1)} %all_to_all.10.arrived_ref, bf16[64,32,128]{2,1,0:T(8,128)(2,1)S(1)} %collective-permute-done.1.got_ref), custom_call_target="tpu_custom_call" | custom-call | tf_op jit(solution)/shard_map/widen/pallas_call | solution.py:251
  64.9 0.0 collective-permute-done.2.other_ref
  64.9 6.3 %correlate.1 = f32[1,256,4096]{2,1,0:T(8,128)} custom-call(bf16[256,4096]{1,0:T(8,128)(2,1)S(1)} %widen.1.ext_ref, bf16[64,32,128]{2,1,0:T(8,128)(2,1)S(1)} %all-to-all-done.1.own_ref, bf16[64,32,128]{2,1,0:T(8,128)(2,1)S(1)} %collective-permute-done.2.other_ref), custom_call_target="tpu_custom_call" | custom-call | tf_op jit(solution)/shard_map/correlate/pallas_call | solution.py:261
Async XLA Ops:
  0.0 4.2 %copy-start.1 = (s32[256]{0:T(256)S(1)}, s32[256]{0:T(256)}, u32[]{:S(2)}) copy-start(s32[256]{0:T(256)} %param.8) | copy-start | bytes 3076
  0.0 4.2 %copy-start = (s32[12288]{0:T(1024)S(1)}, s32[12288]{0:T(1024)}, u32[]{:S(2)}) copy-start(s32[12288]{0:T(1024)} %param.7) | copy-start | bytes 147460
  0.0 7.3 %copy-start.2 = (s32[96,1]{0,1:T(1,128)S(1)}, s32[96,1]{0,1:T(1,128)}, u32[]{:S(2)}) copy-start(s32[96,1]{0,1:T(1,128)} %param.9) | copy-start | bytes 1156
  0.0 0.7 copy-start.3
  5.8 3.1 %collective-permute-start = (bf16[64,32,128]{2,1,0:T(8,128)(2,1)S(1)}, bf16[64,32,128]{2,1,0:T(8,128)(2,1)S(1)}, u32[]{:S(2)}, u32[]{:S(2)}) collective-permute-start(bf16[64,32,128]{2,1,0:T(8,128)(2,1)S(1)} %get-tuple-element.10), channel_id=1, source_target_pairs={{0,4},{4,0},{1,5},{5,1},{2,6},{6,2},{3,7},{7,3},{8,12},{12,8},{9,1... | collective-permute-start | bytes 1572872 | tf_op jit(solution)/shard_map/ppermute | solution.py:186
  43.6 16.7 %all-to-all-start.1 = ((bf16[64,32,128]{2,1,0:T(8,128)(2,1)}), bf16[64,32,128]{2,1,0:T(8,128)(2,1)S(1)}, u32[]{:S(2)}, u32[]{:S(2)}) async-start(bf16[64,32,128]{2,1,0:T(8,128)(2,1)} %get-tuple-element.12), calls=%async_computation.1 | async-start | bytes 1048576 | tf_op jit(solution)/shard_map/all_to_all | solution.py:249
  49.3 14.1 %collective-permute-start.1 = (bf16[64,32,128]{2,1,0:T(8,128)(2,1)S(1)}, bf16[64,32,128]{2,1,0:T(8,128)(2,1)S(1)}, u32[]{:S(2)}, u32[]{:S(2)}) collective-permute-start(bf16[64,32,128]{2,1,0:T(8,128)(2,1)S(1)} %get-tuple-element.11), channel_id=1, source_target_pairs={{0,4},{4,0},{1,5},{5,1},{2,6},{6,2},{3,7},{7,3},{8,12},{12,8},{9,1... | collective-permute-start | bytes 1572872 | tf_op jit(solution)/shard_map/ppermute | solution.py:186
  60.2 4.7 %collective-permute-start.2 = (bf16[64,32,128]{2,1,0:T(8,128)(2,1)S(1)}, bf16[64,32,128]{2,1,0:T(8,128)(2,1)S(1)}, u32[]{:S(2)}, u32[]{:S(2)}) collective-permute-start(bf16[64,32,128]{2,1,0:T(8,128)(2,1)S(1)} %all-to-all-done.1.own_ref), channel_id=1, source_target_pairs={{0,4},{4,0},{1,5},{5,1},{2,6},{6,2},{3,7},{7,3},{8,12},{12,8},{9,1... | collective-permute-start | bytes 1572872 | tf_op jit(solution)/shard_map/ppermute | solution.py:186

commit v8 on v7

--- a/solution.py
+++ b/solution.py
@@ -74,8 +74,9 @@
             dec_ref[r : r + 16, b * LANES : (b + 1) * LANES] = pieces[b]
 
 
-def pick_kernel(dec_ref, ids, refch, keep_ref, give_ref, stage):
+def pick_kernel(dec_ref, ids, refch, keep_ref, give_ref):
     rows = dec_ref.shape[0]
+    count = keep_ref.shape[0]
     core = lax.axis_index("core")
     own = lax.axis_index(AXES)
     at = own * rows
@@ -87,17 +88,15 @@
     ]
     mine = jnp.where(iota((8, LANES), 1) < turn, pair[0], pair[1])[0:1, :rows]
     refcol = jnp.transpose(jnp.broadcast_to(refch[...], (LANES, NREF)))[:, :rows]
-    select = jnp.where(refcol == mine, 1.0, 0.0).astype(BF16)
+    select = jnp.where(refcol == mine, 1.0, 0.0)
+    halves = (select[:count], select[count:])
+    halves = (jnp.where(core == 0, *halves), jnp.where(core == 0, *halves[::-1]))
+    select = jnp.concatenate(halves, axis=0).astype(BF16)
     for b in range(0, LAGS, 2):
-        picked = jnp.dot(select, dec_ref[:, b * LANES : (b + 2) * LANES], preferred_element_type=F32)
-        for g in range(4):
-            for h in range(2):
-                stage[g // 2, pl.ds((g % 2) * LAGS + b + h, CHIPS, stride=2 * LAGS), :] = picked[
-                    g * CHIPS : (g + 1) * CHIPS, h * LANES : (h + 1) * LANES
-                ]
-    shape = (CHIPS, 2 * LAGS, LANES)
-    keep_ref[...] = stage[core].astype(BF16).reshape(shape)
-    give_ref[...] = stage[1 - core].astype(BF16).reshape(shape)
+        span = slice(b * LANES, (b + 2) * LANES)
+        picked = jnp.dot(select, dec_ref[:, span], preferred_element_type=F32).astype(BF16)
+        keep_ref[:, span] = picked[:count]
+        give_ref[:, span] = picked[count:]
 
 
 def route_kernel(dec_ref, owner_ref, packet_ref, stage):
@@ -123,9 +122,16 @@
     packet_ref[:, : 4 * LAGS, :] = stage[...].astype(BF16).reshape(CHIPS, 4 * LAGS, LANES)
 
 
-def add_refs_kernel(packet_in, keep_ref, got_ref, packet_ref):
+def add_refs_kernel(packet_in, keep_ref, got_ref, packet_ref, stage):
     del packet_in
-    packet_ref[:, 4 * LAGS :, :] = (keep_ref[...].astype(F32) + got_ref[...].astype(F32)).astype(BF16)
+    for s in range(2):
+        rows = slice(s * CHIPS, (s + 1) * CHIPS)
+        for b in range(LAGS):
+            lanes = slice(b * LANES, (b + 1) * LANES)
+            stage[pl.ds(s * LAGS + b, CHIPS, stride=2 * LAGS), :] = keep_ref[rows, lanes].astype(F32) + got_ref[
+                rows, lanes
+            ].astype(F32)
+    packet_ref[:, 4 * LAGS :, :] = stage[...].astype(BF16).reshape(CHIPS, 2 * LAGS, LANES)
 
 
 def spread_kernel(arrived_ref, spread_ref, give_ref):
@@ -136,7 +142,14 @@
     give_ref[...] = arrived_ref[:, pl.ds(other, 2 * LAGS), :]
 
 
-def widen_kernel(arrived_ref, got_ref, ext_ref, wide):
+def lay_out_refs(refs_ref, wide, write):
+    wide[...] = refs_ref[...].astype(F32).reshape(wide.shape)
+    for s in range(2):
+        for b in range(LAGS):
+            write(s * CHIPS, b * LANES, wide[pl.ds(s * LAGS + b, CHIPS, stride=2 * LAGS), :].astype(BF16))
+
+
+def widen_kernel(arrived_ref, got_ref, own_ref, ext_ref, mine_ref, wide, wide_refs):
     core = lax.axis_index("core")
     size = CHIPS * 2 * LAGS
     mine = pl.multiple_of(core * 2 * LAGS, 2 * LAGS)
@@ -154,18 +167,23 @@
         moved = jnp.where(lane == LANES - 1, 0.0, moved)
         ext_ref[:, total + b * LANES : total + (b + 1) * LANES] = moved.astype(BF16)
 
-
-def correlate_kernel(ext_ref, own_ref, other_ref, out_hbm, wide, refs, sums, sem):
+    def write(row, lane, piece):
+        mine_ref[row : row + CHIPS, lane : lane + LANES] = piece
+
+    lay_out_refs(own_ref, wide_refs, write)
+
+
+def correlate_kernel(ext_ref, mine_ref, other_ref, out_hbm, wide, refs, sums, sem):
     total = LAGS * LANES
-    size = CHIPS * 2 * LAGS
     core = lax.axis_index("core")
-    wide[core] = own_ref[...].astype(F32).reshape(size, LANES)
-    wide[1 - core] = other_ref[...].astype(F32).reshape(size, LANES)
-    for g in range(4):
-        for b in range(LAGS):
-            refs[g * CHIPS : (g + 1) * CHIPS, b * LANES : (b + 1) * LANES] = wide[
-                g // 2, pl.ds((g % 2) * LAGS + b, CHIPS, stride=2 * LAGS), :
-            ].astype(BF16)
+    half = NREF // 2
+
+    def write(row, lane, piece):
+        row = pl.multiple_of((1 - core) * half + row, CHIPS)
+        refs[pl.ds(row, CHIPS), lane : lane + LANES] = piece
+
+    refs[pl.ds(pl.multiple_of(core * half, half), half), :] = mine_ref[...]
+    lay_out_refs(other_ref, wide, write)
     rows = ext_ref.shape[0]
     copies = []
     lag = 1
@@ -191,6 +209,7 @@
     total = samples // STRIDE
     window = BLOCK * STRIDE + 2 * HALO
     half = jax.ShapeDtypeStruct((CHIPS, 2 * LAGS, LANES), BF16)
+    plain = jax.ShapeDtypeStruct((NREF // 2, total), BF16)
     ids = row_channel.reshape(-1, LANES)
     dec = pl.pallas_call(
         decimate_kernel,
@@ -209,10 +228,9 @@
     )(raw, taps.reshape(1, TAPS))
     keep, give = pl.pallas_call(
         pick_kernel,
-        out_shape=(half, half),
+        out_shape=(plain, plain),
         in_specs=[VMEM] * 3,
         out_specs=(VMEM, VMEM),
-        scratch_shapes=[pltpu.VMEM((2, CHIPS * 2 * LAGS, LANES), F32)],
         compiler_params=params(),
         name="pick",
     )(dec, ids, ref_channel.reshape(1, NREF))
@@ -233,6 +251,7 @@
         out_shape=packet_shape,
         in_specs=[VMEM] * 3,
         out_specs=VMEM,
+        scratch_shapes=[pltpu.VMEM((CHIPS * 2 * LAGS, LANES), F32)],
         input_output_aliases={0: 0},
         compiler_params=params(),
         name="add_refs",
@@ -248,15 +267,18 @@
     )(arrived)
     refs_own = lax.all_to_all(spread, SAME, 0, 0, tiled=True)
     rows_got = swap_cores(rows_give)
-    ext = pl.pallas_call(
+    ext, refs_mine = pl.pallas_call(
         widen_kernel,
-        out_shape=jax.ShapeDtypeStruct((4 * CHIPS, 2 * total), BF16),
-        in_specs=[VMEM, VMEM],
-        out_specs=VMEM,
-        scratch_shapes=[pltpu.VMEM((2, CHIPS * 2 * LAGS, LANES), F32)],
+        out_shape=(jax.ShapeDtypeStruct((4 * CHIPS, 2 * total), BF16), plain),
+        in_specs=[VMEM, VMEM, VMEM],
+        out_specs=(VMEM, VMEM),
+        scratch_shapes=[
+            pltpu.VMEM((2, CHIPS * 2 * LAGS, LANES), F32),
+            pltpu.VMEM((CHIPS * 2 * LAGS, LANES), F32),
+        ],
         compiler_params=params(),
         name="widen",
-    )(arrived, rows_got)
+    )(arrived, rows_got, refs_own)
     refs_other = swap_cores(refs_own)
     return pl.pallas_call(
         correlate_kernel,
@@ -264,14 +286,14 @@
         in_specs=[VMEM, VMEM, VMEM],
         out_specs=HBM,
         scratch_shapes=[
-            pltpu.VMEM((2, CHIPS * 2 * LAGS, LANES), F32),
+            pltpu.VMEM((CHIPS * 2 * LAGS, LANES), F32),
             pltpu.VMEM((NREF, total), BF16),
             pltpu.VMEM((4 * CHIPS, LAGS * NREF), F32),
             pltpu.SemaphoreType.DMA((len(LAG_STEPS),)),
         ],
         compiler_params=params(24),
         name="correlate",
-    )(ext, refs_own, refs_other)
+    )(ext, refs_mine, refs_other)
 
 
 def solution(mesh):

time: 71.7 us -> 71.7 us (level)
    pallas_call x1, Pallas kernels: 0.12 us -> 1.1 us  [on_device(): pl.pallas_call(add_refs_kernel, out_shape=packet_shape, in_specs=[VMEM] *...]
  transfers between devices with their start and end apart: 4 -> 4, of which waited for: 1 -> 1; matrix products, arithmetic and copies ran while one was open for 0% -> 0% of each run, Pallas kernels for 4% -> 5%
where the time goes in v8:
time: 71.7 us; the launch traced here: 71.4 us
  blocking collectives  33.6 us (47%)
  Pallas kernels  15.6 us (22%)
  starting transfers between devices  12.1 us (17%)
  waiting for transfers between devices  9.23 us (13%)
    all_to_all x1, blocking collectives, on_device(): arrived = lax.all_to_all(packet, SAME, 0, 0, tiled=True)  33.6 us
    all_to_all x1, waiting for transfers between devices, on_device(): refs_own = lax.all_to_all(spread, SAME, 0, 0, tiled=True)  9.22 us
    ppermute x3, starting transfers between devices, swap_cores(): return lax.ppermute(x, 'core', [(0, 1), (1, 0)])  6.33 us
    pallas_call x1, Pallas kernels, on_device(): pl.pallas_call(correlate_kernel, out_shape=jax.ShapeDtypeStruct((1, 4 * C...  5.79 us
    all_to_all x1, starting transfers between devices, on_device(): refs_own = lax.all_to_all(spread, SAME, 0, 0, tiled=True)  5.73 us
    pallas_call x1, Pallas kernels, on_device(): pl.pallas_call(decimate_kernel, out_shape=jax.ShapeDtypeStruct((rows_dev,...  3.48 us
    pallas_call x1, Pallas kernels, on_device(): pl.pallas_call(widen_kernel, out_shape=(jax.ShapeDtypeStruct((4 * CHIPS,...  2.2 us
    pallas_call x1, Pallas kernels, on_device(): pl.pallas_call(route_kernel, out_shape=packet_shape, in_specs=[VMEM, VMEM...  1.6 us
  transfers between devices with their start and end apart: 4, of which 1 were waited for; matrix products, arithmetic and copies ran while one was open for 0% of the time, Pallas kernels for 5%

profile of v8, /device:TPU:1, one launch (start us, length us, event | category | flops | bytes accessed | tf_op | source)
XLA Modules:
  0.0 71.4 jit_solution(2498371074233329604)
XLA Ops:
  0.0 0.0 copy-start.1
  0.0 0.0 copy-start
  0.0 0.0 copy-start.2
  0.0 0.0 copy-start.3
  0.0 0.7 copy-done.3
  0.7 3.5 %decimate.1.dec_ref = bf16[96,2048]{1,0:T(8,128)(2,1)S(1)} custom-call(bf16[96,16384]{1,0:T(8,128)(2,1)} %raw_hbm.1, bf16[1,127]{1,0:T(2,128)(2,1)S(1)} %bitcast.7), custom_call_target="tpu_custom_call" | custom-call | tf_op jit(solution)/shard_map/decimate/pallas_call | solution.py:214
  4.2 0.0 copy-done.1
  4.2 0.0 copy-done
  4.2 0.5 pick.1
  4.7 1.5 %collective-permute-start = (bf16[128,2048]{1,0:T(8,128)(2,1)S(1)}, bf16[128,2048]{1,0:T(8,128)(2,1)S(1)}, u32[]{:S(2)}, u32[]{:S(2)}) collective-permute-start(bf16[128,2048]{1,0:T(8,128)(2,1)S(1)} %get-tuple-element.12), channel_id=1, source_target_pairs={{0,4},{4,0},{1,5},{5,1},{2,6},{6,2},{3,7},{7,3},{8,12},{12,8},{9,1... | collective-permute-start | bytes 1572872 | tf_op jit(solution)/shard_map/ppermute | solution.py:204
  6.2 0.0 copy-done.2
  6.2 1.6 %route.1.packet_in = bf16[64,96,128]{2,1,0:T(8,128)(2,1)S(1)} custom-call(bf16[96,2048]{1,0:T(8,128)(2,1)S(1)} %decimate.1.dec_ref, s32[1,96]{1,0:T(1,128)S(1)} %bitcast.6), custom_call_target="tpu_custom_call" | custom-call | flops 100000000 | bytes 4000000 | tf_op jit(solution)/shard_map/route/pallas_call | solution.py:239
  7.8 0.0 collective-permute-done.got_ref
  7.8 1.1 %add_refs.1 = bf16[64,96,128]{2,1,0:T(8,128)(2,1)S(1)} custom-call(bf16[64,96,128]{2,1,0:T(8,128)(2,1)S(1)} %route.1.packet_in, bf16[128,2048]{1,0:T(8,128)(2,1)S(1)} %get-tuple-element.11.keep_ref, bf16[128,2048]{1,0:T(8,128)(2,1)S(1)} %collective-permute-done.got_ref), custom_call_target="tpu_custom_call", output_to_operand_aliasing={{}: (0, {})} | custom-call | tf_op jit(solution)/shard_map/add_refs/pallas_call | solution.py:249
  8.9 33.6 %all_to_all.10.arrived_ref = bf16[64,96,128]{2,1,0:T(8,128)(2,1)S(1)} all-to-all(bf16[64,96,128]{2,1,0:T(8,128)(2,1)S(1)} %add_refs.1), channel_id=1, replica_groups=mesh['x'=4,'z'=4,'core'=2,'chan'=4] {'x','z','chan'}, dimensions={0} | all-to-all | bytes 3145728 | tf_op jit(solution)/shard_map/all_to_all | solution.py:259
  42.5 0.9 %spread.1 = (bf16[64,32,128]{2,1,0:T(8,128)(2,1)}, bf16[64,32,128]{2,1,0:T(8,128)(2,1)S(1)}) custom-call(bf16[64,96,128]{2,1,0:T(8,128)(2,1)S(1)} %all_to_all.10.arrived_ref), custom_call_target="tpu_custom_call" | custom-call | tf_op jit(solution)/shard_map/spread/pallas_call | solution.py:260
  43.4 5.7 %all-to-all-start.1 = ((bf16[64,32,128]{2,1,0:T(8,128)(2,1)}), bf16[64,32,128]{2,1,0:T(8,128)(2,1)S(1)}, u32[]{:S(2)}, u32[]{:S(2)}) async-start(bf16[64,32,128]{2,1,0:T(8,128)(2,1)} %get-tuple-element.14), calls=%async_computation.1 | async-start | bytes 1048576 | tf_op jit(solution)/shard_map/all_to_all | solution.py:268
  49.2 1.7 %collective-permute-start.1 = (bf16[64,32,128]{2,1,0:T(8,128)(2,1)S(1)}, bf16[64,32,128]{2,1,0:T(8,128)(2,1)S(1)}, u32[]{:S(2)}, u32[]{:S(2)}) collective-permute-start(bf16[64,32,128]{2,1,0:T(8,128)(2,1)S(1)} %get-tuple-element.13), channel_id=1, source_target_pairs={{0,4},{4,0},{1,5},{5,1},{2,6},{6,2},{3,7},{7,3},{8,12},{12,8},{9,1... | collective-permute-start | bytes 1572872 | tf_op jit(solution)/shard_map/ppermute | solution.py:204
  50.9 9.2 %all-to-all-done.1.own_ref = bf16[64,32,128]{2,1,0:T(8,128)(2,1)S(1)} async-done(((bf16[64,32,128]{2,1,0:T(8,128)(2,1)}), bf16[64,32,128]{2,1,0:T(8,128)(2,1)S(1)}, u32[]{:S(2)}, u32[]{:S(2)}) %all-to-all-start.1) | async-done | bytes 524320 | tf_op jit(solution)/shard_map/all_to_all | solution.py:268
  60.1 3.1 %collective-permute-start.2 = (bf16[64,32,128]{2,1,0:T(8,128)(2,1)S(1)}, bf16[64,32,128]{2,1,0:T(8,128)(2,1)S(1)}, u32[]{:S(2)}, u32[]{:S(2)}) collective-permute-start(bf16[64,32,128]{2,1,0:T(8,128)(2,1)S(1)} %all-to-all-done.1.own_ref), channel_id=1, source_target_pairs={{0,4},{4,0},{1,5},{5,1},{2,6},{6,2},{3,7},{7,3},{8,12},{12,8},{9,1... | collective-permute-start | bytes 1572872 | tf_op jit(solution)/shard_map/ppermute | solution.py:204
  63.2 0.0 collective-permute-done.1.got_ref
  63.2 2.2 %widen.1 = (bf16[256,4096]{1,0:T(8,128)(2,1)S(1)}, bf16[128,2048]{1,0:T(8,128)(2,1)S(1)}) custom-call(bf16[64,96,128]{2,1,0:T(8,128)(2,1)S(1)} %all_to_all.10.arrived_ref, bf16[64,32,128]{2,1,0:T(8,128)(2,1)S(1)} %collective-permute-done.1.got_ref, bf16[64,32,128]{2,1,0:T(8,128)(2,1)S(1)} %all-to-all-done.1.own_ref), custom_call_target="tpu_custom_call" | custom-call | tf_op jit(solution)/shard_map/widen/pallas_call | solution.py:270
  65.4 0.0 collective-permute-done.2.other_ref
  65.4 5.8 %correlate.1 = f32[1,256,4096]{2,1,0:T(8,128)} custom-call(bf16[256,4096]{1,0:T(8,128)(2,1)S(1)} %get-tuple-element.15.ext_ref, bf16[128,2048]{1,0:T(8,128)(2,1)S(1)} %get-tuple-element.16.mine_ref, bf16[64,32,128]{2,1,0:T(8,128)(2,1)S(1)} %collective-permute-done.2.other_ref), custom_call_target="tpu_custom_call" | custom-call | tf_op jit(solution)/shard_map/correlate/pallas_call | solution.py:283
Async XLA Ops:
  0.0 4.2 %copy-start.1 = (s32[256]{0:T(256)S(1)}, s32[256]{0:T(256)}, u32[]{:S(2)}) copy-start(s32[256]{0:T(256)} %param.8) | copy-start | bytes 3076
  0.0 4.2 %copy-start = (s32[12288]{0:T(1024)S(1)}, s32[12288]{0:T(1024)}, u32[]{:S(2)}) copy-start(s32[12288]{0:T(1024)} %param.7) | copy-start | bytes 147460
  0.0 6.2 %copy-start.2 = (s32[96,1]{0,1:T(1,128)S(1)}, s32[96,1]{0,1:T(1,128)}, u32[]{:S(2)}) copy-start(s32[96,1]{0,1:T(1,128)} %param.9) | copy-start | bytes 1156
  0.0 0.7 copy-start.3
  4.7 3.1 %collective-permute-start = (bf16[128,2048]{1,0:T(8,128)(2,1)S(1)}, bf16[128,2048]{1,0:T(8,128)(2,1)S(1)}, u32[]{:S(2)}, u32[]{:S(2)}) collective-permute-start(bf16[128,2048]{1,0:T(8,128)(2,1)S(1)} %get-tuple-element.12), channel_id=1, source_target_pairs={{0,4},{4,0},{1,5},{5,1},{2,6},{6,2},{3,7},{7,3},{8,12},{12,8},{9,1... | collective-permute-start | bytes 1572872 | tf_op jit(solution)/shard_map/ppermute | solution.py:204
  43.4 16.7 %all-to-all-start.1 = ((bf16[64,32,128]{2,1,0:T(8,128)(2,1)}), bf16[64,32,128]{2,1,0:T(8,128)(2,1)S(1)}, u32[]{:S(2)}, u32[]{:S(2)}) async-start(bf16[64,32,128]{2,1,0:T(8,128)(2,1)} %get-tuple-element.14), calls=%async_computation.1 | async-start | bytes 1048576 | tf_op jit(solution)/shard_map/all_to_all | solution.py:268
  49.2 14.1 %collective-permute-start.1 = (bf16[64,32,128]{2,1,0:T(8,128)(2,1)S(1)}, bf16[64,32,128]{2,1,0:T(8,128)(2,1)S(1)}, u32[]{:S(2)}, u32[]{:S(2)}) collective-permute-start(bf16[64,32,128]{2,1,0:T(8,128)(2,1)S(1)} %get-tuple-element.13), channel_id=1, source_target_pairs={{0,4},{4,0},{1,5},{5,1},{2,6},{6,2},{3,7},{7,3},{8,12},{12,8},{9,1... | collective-permute-start | bytes 1572872 | tf_op jit(solution)/shard_map/ppermute | solution.py:204
  60.1 5.3 %collective-permute-start.2 = (bf16[64,32,128]{2,1,0:T(8,128)(2,1)S(1)}, bf16[64,32,128]{2,1,0:T(8,128)(2,1)S(1)}, u32[]{:S(2)}, u32[]{:S(2)}) collective-permute-start(bf16[64,32,128]{2,1,0:T(8,128)(2,1)S(1)} %all-to-all-done.1.own_ref), channel_id=1, source_target_pairs={{0,4},{4,0},{1,5},{5,1},{2,6},{6,2},{3,7},{7,3},{8,12},{12,8},{9,1... | collective-permute-start | bytes 1572872 | tf_op jit(solution)/shard_map/ppermute | solution.py:204

commit v9 on v8

--- a/solution.py
+++ b/solution.py
@@ -16,6 +16,7 @@
 BLOCK = 128
 HALO = 128
 CHIPS = 64
+PAD = 8
 LAG_STEPS = (3, 5, 4, 2, 2)
 AXES = ("x", "z", "core", "chan")
 SAME = ("x", "z", "chan")
@@ -116,10 +117,12 @@
         picked = jnp.dot(select, dec_ref[:, b * LANES : (b + 2) * LANES], preferred_element_type=F32)
         for g in range(4):
             for h in range(2):
-                stage[pl.ds(g * LAGS + b + h, CHIPS, stride=4 * LAGS), :] = picked[
+                stage[pl.ds(g * LAGS + b + h, CHIPS, stride=4 * LAGS + PAD), :] = picked[
                     g * CHIPS : (g + 1) * CHIPS, h * LANES : (h + 1) * LANES
                 ]
-    packet_ref[:, : 4 * LAGS, :] = stage[...].astype(BF16).reshape(CHIPS, 4 * LAGS, LANES)
+    for g in range(CHIPS):
+        at = g * (4 * LAGS + PAD)
+        packet_ref[g, : 4 * LAGS, :] = stage[at : at + 4 * LAGS, :].astype(BF16)
 
 
 def add_refs_kernel(packet_in, keep_ref, got_ref, packet_ref, stage):
@@ -128,10 +131,12 @@
         rows = slice(s * CHIPS, (s + 1) * CHIPS)
         for b in range(LAGS):
             lanes = slice(b * LANES, (b + 1) * LANES)
-            stage[pl.ds(s * LAGS + b, CHIPS, stride=2 * LAGS), :] = keep_ref[rows, lanes].astype(F32) + got_ref[
+            stage[pl.ds(s * LAGS + b, CHIPS, stride=2 * LAGS + PAD), :] = keep_ref[rows, lanes].astype(F32) + got_ref[
                 rows, lanes
             ].astype(F32)
-    packet_ref[:, 4 * LAGS :, :] = stage[...].astype(BF16).reshape(CHIPS, 2 * LAGS, LANES)
+    for g in range(CHIPS):
+        at = g * (2 * LAGS + PAD)
+        packet_ref[g, 4 * LAGS :, :] = stage[at : at + 2 * LAGS, :].astype(BF16)
 
 
 def spread_kernel(arrived_ref, spread_ref, give_ref):
@@ -143,22 +148,26 @@
 
 
 def lay_out_refs(refs_ref, wide, write):
-    wide[...] = refs_ref[...].astype(F32).reshape(wide.shape)
+    for g in range(CHIPS):
+        at = g * (2 * LAGS + PAD)
+        wide[at : at + 2 * LAGS, :] = refs_ref[g].astype(F32)
     for s in range(2):
         for b in range(LAGS):
-            write(s * CHIPS, b * LANES, wide[pl.ds(s * LAGS + b, CHIPS, stride=2 * LAGS), :].astype(BF16))
+            write(s * CHIPS, b * LANES, wide[pl.ds(s * LAGS + b, CHIPS, stride=2 * LAGS + PAD), :].astype(BF16))
 
 
 def widen_kernel(arrived_ref, got_ref, own_ref, ext_ref, mine_ref, wide, wide_refs):
     core = lax.axis_index("core")
-    size = CHIPS * 2 * LAGS
     mine = pl.multiple_of(core * 2 * LAGS, 2 * LAGS)
-    wide[core] = arrived_ref[:, pl.ds(mine, 2 * LAGS), :].astype(F32).reshape(size, LANES)
-    wide[1 - core] = got_ref[...].astype(F32).reshape(size, LANES)
+    for g in range(CHIPS):
+        for slot in range(2):
+            at = (2 * g + slot) * (LAGS + PAD)
+            wide[core, at : at + LAGS, :] = arrived_ref[g, pl.ds(mine + slot * LAGS, LAGS), :].astype(F32)
+            wide[1 - core, at : at + LAGS, :] = got_ref[g, slot * LAGS : (slot + 1) * LAGS, :].astype(F32)
     total = LAGS * LANES
     lane = iota((4 * CHIPS, LANES), 1)
     for b in range(LAGS):
-        halves = [wide[c, pl.ds(b, 2 * CHIPS, stride=LAGS), :].reshape(CHIPS // 4, 1, 8, LANES) for c in range(2)]
+        halves = [wide[c, pl.ds(b, 2 * CHIPS, stride=LAGS + PAD), :].reshape(CHIPS // 4, 1, 8, LANES) for c in range(2)]
         plane = jnp.concatenate(halves, axis=1).reshape(4 * CHIPS, LANES)
         ext_ref[:, b * LANES : (b + 1) * LANES] = plane.astype(BF16)
         moved = jnp.where(
@@ -241,7 +250,7 @@
         out_shape=packet_shape,
         in_specs=[VMEM, VMEM],
         out_specs=VMEM,
-        scratch_shapes=[pltpu.VMEM((CHIPS * 4 * LAGS, LANES), F32)],
+        scratch_shapes=[pltpu.VMEM((CHIPS * (4 * LAGS + PAD), LANES), F32)],
         compiler_params=params(),
         cost_estimate=pl.CostEstimate(flops=100_000_000, bytes_accessed=4_000_000, transcendentals=0),
         name="route",
@@ -251,7 +260,7 @@
         out_shape=packet_shape,
         in_specs=[VMEM] * 3,
         out_specs=VMEM,
-        scratch_shapes=[pltpu.VMEM((CHIPS * 2 * LAGS, LANES), F32)],
+        scratch_shapes=[pltpu.VMEM((CHIPS * (2 * LAGS + PAD), LANES), F32)],
         input_output_aliases={0: 0},
         compiler_params=params(),
         name="add_refs",
@@ -273,8 +282,8 @@
         in_specs=[VMEM, VMEM, VMEM],
         out_specs=(VMEM, VMEM),
         scratch_shapes=[
-            pltpu.VMEM((2, CHIPS * 2 * LAGS, LANES), F32),
-            pltpu.VMEM((CHIPS * 2 * LAGS, LANES), F32),
+            pltpu.VMEM((2, CHIPS * 2 * (LAGS + PAD), LANES), F32),
+            pltpu.VMEM((CHIPS * (2 * LAGS + PAD), LANES), F32),
         ],
         compiler_params=params(),
         name="widen",
@@ -286,7 +295,7 @@
         in_specs=[VMEM, VMEM, VMEM],
         out_specs=HBM,
         scratch_shapes=[
-            pltpu.VMEM((CHIPS * 2 * LAGS, LANES), F32),
+            pltpu.VMEM((CHIPS * (2 * LAGS + PAD), LANES), F32),
             pltpu.VMEM((NREF, total), BF16),
             pltpu.VMEM((4 * CHIPS, LAGS * NREF), F32),
             pltpu.SemaphoreType.DMA((len(LAG_STEPS),)),

time: 71.7 us -> 69.8 us (0.974)
  Pallas kernels: 15.6 us -> 12.9 us
  waiting for transfers between devices: 9.23 us -> 10.1 us
    ppermute x3, waiting for transfers between devices: 0.01 us -> 1.06 us  [swap_cores(): return lax.ppermute(x, 'core', [(0, 1), (1, 0)])]
    pallas_call x1, Pallas kernels: 2.2 us -> 1.28 us  [on_device(): pl.pallas_call(widen_kernel, out_shape=(jax.ShapeDtypeStruct((4 * CHIPS,...]
    pallas_call x1, Pallas kernels: 1.6 us -> 0.72 us  [on_device(): pl.pallas_call(route_kernel, out_shape=packet_shape, in_specs=[VMEM, VMEM...]
    pallas_call x1, Pallas kernels: 1.1 us -> 0.3 us  [on_device(): pl.pallas_call(add_refs_kernel, out_shape=packet_shape, in_specs=[VMEM] *...]
  transfers between devices with their start and end apart: 4 -> 4, of which waited for: 1 -> 3; matrix products, arithmetic and copies ran while one was open for 0% -> 0% of each run, Pallas kernels for 5% -> 3%
where the time goes in v9:
time: 69.8 us; the launch traced here: 69.5 us
  blocking collectives  33.4 us (48%)
  Pallas kernels  12.9 us (18%)
  starting transfers between devices  12.3 us (18%)
  waiting for transfers between devices  10.1 us (14%)
    all_to_all x1, blocking collectives, on_device(): arrived = lax.all_to_all(packet, SAME, 0, 0, tiled=True)  33.4 us
    all_to_all x1, waiting for transfers between devices, on_device(): refs_own = lax.all_to_all(spread, SAME, 0, 0, tiled=True)  9.09 us
    ppermute x3, starting transfers between devices, swap_cores(): return lax.ppermute(x, 'core', [(0, 1), (1, 0)])  6.45 us
    all_to_all x1, starting transfers between devices, on_device(): refs_own = lax.all_to_all(spread, SAME, 0, 0, tiled=True)  5.81 us
    pallas_call x1, Pallas kernels, on_device(): pl.pallas_call(correlate_kernel, out_shape=jax.ShapeDtypeStruct((1, 4 * C...  5.67 us
    pallas_call x1, Pallas kernels, on_device(): pl.pallas_call(decimate_kernel, out_shape=jax.ShapeDtypeStruct((rows_dev,...  3.48 us
  transfers between devices with their start and end apart: 4, of which 3 were waited for; matrix products, arithmetic and copies ran while one was open for 0% of the time, Pallas kernels for 3%

profile of v9, /device:TPU:1, one launch (start us, length us, event | category | flops | bytes accessed | tf_op | source)
XLA Modules:
  0.0 69.5 jit_solution(2674201827173564643)
XLA Ops:
  0.0 0.0 copy-start.1
  0.0 0.0 copy-start
  0.0 0.0 copy-start.2
  0.0 0.0 copy-start.3
  0.0 0.7 copy-done.3
  0.7 3.5 %decimate.1.dec_ref = bf16[96,2048]{1,0:T(8,128)(2,1)S(1)} custom-call(bf16[96,16384]{1,0:T(8,128)(2,1)} %raw_hbm.1, bf16[1,127]{1,0:T(2,128)(2,1)S(1)} %bitcast.7), custom_call_target="tpu_custom_call" | custom-call | tf_op jit(solution)/shard_map/decimate/pallas_call | solution.py:223
  4.2 0.0 copy-done.1
  4.2 0.0 copy-done
  4.2 0.5 pick.1
  4.7 1.5 %collective-permute-start = (bf16[128,2048]{1,0:T(8,128)(2,1)S(1)}, bf16[128,2048]{1,0:T(8,128)(2,1)S(1)}, u32[]{:S(2)}, u32[]{:S(2)}) collective-permute-start(bf16[128,2048]{1,0:T(8,128)(2,1)S(1)} %get-tuple-element.12), channel_id=1, source_target_pairs={{0,4},{4,0},{1,5},{5,1},{2,6},{6,2},{3,7},{7,3},{8,12},{12,8},{9,1... | collective-permute-start | bytes 1572872 | tf_op jit(solution)/shard_map/ppermute | solution.py:213
  6.2 0.0 copy-done.2
  6.2 0.7 %route.1.packet_in = bf16[64,96,128]{2,1,0:T(8,128)(2,1)S(1)} custom-call(bf16[96,2048]{1,0:T(8,128)(2,1)S(1)} %decimate.1.dec_ref, s32[1,96]{1,0:T(1,128)S(1)} %bitcast.6), custom_call_target="tpu_custom_call" | custom-call | flops 100000000 | bytes 4000000 | tf_op jit(solution)/shard_map/route/pallas_call | solution.py:248
  6.9 0.8 %collective-permute-done.got_ref = bf16[128,2048]{1,0:T(8,128)(2,1)S(1)} collective-permute-done((bf16[128,2048]{1,0:T(8,128)(2,1)S(1)}, bf16[128,2048]{1,0:T(8,128)(2,1)S(1)}, u32[]{:S(2)}, u32[]{:S(2)}) %collective-permute-start) | collective-permute-done | bytes 524320 | tf_op jit(solution)/shard_map/ppermute | solution.py:213
  7.7 0.3 add_refs.1
  8.0 33.4 %all_to_all.10.arrived_ref = bf16[64,96,128]{2,1,0:T(8,128)(2,1)S(1)} all-to-all(bf16[64,96,128]{2,1,0:T(8,128)(2,1)S(1)} %add_refs.1), channel_id=1, replica_groups=mesh['x'=4,'z'=4,'core'=2,'chan'=4] {'x','z','chan'}, dimensions={0} | all-to-all | bytes 3145728 | tf_op jit(solution)/shard_map/all_to_all | solution.py:268
  41.5 0.9 %spread.1 = (bf16[64,32,128]{2,1,0:T(8,128)(2,1)}, bf16[64,32,128]{2,1,0:T(8,128)(2,1)S(1)}) custom-call(bf16[64,96,128]{2,1,0:T(8,128)(2,1)S(1)} %all_to_all.10.arrived_ref), custom_call_target="tpu_custom_call" | custom-call | tf_op jit(solution)/shard_map/spread/pallas_call | solution.py:269
  42.4 5.8 %all-to-all-start.1 = ((bf16[64,32,128]{2,1,0:T(8,128)(2,1)}), bf16[64,32,128]{2,1,0:T(8,128)(2,1)S(1)}, u32[]{:S(2)}, u32[]{:S(2)}) async-start(bf16[64,32,128]{2,1,0:T(8,128)(2,1)} %get-tuple-element.14), calls=%async_computation.1 | async-start | bytes 1048576 | tf_op jit(solution)/shard_map/all_to_all | solution.py:277
  48.2 1.8 %collective-permute-start.1 = (bf16[64,32,128]{2,1,0:T(8,128)(2,1)S(1)}, bf16[64,32,128]{2,1,0:T(8,128)(2,1)S(1)}, u32[]{:S(2)}, u32[]{:S(2)}) collective-permute-start(bf16[64,32,128]{2,1,0:T(8,128)(2,1)S(1)} %get-tuple-element.13), channel_id=1, source_target_pairs={{0,4},{4,0},{1,5},{5,1},{2,6},{6,2},{3,7},{7,3},{8,12},{12,8},{9,1... | collective-permute-start | bytes 1572872 | tf_op jit(solution)/shard_map/ppermute | solution.py:213
  50.0 9.1 %all-to-all-done.1.own_ref = bf16[64,32,128]{2,1,0:T(8,128)(2,1)S(1)} async-done(((bf16[64,32,128]{2,1,0:T(8,128)(2,1)}), bf16[64,32,128]{2,1,0:T(8,128)(2,1)S(1)}, u32[]{:S(2)}, u32[]{:S(2)}) %all-to-all-start.1) | async-done | bytes 524320 | tf_op jit(solution)/shard_map/all_to_all | solution.py:277
  59.1 3.2 %collective-permute-start.2 = (bf16[64,32,128]{2,1,0:T(8,128)(2,1)S(1)}, bf16[64,32,128]{2,1,0:T(8,128)(2,1)S(1)}, u32[]{:S(2)}, u32[]{:S(2)}) collective-permute-start(bf16[64,32,128]{2,1,0:T(8,128)(2,1)S(1)} %all-to-all-done.1.own_ref), channel_id=1, source_target_pairs={{0,4},{4,0},{1,5},{5,1},{2,6},{6,2},{3,7},{7,3},{8,12},{12,8},{9,1... | collective-permute-start | bytes 1572872 | tf_op jit(solution)/shard_map/ppermute | solution.py:213
  62.3 0.0 collective-permute-done.1.got_ref
  62.3 1.3 %widen.1 = (bf16[256,4096]{1,0:T(8,128)(2,1)S(1)}, bf16[128,2048]{1,0:T(8,128)(2,1)S(1)}) custom-call(bf16[64,96,128]{2,1,0:T(8,128)(2,1)S(1)} %all_to_all.10.arrived_ref, bf16[64,32,128]{2,1,0:T(8,128)(2,1)S(1)} %collective-permute-done.1.got_ref, bf16[64,32,128]{2,1,0:T(8,128)(2,1)S(1)} %all-to-all-done.1.own_ref), custom_call_target="tpu_custom_call" | custom-call | tf_op jit(solution)/shard_map/widen/pallas_call | solution.py:279
  63.6 0.2 collective-permute-done.2.other_ref
  63.8 5.7 %correlate.1 = f32[1,256,4096]{2,1,0:T(8,128)} custom-call(bf16[256,4096]{1,0:T(8,128)(2,1)S(1)} %get-tuple-element.15.ext_ref, bf16[128,2048]{1,0:T(8,128)(2,1)S(1)} %get-tuple-element.16.mine_ref, bf16[64,32,128]{2,1,0:T(8,128)(2,1)S(1)} %collective-permute-done.2.other_ref), custom_call_target="tpu_custom_call" | custom-call | tf_op jit(solution)/shard_map/correlate/pallas_call | solution.py:292
Async XLA Ops:
  0.0 4.2 %copy-start.1 = (s32[256]{0:T(256)S(1)}, s32[256]{0:T(256)}, u32[]{:S(2)}) copy-start(s32[256]{0:T(256)} %param.8) | copy-start | bytes 3076
  0.0 4.2 %copy-start = (s32[12288]{0:T(1024)S(1)}, s32[12288]{0:T(1024)}, u32[]{:S(2)}) copy-start(s32[12288]{0:T(1024)} %param.7) | copy-start | bytes 147460
  0.0 6.2 %copy-start.2 = (s32[96,1]{0,1:T(1,128)S(1)}, s32[96,1]{0,1:T(1,128)}, u32[]{:S(2)}) copy-start(s32[96,1]{0,1:T(1,128)} %param.9) | copy-start | bytes 1156
  0.0 0.7 copy-start.3
  4.7 3.0 %collective-permute-start = (bf16[128,2048]{1,0:T(8,128)(2,1)S(1)}, bf16[128,2048]{1,0:T(8,128)(2,1)S(1)}, u32[]{:S(2)}, u32[]{:S(2)}) collective-permute-start(bf16[128,2048]{1,0:T(8,128)(2,1)S(1)} %get-tuple-element.12), channel_id=1, source_target_pairs={{0,4},{4,0},{1,5},{5,1},{2,6},{6,2},{3,7},{7,3},{8,12},{12,8},{9,1... | collective-permute-start | bytes 1572872 | tf_op jit(solution)/shard_map/ppermute | solution.py:213
  42.4 16.7 %all-to-all-start.1 = ((bf16[64,32,128]{2,1,0:T(8,128)(2,1)}), bf16[64,32,128]{2,1,0:T(8,128)(2,1)S(1)}, u32[]{:S(2)}, u32[]{:S(2)}) async-start(bf16[64,32,128]{2,1,0:T(8,128)(2,1)} %get-tuple-element.14), calls=%async_computation.1 | async-start | bytes 1048576 | tf_op jit(solution)/shard_map/all_to_all | solution.py:277
  48.2 14.1 %collective-permute-start.1 = (bf16[64,32,128]{2,1,0:T(8,128)(2,1)S(1)}, bf16[64,32,128]{2,1,0:T(8,128)(2,1)S(1)}, u32[]{:S(2)}, u32[]{:S(2)}) collective-permute-start(bf16[64,32,128]{2,1,0:T(8,128)(2,1)S(1)} %get-tuple-element.13), channel_id=1, source_target_pairs={{0,4},{4,0},{1,5},{5,1},{2,6},{6,2},{3,7},{7,3},{8,12},{12,8},{9,1... | collective-permute-start | bytes 1572872 | tf_op jit(solution)/shard_map/ppermute | solution.py:213
  59.1 4.7 %collective-permute-start.2 = (bf16[64,32,128]{2,1,0:T(8,128)(2,1)S(1)}, bf16[64,32,128]{2,1,0:T(8,128)(2,1)S(1)}, u32[]{:S(2)}, u32[]{:S(2)}) collective-permute-start(bf16[64,32,128]{2,1,0:T(8,128)(2,1)S(1)} %all-to-all-done.1.own_ref), channel_id=1, source_target_pairs={{0,4},{4,0},{1,5},{5,1},{2,6},{6,2},{3,7},{7,3},{8,12},{12,8},{9,1... | collective-permute-start | bytes 1572872 | tf_op jit(solution)/shard_map/ppermute | solution.py:213

commit v10 on v9

--- a/solution.py
+++ b/solution.py
@@ -75,29 +75,22 @@
             dec_ref[r : r + 16, b * LANES : (b + 1) * LANES] = pieces[b]
 
 
-def pick_kernel(dec_ref, ids, refch, keep_ref, give_ref):
-    rows = dec_ref.shape[0]
-    count = keep_ref.shape[0]
+def find_kernel(ids, refch, select_ref):
+    count, rows = select_ref.shape[1:]
     core = lax.axis_index("core")
     own = lax.axis_index(AXES)
-    at = own * rows
-    line0 = at // LANES
-    line1 = jnp.minimum(line0 + 1, ids.shape[0] - 1)
-    turn = LANES - (at - line0 * LANES)
-    pair = [
-        pltpu.roll(jnp.broadcast_to(ids[pl.ds(i, 1), :], (8, LANES)), turn, 1) for i in (line0, line1)
-    ]
-    mine = jnp.where(iota((8, LANES), 1) < turn, pair[0], pair[1])[0:1, :rows]
     refcol = jnp.transpose(jnp.broadcast_to(refch[...], (LANES, NREF)))[:, :rows]
-    select = jnp.where(refcol == mine, 1.0, 0.0)
-    halves = (select[:count], select[count:])
-    halves = (jnp.where(core == 0, *halves), jnp.where(core == 0, *halves[::-1]))
-    select = jnp.concatenate(halves, axis=0).astype(BF16)
-    for b in range(0, LAGS, 2):
-        span = slice(b * LANES, (b + 2) * LANES)
-        picked = jnp.dot(select, dec_ref[:, span], preferred_element_type=F32).astype(BF16)
-        keep_ref[:, span] = picked[:count]
-        give_ref[:, span] = picked[count:]
+    refcol = jnp.where(core == 0, refcol[:count], refcol[count:])
+    for i, device in enumerate((own, own + 4 - 8 * core)):
+        at = device * rows
+        line0 = at // LANES
+        line1 = jnp.minimum(line0 + 1, ids.shape[0] - 1)
+        turn = LANES - (at - line0 * LANES)
+        pair = [
+            pltpu.roll(jnp.broadcast_to(ids[pl.ds(k, 1), :], (8, LANES)), turn, 1) for k in (line0, line1)
+        ]
+        there = jnp.where(iota((8, LANES), 1) < turn, pair[0], pair[1])[0:1, :rows]
+        select_ref[i] = jnp.where(refcol == there, 1.0, 0.0).astype(BF16)
 
 
 def route_kernel(dec_ref, owner_ref, packet_ref, stage):
@@ -125,15 +118,17 @@
         packet_ref[g, : 4 * LAGS, :] = stage[at : at + 4 * LAGS, :].astype(BF16)
 
 
-def add_refs_kernel(packet_in, keep_ref, got_ref, packet_ref, stage):
+def add_refs_kernel(packet_in, select_ref, dec_ref, got_ref, packet_ref, stage):
     del packet_in
-    for s in range(2):
-        rows = slice(s * CHIPS, (s + 1) * CHIPS)
-        for b in range(LAGS):
-            lanes = slice(b * LANES, (b + 1) * LANES)
-            stage[pl.ds(s * LAGS + b, CHIPS, stride=2 * LAGS + PAD), :] = keep_ref[rows, lanes].astype(F32) + got_ref[
-                rows, lanes
-            ].astype(F32)
+    for b in range(0, LAGS, 2):
+        span = slice(b * LANES, (b + 2) * LANES)
+        picked = jnp.dot(select_ref[0], dec_ref[:, span], preferred_element_type=F32)
+        picked = picked + jnp.dot(select_ref[1], got_ref[:, span], preferred_element_type=F32)
+        for s in range(2):
+            for h in range(2):
+                stage[pl.ds(s * LAGS + b + h, CHIPS, stride=2 * LAGS + PAD), :] = picked[
+                    s * CHIPS : (s + 1) * CHIPS, h * LANES : (h + 1) * LANES
+                ]
     for g in range(CHIPS):
         at = g * (2 * LAGS + PAD)
         packet_ref[g, 4 * LAGS :, :] = stage[at : at + 2 * LAGS, :].astype(BF16)
@@ -235,15 +230,15 @@
         compiler_params=params(52),
         name="decimate",
     )(raw, taps.reshape(1, TAPS))
-    keep, give = pl.pallas_call(
-        pick_kernel,
-        out_shape=(plain, plain),
-        in_specs=[VMEM] * 3,
-        out_specs=(VMEM, VMEM),
-        compiler_params=params(),
-        name="pick",
-    )(dec, ids, ref_channel.reshape(1, NREF))
-    got = swap_cores(give)
+    got = swap_cores(dec)
+    select = pl.pallas_call(
+        find_kernel,
+        out_shape=jax.ShapeDtypeStruct((2, NREF // 2, rows_dev), BF16),
+        in_specs=[VMEM] * 2,
+        out_specs=VMEM,
+        compiler_params=params(),
+        name="find",
+    )(ids, ref_channel.reshape(1, NREF))
     packet_shape = jax.ShapeDtypeStruct((CHIPS, 6 * LAGS, LANES), BF16)
     packet = pl.pallas_call(
         route_kernel,
@@ -258,13 +253,13 @@
     packet = pl.pallas_call(
         add_refs_kernel,
         out_shape=packet_shape,
-        in_specs=[VMEM] * 3,
+        in_specs=[VMEM] * 4,
         out_specs=VMEM,
         scratch_shapes=[pltpu.VMEM((CHIPS * (2 * LAGS + PAD), LANES), F32)],
         input_output_aliases={0: 0},
         compiler_params=params(),
         name="add_refs",
-    )(packet, keep, got)
+    )(packet, select, dec, got)
     arrived = lax.all_to_all(packet, SAME, 0, 0, tiled=True)
     spread, rows_give = pl.pallas_call(
         spread_kernel,

time: 69.8 us -> 69.2 us (level)
  no operation moved by 1% of the time
where the time goes in v10:
time: 69.2 us; the launch traced here: 68.9 us
  blocking collectives  33.4 us (48%)
  Pallas kernels  12.7 us (18%)
  starting transfers between devices  12.3 us (18%)
  waiting for transfers between devices  9.78 us (14%)
    all_to_all x1, blocking collectives, on_device(): arrived = lax.all_to_all(packet, SAME, 0, 0, tiled=True)  33.4 us
    all_to_all x1, waiting for transfers between devices, on_device(): refs_own = lax.all_to_all(spread, SAME, 0, 0, tiled=True)  9.09 us
    ppermute x3, starting transfers between devices, swap_cores(): return lax.ppermute(x, 'core', [(0, 1), (1, 0)])  6.45 us
    all_to_all x1, starting transfers between devices, on_device(): refs_own = lax.all_to_all(spread, SAME, 0, 0, tiled=True)  5.81 us
    pallas_call x1, Pallas kernels, on_device(): pl.pallas_call(correlate_kernel, out_shape=jax.ShapeDtypeStruct((1, 4 * C...  5.67 us
    pallas_call x1, Pallas kernels, on_device(): pl.pallas_call(decimate_kernel, out_shape=jax.ShapeDtypeStruct((rows_dev,...  3.48 us
  transfers between devices with their start and end apart: 4, of which 3 were waited for; matrix products, arithmetic and copies ran while one was open for 0% of the time, Pallas kernels for 3%

profile of v10, /device:TPU:1, one launch (start us, length us, event | category | flops | bytes accessed | tf_op | source)
XLA Modules:
  0.0 68.9 jit_solution(372252567744991540)
XLA Ops:
  0.0 0.0 copy-start.1
  0.0 0.0 copy-start
  0.0 0.0 copy-start.2
  0.0 0.0 copy-start.3
  0.0 0.7 copy-done.3
  0.7 3.5 %decimate.1.dec_ref = bf16[96,2048]{1,0:T(8,128)(2,1)S(1)} custom-call(bf16[96,16384]{1,0:T(8,128)(2,1)} %raw_hbm.1, bf16[1,127]{1,0:T(2,128)(2,1)S(1)} %bitcast.7), custom_call_target="tpu_custom_call" | custom-call | tf_op jit(solution)/shard_map/decimate/pallas_call | solution.py:218
  4.2 1.5 %collective-permute-start = (bf16[96,2048]{1,0:T(8,128)(2,1)S(1)}, bf16[96,2048]{1,0:T(8,128)(2,1)S(1)}, u32[]{:S(2)}, u32[]{:S(2)}) collective-permute-start(bf16[96,2048]{1,0:T(8,128)(2,1)S(1)} %decimate.1.dec_ref), channel_id=1, source_target_pairs={{0,4},{4,0},{1,5},{5,1},{2,6},{6,2},{3,7},{7,3},{8,12},{12,8},{9,1... | collective-permute-start | bytes 1179656 | tf_op jit(solution)/shard_map/ppermute | solution.py:208
  5.7 0.0 copy-done.1
  5.7 0.0 copy-done
  5.7 0.2 find.1.select_ref
  5.8 0.0 copy-done.2
  5.8 0.7 %route.1.packet_in = bf16[64,96,128]{2,1,0:T(8,128)(2,1)S(1)} custom-call(bf16[96,2048]{1,0:T(8,128)(2,1)S(1)} %decimate.1.dec_ref, s32[1,96]{1,0:T(1,128)S(1)} %bitcast.6), custom_call_target="tpu_custom_call" | custom-call | flops 100000000 | bytes 4000000 | tf_op jit(solution)/shard_map/route/pallas_call | solution.py:243
  6.6 0.4 collective-permute-done.got_ref
  7.0 0.5 add_refs.1
  7.5 33.4 %all_to_all.10.arrived_ref = bf16[64,96,128]{2,1,0:T(8,128)(2,1)S(1)} all-to-all(bf16[64,96,128]{2,1,0:T(8,128)(2,1)S(1)} %add_refs.1), channel_id=1, replica_groups=mesh['x'=4,'z'=4,'core'=2,'chan'=4] {'x','z','chan'}, dimensions={0} | all-to-all | bytes 3145728 | tf_op jit(solution)/shard_map/all_to_all | solution.py:263
  40.9 0.9 %spread.1 = (bf16[64,32,128]{2,1,0:T(8,128)(2,1)}, bf16[64,32,128]{2,1,0:T(8,128)(2,1)S(1)}) custom-call(bf16[64,96,128]{2,1,0:T(8,128)(2,1)S(1)} %all_to_all.10.arrived_ref), custom_call_target="tpu_custom_call" | custom-call | tf_op jit(solution)/shard_map/spread/pallas_call | solution.py:264
  41.8 5.8 %all-to-all-start.1 = ((bf16[64,32,128]{2,1,0:T(8,128)(2,1)}), bf16[64,32,128]{2,1,0:T(8,128)(2,1)S(1)}, u32[]{:S(2)}, u32[]{:S(2)}) async-start(bf16[64,32,128]{2,1,0:T(8,128)(2,1)} %get-tuple-element.10), calls=%async_computation.1 | async-start | bytes 1048576 | tf_op jit(solution)/shard_map/all_to_all | solution.py:272
  47.7 1.8 %collective-permute-start.1 = (bf16[64,32,128]{2,1,0:T(8,128)(2,1)S(1)}, bf16[64,32,128]{2,1,0:T(8,128)(2,1)S(1)}, u32[]{:S(2)}, u32[]{:S(2)}) collective-permute-start(bf16[64,32,128]{2,1,0:T(8,128)(2,1)S(1)} %get-tuple-element.9), channel_id=1, source_target_pairs={{0,4},{4,0},{1,5},{5,1},{2,6},{6,2},{3,7},{7,3},{8,12},{12,8},{9,1... | collective-permute-start | bytes 1572872 | tf_op jit(solution)/shard_map/ppermute | solution.py:208
  49.5 9.1 %all-to-all-done.1.own_ref = bf16[64,32,128]{2,1,0:T(8,128)(2,1)S(1)} async-done(((bf16[64,32,128]{2,1,0:T(8,128)(2,1)}), bf16[64,32,128]{2,1,0:T(8,128)(2,1)S(1)}, u32[]{:S(2)}, u32[]{:S(2)}) %all-to-all-start.1) | async-done | bytes 524320 | tf_op jit(solution)/shard_map/all_to_all | solution.py:272
  58.6 3.2 %collective-permute-start.2 = (bf16[64,32,128]{2,1,0:T(8,128)(2,1)S(1)}, bf16[64,32,128]{2,1,0:T(8,128)(2,1)S(1)}, u32[]{:S(2)}, u32[]{:S(2)}) collective-permute-start(bf16[64,32,128]{2,1,0:T(8,128)(2,1)S(1)} %all-to-all-done.1.own_ref), channel_id=1, source_target_pairs={{0,4},{4,0},{1,5},{5,1},{2,6},{6,2},{3,7},{7,3},{8,12},{12,8},{9,1... | collective-permute-start | bytes 1572872 | tf_op jit(solution)/shard_map/ppermute | solution.py:208
  61.7 0.0 collective-permute-done.1.got_ref
  61.7 1.3 %widen.1 = (bf16[256,4096]{1,0:T(8,128)(2,1)S(1)}, bf16[128,2048]{1,0:T(8,128)(2,1)S(1)}) custom-call(bf16[64,96,128]{2,1,0:T(8,128)(2,1)S(1)} %all_to_all.10.arrived_ref, bf16[64,32,128]{2,1,0:T(8,128)(2,1)S(1)} %collective-permute-done.1.got_ref, bf16[64,32,128]{2,1,0:T(8,128)(2,1)S(1)} %all-to-all-done.1.own_ref), custom_call_target="tpu_custom_call" | custom-call | tf_op jit(solution)/shard_map/widen/pallas_call | solution.py:274
  63.0 0.2 collective-permute-done.2.other_ref
  63.2 5.7 %correlate.1 = f32[1,256,4096]{2,1,0:T(8,128)} custom-call(bf16[256,4096]{1,0:T(8,128)(2,1)S(1)} %get-tuple-element.11.ext_ref, bf16[128,2048]{1,0:T(8,128)(2,1)S(1)} %get-tuple-element.12.mine_ref, bf16[64,32,128]{2,1,0:T(8,128)(2,1)S(1)} %collective-permute-done.2.other_ref), custom_call_target="tpu_custom_call" | custom-call | tf_op jit(solution)/shard_map/correlate/pallas_call | solution.py:287
Async XLA Ops:
  0.0 5.7 %copy-start.1 = (s32[256]{0:T(256)S(1)}, s32[256]{0:T(256)}, u32[]{:S(2)}) copy-start(s32[256]{0:T(256)} %param.8) | copy-start | bytes 3076
  0.0 5.7 %copy-start = (s32[12288]{0:T(1024)S(1)}, s32[12288]{0:T(1024)}, u32[]{:S(2)}) copy-start(s32[12288]{0:T(1024)} %param.7) | copy-start | bytes 147460
  0.0 5.8 %copy-start.2 = (s32[96,1]{0,1:T(1,128)S(1)}, s32[96,1]{0,1:T(1,128)}, u32[]{:S(2)}) copy-start(s32[96,1]{0,1:T(1,128)} %param.9) | copy-start | bytes 1156
  0.0 0.7 copy-start.3
  4.2 2.8 %collective-permute-start = (bf16[96,2048]{1,0:T(8,128)(2,1)S(1)}, bf16[96,2048]{1,0:T(8,128)(2,1)S(1)}, u32[]{:S(2)}, u32[]{:S(2)}) collective-permute-start(bf16[96,2048]{1,0:T(8,128)(2,1)S(1)} %decimate.1.dec_ref), channel_id=1, source_target_pairs={{0,4},{4,0},{1,5},{5,1},{2,6},{6,2},{3,7},{7,3},{8,12},{12,8},{9,1... | collective-permute-start | bytes 1179656 | tf_op jit(solution)/shard_map/ppermute | solution.py:208
  41.8 16.7 %all-to-all-start.1 = ((bf16[64,32,128]{2,1,0:T(8,128)(2,1)}), bf16[64,32,128]{2,1,0:T(8,128)(2,1)S(1)}, u32[]{:S(2)}, u32[]{:S(2)}) async-start(bf16[64,32,128]{2,1,0:T(8,128)(2,1)} %get-tuple-element.10), calls=%async_computation.1 | async-start | bytes 1048576 | tf_op jit(solution)/shard_map/all_to_all | solution.py:272
  47.7 14.1 %collective-permute-start.1 = (bf16[64,32,128]{2,1,0:T(8,128)(2,1)S(1)}, bf16[64,32,128]{2,1,0:T(8,128)(2,1)S(1)}, u32[]{:S(2)}, u32[]{:S(2)}) collective-permute-start(bf16[64,32,128]{2,1,0:T(8,128)(2,1)S(1)} %get-tuple-element.9), channel_id=1, source_target_pairs={{0,4},{4,0},{1,5},{5,1},{2,6},{6,2},{3,7},{7,3},{8,12},{12,8},{9,1... | collective-permute-start | bytes 1572872 | tf_op jit(solution)/shard_map/ppermute | solution.py:208
  58.6 4.7 %collective-permute-start.2 = (bf16[64,32,128]{2,1,0:T(8,128)(2,1)S(1)}, bf16[64,32,128]{2,1,0:T(8,128)(2,1)S(1)}, u32[]{:S(2)}, u32[]{:S(2)}) collective-permute-start(bf16[64,32,128]{2,1,0:T(8,128)(2,1)S(1)} %all-to-all-done.1.own_ref), channel_id=1, source_target_pairs={{0,4},{4,0},{1,5},{5,1},{2,6},{6,2},{3,7},{7,3},{8,12},{12,8},{9,1... | collective-permute-start | bytes 1572872 | tf_op jit(solution)/shard_map/ppermute | solution.py:208

commit v11 on v10

--- a/solution.py
+++ b/solution.py
@@ -75,8 +75,8 @@
             dec_ref[r : r + 16, b * LANES : (b + 1) * LANES] = pieces[b]
 
 
-def find_kernel(ids, refch, select_ref):
-    count, rows = select_ref.shape[1:]
+def find_kernel(ids, refch, dec_ref, select_ref, keep_ref):
+    count, rows = select_ref.shape
     core = lax.axis_index("core")
     own = lax.axis_index(AXES)
     refcol = jnp.transpose(jnp.broadcast_to(refch[...], (LANES, NREF)))[:, :rows]
@@ -90,7 +90,11 @@
             pltpu.roll(jnp.broadcast_to(ids[pl.ds(k, 1), :], (8, LANES)), turn, 1) for k in (line0, line1)
         ]
         there = jnp.where(iota((8, LANES), 1) < turn, pair[0], pair[1])[0:1, :rows]
-        select_ref[i] = jnp.where(refcol == there, 1.0, 0.0).astype(BF16)
+        select = jnp.where(refcol == there, 1.0, 0.0).astype(BF16)
+        if i:
+            select_ref[...] = select
+        else:
+            keep_ref[...] = jnp.dot(select, dec_ref[...], preferred_element_type=F32).astype(BF16)
 
 
 def route_kernel(dec_ref, owner_ref, packet_ref, stage):
@@ -118,12 +122,12 @@
         packet_ref[g, : 4 * LAGS, :] = stage[at : at + 4 * LAGS, :].astype(BF16)
 
 
-def add_refs_kernel(packet_in, select_ref, dec_ref, got_ref, packet_ref, stage):
+def add_refs_kernel(packet_in, select_ref, keep_ref, got_ref, packet_ref, stage):
     del packet_in
     for b in range(0, LAGS, 2):
         span = slice(b * LANES, (b + 2) * LANES)
-        picked = jnp.dot(select_ref[0], dec_ref[:, span], preferred_element_type=F32)
-        picked = picked + jnp.dot(select_ref[1], got_ref[:, span], preferred_element_type=F32)
+        picked = jnp.dot(select_ref[...], got_ref[:, span], preferred_element_type=F32)
+        picked = picked + keep_ref[:, span].astype(F32)
         for s in range(2):
             for h in range(2):
                 stage[pl.ds(s * LAGS + b + h, CHIPS, stride=2 * LAGS + PAD), :] = picked[
@@ -231,14 +235,14 @@
         name="decimate",
     )(raw, taps.reshape(1, TAPS))
     got = swap_cores(dec)
-    select = pl.pallas_call(
+    select, keep = pl.pallas_call(
         find_kernel,
-        out_shape=jax.ShapeDtypeStruct((2, NREF // 2, rows_dev), BF16),
-        in_specs=[VMEM] * 2,
-        out_specs=VMEM,
+        out_shape=(jax.ShapeDtypeStruct((NREF // 2, rows_dev), BF16), plain),
+        in_specs=[VMEM] * 3,
+        out_specs=(VMEM, VMEM),
         compiler_params=params(),
         name="find",
-    )(ids, ref_channel.reshape(1, NREF))
+    )(ids, ref_channel.reshape(1, NREF), dec)
     packet_shape = jax.ShapeDtypeStruct((CHIPS, 6 * LAGS, LANES), BF16)
     packet = pl.pallas_call(
         route_kernel,
@@ -259,7 +263,7 @@
         input_output_aliases={0: 0},
         compiler_params=params(),
         name="add_refs",
-    )(packet, select, dec, got)
+    )(packet, select, keep, got)
     arrived = lax.all_to_all(packet, SAME, 0, 0, tiled=True)
     spread, rows_give = pl.pallas_call(
         spread_kernel,

time: 69.2 us -> 69.1 us (level)
  no operation moved by 1% of the time
where the time goes in v11:
time: 69.1 us; the launch traced here: 68.8 us
  blocking collectives  33.6 us (49%)
  Pallas kernels  12.8 us (19%)
  starting transfers between devices  12.1 us (18%)
  waiting for transfers between devices  9.57 us (14%)
    all_to_all x1, blocking collectives, on_device(): arrived = lax.all_to_all(packet, SAME, 0, 0, tiled=True)  33.6 us
    all_to_all x1, waiting for transfers between devices, on_device(): refs_own = lax.all_to_all(spread, SAME, 0, 0, tiled=True)  9.09 us
    ppermute x3, starting transfers between devices, swap_cores(): return lax.ppermute(x, 'core', [(0, 1), (1, 0)])  6.45 us
    all_to_all x1, starting transfers between devices, on_device(): refs_own = lax.all_to_all(spread, SAME, 0, 0, tiled=True)  5.68 us
    pallas_call x1, Pallas kernels, on_device(): pl.pallas_call(correlate_kernel, out_shape=jax.ShapeDtypeStruct((1, 4 * C...  5.67 us
    pallas_call x1, Pallas kernels, on_device(): pl.pallas_call(decimate_kernel, out_shape=jax.ShapeDtypeStruct((rows_dev,...  3.48 us
  transfers between devices with their start and end apart: 4, of which 3 were waited for; matrix products, arithmetic and copies ran while one was open for 0% of the time, Pallas kernels for 3%

profile of v11, /device:TPU:1, one launch (start us, length us, event | category | flops | bytes accessed | tf_op | source)
XLA Modules:
  0.0 68.8 jit_solution(7844526642661491484)
XLA Ops:
  0.0 0.0 copy-start.1
  0.0 0.0 copy-start
  0.0 0.0 copy-start.2
  0.0 0.0 copy-start.3
  0.0 0.7 copy-done.3
  0.7 3.5 %decimate.1.dec_ref = bf16[96,2048]{1,0:T(8,128)(2,1)S(1)} custom-call(bf16[96,16384]{1,0:T(8,128)(2,1)} %raw_hbm.1, bf16[1,127]{1,0:T(2,128)(2,1)S(1)} %bitcast.7), custom_call_target="tpu_custom_call" | custom-call | tf_op jit(solution)/shard_map/decimate/pallas_call | solution.py:222
  4.2 1.5 %collective-permute-start = (bf16[96,2048]{1,0:T(8,128)(2,1)S(1)}, bf16[96,2048]{1,0:T(8,128)(2,1)S(1)}, u32[]{:S(2)}, u32[]{:S(2)}) collective-permute-start(bf16[96,2048]{1,0:T(8,128)(2,1)S(1)} %decimate.1.dec_ref), channel_id=1, source_target_pairs={{0,4},{4,0},{1,5},{5,1},{2,6},{6,2},{3,7},{7,3},{8,12},{12,8},{9,1... | collective-permute-start | bytes 1179656 | tf_op jit(solution)/shard_map/ppermute | solution.py:212
  5.7 0.0 copy-done.1
  5.7 0.0 copy-done
  5.7 0.4 find.1
  6.1 0.0 copy-done.2
  6.1 0.7 %route.1.packet_in = bf16[64,96,128]{2,1,0:T(8,128)(2,1)S(1)} custom-call(bf16[96,2048]{1,0:T(8,128)(2,1)S(1)} %decimate.1.dec_ref, s32[1,96]{1,0:T(1,128)S(1)} %bitcast.6), custom_call_target="tpu_custom_call" | custom-call | flops 100000000 | bytes 4000000 | tf_op jit(solution)/shard_map/route/pallas_call | solution.py:247
  6.8 0.2 collective-permute-done.got_ref
  7.0 0.4 add_refs.1
  7.4 33.6 %all_to_all.10.arrived_ref = bf16[64,96,128]{2,1,0:T(8,128)(2,1)S(1)} all-to-all(bf16[64,96,128]{2,1,0:T(8,128)(2,1)S(1)} %add_refs.1), channel_id=1, replica_groups=mesh['x'=4,'z'=4,'core'=2,'chan'=4] {'x','z','chan'}, dimensions={0} | all-to-all | bytes 3145728 | tf_op jit(solution)/shard_map/all_to_all | solution.py:267
  41.0 0.9 %spread.1 = (bf16[64,32,128]{2,1,0:T(8,128)(2,1)}, bf16[64,32,128]{2,1,0:T(8,128)(2,1)S(1)}) custom-call(bf16[64,96,128]{2,1,0:T(8,128)(2,1)S(1)} %all_to_all.10.arrived_ref), custom_call_target="tpu_custom_call" | custom-call | tf_op jit(solution)/shard_map/spread/pallas_call | solution.py:268
  41.9 5.7 %all-to-all-start.1 = ((bf16[64,32,128]{2,1,0:T(8,128)(2,1)}), bf16[64,32,128]{2,1,0:T(8,128)(2,1)S(1)}, u32[]{:S(2)}, u32[]{:S(2)}) async-start(bf16[64,32,128]{2,1,0:T(8,128)(2,1)} %get-tuple-element.14), calls=%async_computation.1 | async-start | bytes 1048576 | tf_op jit(solution)/shard_map/all_to_all | solution.py:276
  47.6 1.8 %collective-permute-start.1 = (bf16[64,32,128]{2,1,0:T(8,128)(2,1)S(1)}, bf16[64,32,128]{2,1,0:T(8,128)(2,1)S(1)}, u32[]{:S(2)}, u32[]{:S(2)}) collective-permute-start(bf16[64,32,128]{2,1,0:T(8,128)(2,1)S(1)} %get-tuple-element.13), channel_id=1, source_target_pairs={{0,4},{4,0},{1,5},{5,1},{2,6},{6,2},{3,7},{7,3},{8,12},{12,8},{9,1... | collective-permute-start | bytes 1572872 | tf_op jit(solution)/shard_map/ppermute | solution.py:212
  49.4 9.1 %all-to-all-done.1.own_ref = bf16[64,32,128]{2,1,0:T(8,128)(2,1)S(1)} async-done(((bf16[64,32,128]{2,1,0:T(8,128)(2,1)}), bf16[64,32,128]{2,1,0:T(8,128)(2,1)S(1)}, u32[]{:S(2)}, u32[]{:S(2)}) %all-to-all-start.1) | async-done | bytes 524320 | tf_op jit(solution)/shard_map/all_to_all | solution.py:276
  58.5 3.2 %collective-permute-start.2 = (bf16[64,32,128]{2,1,0:T(8,128)(2,1)S(1)}, bf16[64,32,128]{2,1,0:T(8,128)(2,1)S(1)}, u32[]{:S(2)}, u32[]{:S(2)}) collective-permute-start(bf16[64,32,128]{2,1,0:T(8,128)(2,1)S(1)} %all-to-all-done.1.own_ref), channel_id=1, source_target_pairs={{0,4},{4,0},{1,5},{5,1},{2,6},{6,2},{3,7},{7,3},{8,12},{12,8},{9,1... | collective-permute-start | bytes 1572872 | tf_op jit(solution)/shard_map/ppermute | solution.py:212
  61.6 0.0 collective-permute-done.1.got_ref
  61.6 1.3 %widen.1 = (bf16[256,4096]{1,0:T(8,128)(2,1)S(1)}, bf16[128,2048]{1,0:T(8,128)(2,1)S(1)}) custom-call(bf16[64,96,128]{2,1,0:T(8,128)(2,1)S(1)} %all_to_all.10.arrived_ref, bf16[64,32,128]{2,1,0:T(8,128)(2,1)S(1)} %collective-permute-done.1.got_ref, bf16[64,32,128]{2,1,0:T(8,128)(2,1)S(1)} %all-to-all-done.1.own_ref), custom_call_target="tpu_custom_call" | custom-call | tf_op jit(solution)/shard_map/widen/pallas_call | solution.py:278
  62.9 0.2 collective-permute-done.2.other_ref
  63.2 5.7 %correlate.1 = f32[1,256,4096]{2,1,0:T(8,128)} custom-call(bf16[256,4096]{1,0:T(8,128)(2,1)S(1)} %get-tuple-element.15.ext_ref, bf16[128,2048]{1,0:T(8,128)(2,1)S(1)} %get-tuple-element.16.mine_ref, bf16[64,32,128]{2,1,0:T(8,128)(2,1)S(1)} %collective-permute-done.2.other_ref), custom_call_target="tpu_custom_call" | custom-call | tf_op jit(solution)/shard_map/correlate/pallas_call | solution.py:291
Async XLA Ops:
  0.0 5.7 %copy-start.1 = (s32[256]{0:T(256)S(1)}, s32[256]{0:T(256)}, u32[]{:S(2)}) copy-start(s32[256]{0:T(256)} %param.8) | copy-start | bytes 3076
  0.0 5.7 %copy-start = (s32[12288]{0:T(1024)S(1)}, s32[12288]{0:T(1024)}, u32[]{:S(2)}) copy-start(s32[12288]{0:T(1024)} %param.7) | copy-start | bytes 147460
  0.0 6.1 %copy-start.2 = (s32[96,1]{0,1:T(1,128)S(1)}, s32[96,1]{0,1:T(1,128)}, u32[]{:S(2)}) copy-start(s32[96,1]{0,1:T(1,128)} %param.9) | copy-start | bytes 1156
  0.0 0.7 copy-start.3
  4.2 2.8 %collective-permute-start = (bf16[96,2048]{1,0:T(8,128)(2,1)S(1)}, bf16[96,2048]{1,0:T(8,128)(2,1)S(1)}, u32[]{:S(2)}, u32[]{:S(2)}) collective-permute-start(bf16[96,2048]{1,0:T(8,128)(2,1)S(1)} %decimate.1.dec_ref), channel_id=1, source_target_pairs={{0,4},{4,0},{1,5},{5,1},{2,6},{6,2},{3,7},{7,3},{8,12},{12,8},{9,1... | collective-permute-start | bytes 1179656 | tf_op jit(solution)/shard_map/ppermute | solution.py:212
  41.9 16.6 %all-to-all-start.1 = ((bf16[64,32,128]{2,1,0:T(8,128)(2,1)}), bf16[64,32,128]{2,1,0:T(8,128)(2,1)S(1)}, u32[]{:S(2)}, u32[]{:S(2)}) async-start(bf16[64,32,128]{2,1,0:T(8,128)(2,1)} %get-tuple-element.14), calls=%async_computation.1 | async-start | bytes 1048576 | tf_op jit(solution)/shard_map/all_to_all | solution.py:276
  47.6 14.1 %collective-permute-start.1 = (bf16[64,32,128]{2,1,0:T(8,128)(2,1)S(1)}, bf16[64,32,128]{2,1,0:T(8,128)(2,1)S(1)}, u32[]{:S(2)}, u32[]{:S(2)}) collective-permute-start(bf16[64,32,128]{2,1,0:T(8,128)(2,1)S(1)} %get-tuple-element.13), channel_id=1, source_target_pairs={{0,4},{4,0},{1,5},{5,1},{2,6},{6,2},{3,7},{7,3},{8,12},{12,8},{9,1... | collective-permute-start | bytes 1572872 | tf_op jit(solution)/shard_map/ppermute | solution.py:212
  58.5 4.7 %collective-permute-start.2 = (bf16[64,32,128]{2,1,0:T(8,128)(2,1)S(1)}, bf16[64,32,128]{2,1,0:T(8,128)(2,1)S(1)}, u32[]{:S(2)}, u32[]{:S(2)}) collective-permute-start(bf16[64,32,128]{2,1,0:T(8,128)(2,1)S(1)} %all-to-all-done.1.own_ref), channel_id=1, source_target_pairs={{0,4},{4,0},{1,5},{5,1},{2,6},{6,2},{3,7},{7,3},{8,12},{12,8},{9,1... | collective-permute-start | bytes 1572872 | tf_op jit(solution)/shard_map/ppermute | solution.py:212

commit v12 on v11

--- a/solution.py
+++ b/solution.py
@@ -17,7 +17,7 @@
 HALO = 128
 CHIPS = 64
 PAD = 8
-LAG_STEPS = (3, 5, 4, 2, 2)
+LAG_STEPS = (3, 5, 4, 3, 1)
 AXES = ("x", "z", "core", "chan")
 SAME = ("x", "z", "chan")
 NT = (((1,), (1,)), ((), ()))

time: 69.1 us -> 69.1 us (level)
  no operation moved by 1% of the time
where the time goes in v12:
time: 69.1 us; the launch traced here: 68.8 us
  blocking collectives  33.6 us (49%)
  Pallas kernels  12.8 us (19%)
  starting transfers between devices  12.1 us (18%)
  waiting for transfers between devices  9.57 us (14%)
    all_to_all x1, blocking collectives, on_device(): arrived = lax.all_to_all(packet, SAME, 0, 0, tiled=True)  33.6 us
    all_to_all x1, waiting for transfers between devices, on_device(): refs_own = lax.all_to_all(spread, SAME, 0, 0, tiled=True)  9.09 us
    ppermute x3, starting transfers between devices, swap_cores(): return lax.ppermute(x, 'core', [(0, 1), (1, 0)])  6.45 us
    all_to_all x1, starting transfers between devices, on_device(): refs_own = lax.all_to_all(spread, SAME, 0, 0, tiled=True)  5.68 us
    pallas_call x1, Pallas kernels, on_device(): pl.pallas_call(correlate_kernel, out_shape=jax.ShapeDtypeStruct((1, 4 * C...  5.66 us
    pallas_call x1, Pallas kernels, on_device(): pl.pallas_call(decimate_kernel, out_shape=jax.ShapeDtypeStruct((rows_dev,...  3.48 us
  transfers between devices with their start and end apart: 4, of which 3 were waited for; matrix products, arithmetic and copies ran while one was open for 0% of the time, Pallas kernels for 3%

profile of v12, /device:TPU:1, one launch (start us, length us, event | category | flops | bytes accessed | tf_op | source)
XLA Modules:
  0.0 68.8 jit_solution(13822319193170414088)
XLA Ops:
  0.0 0.0 copy-start.1
  0.0 0.0 copy-start
  0.0 0.0 copy-start.2
  0.0 0.0 copy-start.3
  0.0 0.7 copy-done.3
  0.7 3.5 %decimate.1.dec_ref = bf16[96,2048]{1,0:T(8,128)(2,1)S(1)} custom-call(bf16[96,16384]{1,0:T(8,128)(2,1)} %raw_hbm.1, bf16[1,127]{1,0:T(2,128)(2,1)S(1)} %bitcast.7), custom_call_target="tpu_custom_call" | custom-call | tf_op jit(solution)/shard_map/decimate/pallas_call | solution.py:222
  4.2 1.5 %collective-permute-start = (bf16[96,2048]{1,0:T(8,128)(2,1)S(1)}, bf16[96,2048]{1,0:T(8,128)(2,1)S(1)}, u32[]{:S(2)}, u32[]{:S(2)}) collective-permute-start(bf16[96,2048]{1,0:T(8,128)(2,1)S(1)} %decimate.1.dec_ref), channel_id=1, source_target_pairs={{0,4},{4,0},{1,5},{5,1},{2,6},{6,2},{3,7},{7,3},{8,12},{12,8},{9,1... | collective-permute-start | bytes 1179656 | tf_op jit(solution)/shard_map/ppermute | solution.py:212
  5.7 0.0 copy-done.1
  5.7 0.0 copy-done
  5.7 0.4 find.1
  6.1 0.0 copy-done.2
  6.1 0.7 %route.1.packet_in = bf16[64,96,128]{2,1,0:T(8,128)(2,1)S(1)} custom-call(bf16[96,2048]{1,0:T(8,128)(2,1)S(1)} %decimate.1.dec_ref, s32[1,96]{1,0:T(1,128)S(1)} %bitcast.6), custom_call_target="tpu_custom_call" | custom-call | flops 100000000 | bytes 4000000 | tf_op jit(solution)/shard_map/route/pallas_call | solution.py:247
  6.8 0.2 collective-permute-done.got_ref
  7.0 0.4 add_refs.1
  7.4 33.6 %all_to_all.10.arrived_ref = bf16[64,96,128]{2,1,0:T(8,128)(2,1)S(1)} all-to-all(bf16[64,96,128]{2,1,0:T(8,128)(2,1)S(1)} %add_refs.1), channel_id=1, replica_groups=mesh['x'=4,'z'=4,'core'=2,'chan'=4] {'x','z','chan'}, dimensions={0} | all-to-all | bytes 3145728 | tf_op jit(solution)/shard_map/all_to_all | solution.py:267
  41.0 0.9 %spread.1 = (bf16[64,32,128]{2,1,0:T(8,128)(2,1)}, bf16[64,32,128]{2,1,0:T(8,128)(2,1)S(1)}) custom-call(bf16[64,96,128]{2,1,0:T(8,128)(2,1)S(1)} %all_to_all.10.arrived_ref), custom_call_target="tpu_custom_call" | custom-call | tf_op jit(solution)/shard_map/spread/pallas_call | solution.py:268
  41.9 5.7 %all-to-all-start.1 = ((bf16[64,32,128]{2,1,0:T(8,128)(2,1)}), bf16[64,32,128]{2,1,0:T(8,128)(2,1)S(1)}, u32[]{:S(2)}, u32[]{:S(2)}) async-start(bf16[64,32,128]{2,1,0:T(8,128)(2,1)} %get-tuple-element.14), calls=%async_computation.1 | async-start | bytes 1048576 | tf_op jit(solution)/shard_map/all_to_all | solution.py:276
  47.6 1.8 %collective-permute-start.1 = (bf16[64,32,128]{2,1,0:T(8,128)(2,1)S(1)}, bf16[64,32,128]{2,1,0:T(8,128)(2,1)S(1)}, u32[]{:S(2)}, u32[]{:S(2)}) collective-permute-start(bf16[64,32,128]{2,1,0:T(8,128)(2,1)S(1)} %get-tuple-element.13), channel_id=1, source_target_pairs={{0,4},{4,0},{1,5},{5,1},{2,6},{6,2},{3,7},{7,3},{8,12},{12,8},{9,1... | collective-permute-start | bytes 1572872 | tf_op jit(solution)/shard_map/ppermute | solution.py:212
  49.4 9.1 %all-to-all-done.1.own_ref = bf16[64,32,128]{2,1,0:T(8,128)(2,1)S(1)} async-done(((bf16[64,32,128]{2,1,0:T(8,128)(2,1)}), bf16[64,32,128]{2,1,0:T(8,128)(2,1)S(1)}, u32[]{:S(2)}, u32[]{:S(2)}) %all-to-all-start.1) | async-done | bytes 524320 | tf_op jit(solution)/shard_map/all_to_all | solution.py:276
  58.5 3.2 %collective-permute-start.2 = (bf16[64,32,128]{2,1,0:T(8,128)(2,1)S(1)}, bf16[64,32,128]{2,1,0:T(8,128)(2,1)S(1)}, u32[]{:S(2)}, u32[]{:S(2)}) collective-permute-start(bf16[64,32,128]{2,1,0:T(8,128)(2,1)S(1)} %all-to-all-done.1.own_ref), channel_id=1, source_target_pairs={{0,4},{4,0},{1,5},{5,1},{2,6},{6,2},{3,7},{7,3},{8,12},{12,8},{9,1... | collective-permute-start | bytes 1572872 | tf_op jit(solution)/shard_map/ppermute | solution.py:212
  61.6 0.0 collective-permute-done.1.got_ref
  61.6 1.3 %widen.1 = (bf16[256,4096]{1,0:T(8,128)(2,1)S(1)}, bf16[128,2048]{1,0:T(8,128)(2,1)S(1)}) custom-call(bf16[64,96,128]{2,1,0:T(8,128)(2,1)S(1)} %all_to_all.10.arrived_ref, bf16[64,32,128]{2,1,0:T(8,128)(2,1)S(1)} %collective-permute-done.1.got_ref, bf16[64,32,128]{2,1,0:T(8,128)(2,1)S(1)} %all-to-all-done.1.own_ref), custom_call_target="tpu_custom_call" | custom-call | tf_op jit(solution)/shard_map/widen/pallas_call | solution.py:278
  62.9 0.2 collective-permute-done.2.other_ref
  63.2 5.7 %correlate.1 = f32[1,256,4096]{2,1,0:T(8,128)} custom-call(bf16[256,4096]{1,0:T(8,128)(2,1)S(1)} %get-tuple-element.15.ext_ref, bf16[128,2048]{1,0:T(8,128)(2,1)S(1)} %get-tuple-element.16.mine_ref, bf16[64,32,128]{2,1,0:T(8,128)(2,1)S(1)} %collective-permute-done.2.other_ref), custom_call_target="tpu_custom_call" | custom-call | tf_op jit(solution)/shard_map/correlate/pallas_call | solution.py:291
Async XLA Ops:
  0.0 5.7 %copy-start.1 = (s32[256]{0:T(256)S(1)}, s32[256]{0:T(256)}, u32[]{:S(2)}) copy-start(s32[256]{0:T(256)} %param.8) | copy-start | bytes 3076
  0.0 5.7 %copy-start = (s32[12288]{0:T(1024)S(1)}, s32[12288]{0:T(1024)}, u32[]{:S(2)}) copy-start(s32[12288]{0:T(1024)} %param.7) | copy-start | bytes 147460
  0.0 6.1 %copy-start.2 = (s32[96,1]{0,1:T(1,128)S(1)}, s32[96,1]{0,1:T(1,128)}, u32[]{:S(2)}) copy-start(s32[96,1]{0,1:T(1,128)} %param.9) | copy-start | bytes 1156
  0.0 0.7 copy-start.3
  4.2 2.8 %collective-permute-start = (bf16[96,2048]{1,0:T(8,128)(2,1)S(1)}, bf16[96,2048]{1,0:T(8,128)(2,1)S(1)}, u32[]{:S(2)}, u32[]{:S(2)}) collective-permute-start(bf16[96,2048]{1,0:T(8,128)(2,1)S(1)} %decimate.1.dec_ref), channel_id=1, source_target_pairs={{0,4},{4,0},{1,5},{5,1},{2,6},{6,2},{3,7},{7,3},{8,12},{12,8},{9,1... | collective-permute-start | bytes 1179656 | tf_op jit(solution)/shard_map/ppermute | solution.py:212
  41.9 16.6 %all-to-all-start.1 = ((bf16[64,32,128]{2,1,0:T(8,128)(2,1)}), bf16[64,32,128]{2,1,0:T(8,128)(2,1)S(1)}, u32[]{:S(2)}, u32[]{:S(2)}) async-start(bf16[64,32,128]{2,1,0:T(8,128)(2,1)} %get-tuple-element.14), calls=%async_computation.1 | async-start | bytes 1048576 | tf_op jit(solution)/shard_map/all_to_all | solution.py:276
  47.6 14.1 %collective-permute-start.1 = (bf16[64,32,128]{2,1,0:T(8,128)(2,1)S(1)}, bf16[64,32,128]{2,1,0:T(8,128)(2,1)S(1)}, u32[]{:S(2)}, u32[]{:S(2)}) collective-permute-start(bf16[64,32,128]{2,1,0:T(8,128)(2,1)S(1)} %get-tuple-element.13), channel_id=1, source_target_pairs={{0,4},{4,0},{1,5},{5,1},{2,6},{6,2},{3,7},{7,3},{8,12},{12,8},{9,1... | collective-permute-start | bytes 1572872 | tf_op jit(solution)/shard_map/ppermute | solution.py:212
  58.5 4.7 %collective-permute-start.2 = (bf16[64,32,128]{2,1,0:T(8,128)(2,1)S(1)}, bf16[64,32,128]{2,1,0:T(8,128)(2,1)S(1)}, u32[]{:S(2)}, u32[]{:S(2)}) collective-permute-start(bf16[64,32,128]{2,1,0:T(8,128)(2,1)S(1)} %all-to-all-done.1.own_ref), channel_id=1, source_target_pairs={{0,4},{4,0},{1,5},{5,1},{2,6},{6,2},{3,7},{7,3},{8,12},{12,8},{9,1... | collective-permute-start | bytes 1572872 | tf_op jit(solution)/shard_map/ppermute | solution.py:212
